TPU v7x, 32 devices: a whole 2x2x4 slice. The times are simulated.
32 devices in a mesh: dom: 8 (over z, y), mat: 4 (over x, core).
Axes of the slice: x: 2, y: 2, z: 4, core: 2. Of those that a mesh axis runs over, the one named last changes fastest.
Arguments:
- orbitals: bfloat16 [2048, 12, 32, 128], P('dom', None, 'mat')
- potential: float32 [32, 32, 128], P('dom', 'mat'), may hold values from -3 to 3
- centre_first: int32 [2048], P('dom'), may hold values from 0 to 3
- centre_second: int32 [2048], P('dom'), may hold values from 0 to 31
- centre_third: int32 [2048], P('dom'), may hold values from 0 to 127
- correlation_pairs: int32 [16, 5, 2], P('dom'), may hold values from 0 to 1, as said below
Outputs:
- gram_rows: float32 [5, 256, 2048], P(None, 'mat', 'dom')
- hamiltonian_rows: float32 [5, 256, 2048], P(None, 'mat', 'dom')
Inputs may be any that keep to these rules, and one draw needn't show every extreme that they name: correlation_pairs[g, k, b] refers to block b of the domain k - 2 away from block g's owner (wrapping); the pattern is symmetric between the two blocks, and every pair of blocks of one domain is 1.
All inputs are finite; a program needn't handle non-finite values.
Results may differ from a plain program's by a relative error of at most 0.00043.
Values may be sent and summed in bfloat16 or wider, within the bound.
No kernel may reach another device: no remote copies, remote signals or barrier semaphores. Data moves between devices by JAX's collectives and lax.ppermute only.
A program may use at most 128 MiB of HBM per device.

v0:
```python
import jax
import jax.numpy as jnp
from jax import lax
from jax.sharding import PartitionSpec as P


def extended_2(array, sides, width):
    for axis, dim in sides:
        size, length = (lax.axis_size(axis), array.shape[dim])
        up = [(i, (i + 1) % size) for i in range(size)]
        down = [(j, i) for i, j in up]
        last = lax.slice_in_dim(array, length - width, length, axis=dim)
        first = lax.slice_in_dim(array, 0, width, axis=dim)
        before = lax.ppermute(last, axis, up)
        after = lax.ppermute(first, axis, down)
        array = jnp.concatenate([before, array, after], axis=dim)
    return array


def passed_along(block, axis, distance):
    devices = range(lax.axis_size(axis))
    route = [((i - distance) % len(devices), i) for i in devices]
    return lax.ppermute(block, axis, route)


def sphere_mask(
    centre_first,
    centre_second,
    centre_third,
    window_cells,
    patch_cells,
    second_cells,
    second_start,
    second_total,
    third_cells,
):
    planes = lax.iota(jnp.int32, window_cells)
    off_first = planes[None, :] - (patch_cells + centre_first[:, None])
    interior = (planes >= 1) & (planes <= window_cells - 2)
    second_coord = second_start + lax.iota(jnp.int32, second_cells)
    off_second = jnp.mod(second_coord[None, :] - centre_second[:, None], second_total)
    off_second = jnp.minimum(off_second, second_total - off_second)
    off_third = lax.iota(jnp.int32, third_cells)[None, :] - centre_third[:, None]
    radius = window_cells // 2
    distance = (
        (off_first * off_first)[:, :, None, None]
        + (off_second * off_second)[:, None, :, None]
        + (off_third * off_third)[:, None, None, :]
    )
    return (distance <= radius * radius) & interior[None, :, None, None]


def stencil(extended, potential_slab):
    centre_cells = extended[:, 1:-1, 1:-1, :].astype(jnp.float32)
    beside = extended[:, 2:, 1:-1, :].astype(jnp.float32) + extended[:, :-2, 1:-1, :].astype(
        jnp.float32
    )
    beside = (
        beside
        + extended[:, 1:-1, 2:, :].astype(jnp.float32)
        + extended[:, 1:-1, :-2, :].astype(jnp.float32)
    )
    third_padded = jnp.pad(centre_cells, ((0, 0), (0, 0), (0, 0), (1, 1)))
    beside = beside + third_padded[..., 2:] + third_padded[..., :-2]
    return 0.5 * (6.0 * centre_cells - beside) + potential_slab[None] * centre_cells


def on_device(orbitals, potential, centre_first, centre_second, centre_third, correlation_pairs):
    block_orbs, window_cells, second_cells, third_cells = orbitals.shape
    patch_cells = potential.shape[0]
    local_blocks = correlation_pairs.shape[0]
    per_block = block_orbs // local_blocks
    mat_count = lax.axis_size("mat")
    second_start = lax.axis_index("mat") * second_cells
    inside = sphere_mask(
        centre_first,
        centre_second,
        centre_third,
        window_cells,
        patch_cells,
        second_cells,
        second_start,
        second_cells * mat_count,
        third_cells,
    )
    masked = jnp.where(inside, orbitals, jnp.zeros_like(orbitals))
    upper_start = 2 * patch_cells
    rimmed = extended_2(masked, (("mat", 2),), 1)
    rimmed = jnp.pad(rimmed, ((0, 0), (1, 1), (0, 0), (0, 0)))
    potential_window = extended_2(potential, (("dom", 0),), patch_cells)
    applied = stencil(rimmed, potential_window).astype(jnp.bfloat16)
    paired = jnp.stack([masked, applied])
    received = []
    for offset, low_plane in ((1, upper_start), (-1, 0)):
        sent_piece = paired[:, :, low_plane : low_plane + patch_cells]
        received.append(passed_along(sent_piece, "dom", offset))
    middle = paired[:, :, patch_cells:upper_start]
    slot_stack = jnp.concatenate([received[0], middle, received[1]], axis=1)
    orbital_block = slot_stack[0].reshape(3 * block_orbs, -1)
    applied_block = slot_stack[1].reshape(3 * block_orbs, -1)
    gram_full = lax.dot_general(
        orbital_block, orbital_block, (((1,), (1,)), ((), ())), preferred_element_type=jnp.float32
    )
    energy_full = lax.dot_general(
        applied_block, orbital_block, (((1,), (1,)), ((), ())), preferred_element_type=jnp.float32
    )
    gram_full = gram_full.reshape(3, block_orbs, 3, block_orbs)
    energy_full = energy_full.reshape(3, block_orbs, 3, block_orbs)
    gram_part, energy_part = (
        lax.psum_scatter(gram_full, "mat", scatter_dimension=1, tiled=True),
        lax.psum_scatter(energy_full, "mat", scatter_dimension=1, tiled=True),
    )
    col_count = block_orbs // mat_count
    strips = jnp.stack([gram_part, energy_part])
    assembled = jnp.pad(strips[:, :, :, 1], ((0, 0), (1, 1), (0, 0), (0, 0)))
    for slot_index, offset in ((0, -1), (2, 1)):
        arrived = passed_along(strips[:, :, :, slot_index], "dom", offset)
        assembled = assembled + jnp.pad(
            arrived, ((0, 0), (2 - slot_index, slot_index), (0, 0), (0, 0))
        )
    columns = lax.axis_index("mat") * col_count + lax.iota(jnp.int32, col_count)
    block_ids = lax.iota(jnp.int32, local_blocks)
    column_pick = ((columns // per_block)[:, None] == block_ids[None, :]).astype(jnp.float32)
    row_pick = (
        (lax.iota(jnp.int32, block_orbs) // per_block)[:, None] == block_ids[None, :]
    ).astype(jnp.float32)
    select = jnp.einsum(
        "rkb,cb,ar->kca", correlation_pairs.astype(jnp.float32), column_pick, row_pick
    )
    return (assembled[0] * select, assembled[1] * select)


def solution(mesh):
    return jax.shard_map(
        on_device,
        mesh=mesh,
        in_specs=(
            P("dom", None, "mat", None),
            P("dom", "mat", None),
            P("dom"),
            P("dom"),
            P("dom"),
            P("dom", None, None),
        ),
        out_specs=(P(None, "mat", "dom"), P(None, "mat", "dom")),
        check_vma=False,
    )
```

profile of v0, /device:TPU:0, one launch (start us, length us, event | category | flops | bytes accessed | tf_op | source)
XLA Modules:
  0.0 409.6 jit_solution(4848601391768304545)
XLA Ops:
  9.5 8.1 %fusion.40 = (f32[256,12,8,128]{3,0,2,1:T(8,128)}, bf16[256,12,8,128]{3,0,2,1:T(8,128)(2,1)S(1)}) fusion(bf16[256,12,8,128]{3,2,1,0:T(8,128)(2,1)} %param.6, pred[12]{0:T(512)(128)(4,1)S(1)} %compare_and_fusion, s32[256,128]{1,0:T(8,128)S(1)} %subtract_multiply_fusion, s32[256,12,8]{0,2,1:T(8,128)S(1)} %broadcast_add_fusion), kind=kLoop, calls=%fused_computation.83 | loop fusion | flops 15728640 | bytes 25395212 | tf_op jit(solution)/shard_map/convert_element_type | solution.py:54
  18.3 2.0 collective-permute-start.1
  20.2 2.3 collective-permute-start.2
  22.5 3.0 collective-permute-start.3
  27.3 8.3 %collective-permute-done = bf16[256,12,1,128]{3,0,2,1:T(8,128)(2,1)S(1)} collective-permute-done((bf16[256,12,1,128]{3,0,2,1:T(8,128)(2,1)S(1)}, bf16[256,12,1,128]{3,0,2,1:T(8,128)(2,1)S(1)}, u32[]{:S(2)}, u32[]{:S(2)}) %collective-permute-start) | collective-permute-done | bytes 786464 | tf_op jit(solution)/shard_map/ppermute | solution.py:14
  35.6 2.5 collective-permute-done.1
  38.1 3.2 fusion.15
  41.3 21.0 %fusion.18 = bf16[1,256,12,8,128]{4,1,3,2,0:T(8,128)(2,1)} fusion(f32[256,12,8,128]{3,0,2,1:T(8,128)} %get-tuple-element.2, f32[12,8,128]{2,1,0:T(8,128)S(1)} %pad_maximum_fusion.5, bf16[256,12,8,128]{3,0,2,1:T(8,128)(2,1)S(1)} %get-tuple-element.3, bf16[256,12,1,128]{3,0,2,1:T(8,128)(2,1)S(1)} %collective-permute-done, ...), kind=kLoop, calls=%fused_computation.30 | loop fusion | flops 53477376 | bytes 39370752 | tf_op jit(solution)/shard_map/stack | solution.py:92
  62.3 4.1 fusion.20
  67.9 3.3 collective-permute-start.5
  71.2 177.4 %collective-permute-done.4 = bf16[2,256,4,8,128]{4,1,3,2,0:T(8,128)(2,1)S(1)} collective-permute-done((bf16[2,256,4,8,128]{4,1,3,2,0:T(8,128)(2,1)S(1)}, bf16[2,256,4,8,128]{4,1,3,2,0:T(8,128)(2,1)S(1)}, u32[]{:S(2)}, u32[]{:S(2)}) %collective-permute-start.4) | collective-permute-done | bytes 4194336 | tf_op jit(solution)/shard_map/ppermute | solution.py:23
  248.6 2.2 collective-permute-done.5
  250.8 9.9 %pad_maximum_fusion = bf16[2,768,4,8,128]{4,1,3,2,0:T(8,128)(2,1)S(1)} fusion(bf16[2,256,4,8,128]{4,1,3,2,0:T(8,128)(2,1)S(1)} %collective-permute-done.5, bf16[2,256,4,8,128]{4,1,3,2,0:T(8,128)(2,1)S(1)} %get-tuple-element.8, bf16[2,256,4,8,128]{4,1,3,2,0:T(8,128)(2,1)S(1)} %collective-permute-done.4), kind=kLoop, calls=%fused_computation.15 | loop fusion | flops 37748736 | bytes 25165824 | tf_op jit(solution)/shard_map/concatenate | solution.py:98
  260.7 4.2 %fusion.42 = (bf16[1,768,4,8,128]{4,1,3,2,0:T(8,128)(2,1)}, bf16[1,768,4,8,128]{4,1,3,2,0:T(8,128)(2,1)S(1)}) fusion(bf16[2,768,4,8,128]{4,1,3,2,0:T(8,128)(2,1)S(1)} %pad_maximum_fusion), kind=kLoop, calls=%fused_computation.84 | loop fusion | bytes 25165824 | tf_op jit(solution)/shard_map/slice | solution.py:100
  264.9 6.6 %copy.11 = bf16[1,768,4,8,128]{4,3,2,1,0:T(8,128)(2,1)} copy(bf16[1,768,4,8,128]{4,1,3,2,0:T(8,128)(2,1)S(1)} %get-tuple-element.5) | data formatting | bytes 12582912 | tf_op jit(solution)/shard_map/slice | solution.py:99
  271.6 10.3 %reshape.145 = bf16[3,256,4096,1]{2,1,0,3:T(8,128)(2,1)} reshape(bf16[1,768,4,8,128]{4,3,2,1,0:T(8,128)(2,1)} %copy.11) | data formatting | bytes 12582912 | tf_op jit(solution)/shard_map/dot_general | solution.py:101
  281.9 9.4 %copy.12 = bf16[1,768,4,8,128]{4,3,2,1,0:T(8,128)(2,1)} copy(bf16[1,768,4,8,128]{4,1,3,2,0:T(8,128)(2,1)} %get-tuple-element.4) | data formatting | bytes 12582912 | tf_op jit(solution)/shard_map/slice | solution.py:100
  291.3 10.3 %reshape.146 = bf16[3,256,4096,1]{2,1,0,3:T(8,128)(2,1)} reshape(bf16[1,768,4,8,128]{4,3,2,1,0:T(8,128)(2,1)} %copy.12) | data formatting | bytes 12582912 | tf_op jit(solution)/shard_map/dot_general | solution.py:104
  301.6 10.1 %fusion.16 = f32[3,256,3,256]{3,1,2,0:T(8,128)} fusion(bf16[3,256,4096,1]{2,1,0,3:T(8,128)(2,1)} %reshape.145, bf16[3,256,4096,1]{2,1,0,3:T(8,128)(2,1)} %reshape.146), kind=kOutput, calls=%fused_computation.28 | convolution fusion | flops 4831838208 | bytes 14942208 | tf_op jit(solution)/shard_map/dot_general | solution.py:104
  311.8 10.1 %fusion.12 = f32[3,256,3,256]{3,1,2,0:T(8,128)} fusion(bf16[3,256,4096,1]{2,1,0,3:T(8,128)(2,1)} %reshape.145), kind=kOutput, calls=%fused_computation.22 | convolution fusion | flops 4831838208 | bytes 8650752 | tf_op jit(solution)/shard_map/dot_general | solution.py:101
  321.9 23.0 %reduce-scatter.5.cloned.1.call-done = f32[3,64,3,256]{3,1,2,0:T(8,128)} async-done(((f32[3,256,3,256]{3,1,2,0:T(8,128)}), f32[3,64,3,256]{3,1,2,0:T(8,128)}) %reduce-scatter.5.cloned.1.call-update) | async-done | bytes 589840 | tf_op jit(solution)/shard_map/reduce_scatter | solution.py:111
  344.9 35.8 %reduce-scatter.3.cloned.1.call-done = f32[3,64,3,256]{3,1,2,0:T(8,128)} async-done(((f32[3,256,3,256]{3,1,2,0:T(8,128)}), f32[3,64,3,256]{3,1,2,0:T(8,128)}) %reduce-scatter.3.cloned.1.call-update) | async-done | bytes 589840 | tf_op jit(solution)/shard_map/reduce_scatter | solution.py:110
  382.2 4.3 %collective-permute-start.6 = (f32[2,3,64,256]{3,2,1,0:T(8,128)S(1)}, f32[2,3,64,256]{3,2,1,0:T(8,128)S(1)}, u32[]{:S(2)}, u32[]{:S(2)}) collective-permute-start(f32[2,3,64,256]{3,2,1,0:T(8,128)S(1)} %get-tuple-element.13), channel_id=1, source_target_pairs={{4,0},{8,4},{12,8},{16,12},{20,16},{24,20},{28,24},{0,28},{5,1},{9... | collective-permute-start | bytes 1179656 | tf_op jit(solution)/shard_map/ppermute | solution.py:23
  386.7 14.8 %collective-permute-done.6 = f32[2,3,64,256]{3,2,1,0:T(8,128)S(1)} collective-permute-done((f32[2,3,64,256]{3,2,1,0:T(8,128)S(1)}, f32[2,3,64,256]{3,2,1,0:T(8,128)S(1)}, u32[]{:S(2)}, u32[]{:S(2)}) %collective-permute-start.6) | collective-permute-done | bytes 393248 | tf_op jit(solution)/shard_map/ppermute | solution.py:23
  (29 shorter events, 9.1 us)
Async XLA Ops:
  7.2 337.8 %reduce-scatter.5.cloned.1.call-start = ((), (), s32[]{:S(2)}) async-start(), calls=%async_computation.3 | async-start | bytes 2949120 | tf_op jit(solution)/shard_map/reduce_scatter | solution.py:111
  9.5 10.8 %copy-start = (f32[4,8,128]{2,1,0:T(8,128)S(1)}, f32[4,8,128]{2,1,0:T(8,128)}, u32[]{:S(2)}) copy-start(f32[4,8,128]{2,1,0:T(8,128)} %param.7) | copy-start | bytes 49156
  17.7 17.9 %collective-permute-start = (bf16[256,12,1,128]{3,0,2,1:T(8,128)(2,1)S(1)}, bf16[256,12,1,128]{3,0,2,1:T(8,128)(2,1)S(1)}, u32[]{:S(2)}, u32[]{:S(2)}) collective-permute-start(bf16[256,12,1,128]{3,0,2,1:T(8,128)(2,1)S(1)} %get-tuple-element.10), channel_id=1, source_target_pairs={{0,1},{1,2},{2,3},{3,0},{4,5},{5,6},{6,7},{7,4},{8,9},{9,10},{10,1... | collective-permute-start | bytes 2359304 | tf_op jit(solution)/shard_map/ppermute | solution.py:14
  18.3 19.8 %collective-permute-start.1 = (bf16[256,12,1,128]{3,0,2,1:T(8,128)(2,1)S(1)}, bf16[256,12,1,128]{3,0,2,1:T(8,128)(2,1)S(1)}, u32[]{:S(2)}, u32[]{:S(2)}) collective-permute-start(bf16[256,12,1,128]{3,0,2,1:T(8,128)(2,1)S(1)} %get-tuple-element.9), channel_id=1, source_target_pairs={{1,0},{2,1},{3,2},{0,3},{5,4},{6,5},{7,6},{4,7},{9,8},{10,9},{11,1... | collective-permute-start | bytes 2359304 | tf_op jit(solution)/shard_map/ppermute | solution.py:15
  20.2 7.0 %collective-permute-start.2 = (f32[4,8,128]{2,1,0:T(8,128)S(1)}, f32[4,8,128]{2,1,0:T(8,128)S(1)}, u32[]{:S(2)}, u32[]{:S(2)}) collective-permute-start(f32[4,8,128]{2,1,0:T(8,128)S(1)} %copy-done), channel_id=1, source_target_pairs={{0,4},{4,8},{8,12},{12,16},{16,20},{20,24},{24,28},{28,0},{1,5},{5... | collective-permute-start | bytes 49160 | tf_op jit(solution)/shard_map/ppermute | solution.py:14
  22.5 4.8 %collective-permute-start.3 = (f32[4,8,128]{2,1,0:T(8,128)S(1)}, f32[4,8,128]{2,1,0:T(8,128)S(1)}, u32[]{:S(2)}, u32[]{:S(2)}) collective-permute-start(f32[4,8,128]{2,1,0:T(8,128)S(1)} %copy-done), channel_id=1, source_target_pairs={{4,0},{8,4},{12,8},{16,12},{20,16},{24,20},{28,24},{0,28},{5,1},{9... | collective-permute-start | bytes 49160 | tf_op jit(solution)/shard_map/ppermute | solution.py:15
  66.4 182.3 %collective-permute-start.4 = (bf16[2,256,4,8,128]{4,1,3,2,0:T(8,128)(2,1)S(1)}, bf16[2,256,4,8,128]{4,1,3,2,0:T(8,128)(2,1)S(1)}, u32[]{:S(2)}, u32[]{:S(2)}) collective-permute-start(bf16[2,256,4,8,128]{4,1,3,2,0:T(8,128)(2,1)S(1)} %get-tuple-element.6), channel_id=1, source_target_pairs={{28,0},{0,4},{4,8},{8,12},{12,16},{16,20},{20,24},{24,28},{29,1},{... | collective-permute-start | bytes 12582920 | tf_op jit(solution)/shard_map/ppermute | solution.py:23
  67.9 182.9 %collective-permute-start.5 = (bf16[2,256,4,8,128]{4,1,3,2,0:T(8,128)(2,1)S(1)}, bf16[2,256,4,8,128]{4,1,3,2,0:T(8,128)(2,1)S(1)}, u32[]{:S(2)}, u32[]{:S(2)}) collective-permute-start(bf16[2,256,4,8,128]{4,1,3,2,0:T(8,128)(2,1)S(1)} %get-tuple-element.7), channel_id=1, source_target_pairs={{4,0},{8,4},{12,8},{16,12},{20,16},{24,20},{28,24},{0,28},{5,1},{9... | collective-permute-start | bytes 12582920 | tf_op jit(solution)/shard_map/ppermute | solution.py:23
  311.7 74.8 %copy-start.1 = (s32[2,5,2]{1,2,0:T(2,128)S(1)}, s32[2,5,2]{1,2,0:T(2,128)}, u32[]{:S(2)}) copy-start(s32[2,5,2]{1,2,0:T(2,128)} %param.11) | copy-start | bytes 244
  311.7 69.0 %reduce-scatter.3.cloned.1.call-start = ((), (), s32[]{:S(2)}) async-start(), calls=%async_computation.2 | async-start | bytes 2949120 | tf_op jit(solution)/shard_map/reduce_scatter | solution.py:110
  382.2 19.3 %collective-permute-start.6 = (f32[2,3,64,256]{3,2,1,0:T(8,128)S(1)}, f32[2,3,64,256]{3,2,1,0:T(8,128)S(1)}, u32[]{:S(2)}, u32[]{:S(2)}) collective-permute-start(f32[2,3,64,256]{3,2,1,0:T(8,128)S(1)} %get-tuple-element.13), channel_id=1, source_target_pairs={{4,0},{8,4},{12,8},{16,12},{20,16},{24,20},{28,24},{0,28},{5,1},{9... | collective-permute-start | bytes 1179656 | tf_op jit(solution)/shard_map/ppermute | solution.py:23
  386.5 15.0 %collective-permute-start.7 = (f32[2,3,64,256]{3,2,1,0:T(8,128)S(1)}, f32[2,3,64,256]{3,2,1,0:T(8,128)S(1)}, u32[]{:S(2)}, u32[]{:S(2)}) collective-permute-start(f32[2,3,64,256]{3,2,1,0:T(8,128)S(1)} %get-tuple-element.12), channel_id=1, source_target_pairs={{28,0},{0,4},{4,8},{8,12},{12,16},{16,20},{20,24},{24,28},{29,1},{... | collective-permute-start | bytes 1179656 | tf_op jit(solution)/shard_map/ppermute | solution.py:23
Sparse Core Ops, SparseCore 0:
  311.9 33.0 reduce-scatter.4
  347.6 33.0 reduce-scatter.2
where the time goes:
time: 410 us
  waiting for transfers between devices  266 us (65%)
  other arithmetic  50 us (12%)
  local copies, waits for them, and re-layouts  41.1 us (10%)
  matrix products  21.5 us (5%)
  starting transfers between devices  17 us (4%)
  between operations  14.2 us (3%)
    ppermute x4, waiting for transfers between devices, passed_along(): return lax.ppermute(block, axis, route)  194 us
    reduce_scatter x1, waiting for transfers between devices, on_device(): lax.psum_scatter(gram_full, 'mat', scatter_dimension=1, tiled=True)  35.8 us
    another operation x2, other arithmetic, on_device(): paired = jnp.stack([masked, applied])  25.1 us
    reduce_scatter x1, waiting for transfers between devices, on_device(): lax.psum_scatter(energy_full, 'mat', scatter_dimension=1, tiled=True)  23 us
    slice x2, local copies, waits for them, and re-layouts, on_device(): applied_block = slot_stack[1].reshape(3 * block_orbs, -1)  13.7 us
    dot_general x1, local copies, waits for them, and re-layouts, on_device(): lax.dot_general(orbital_block, orbital_block, (((1,), (1,)), ((), ())), p...  10.3 us
    dot_general x1, local copies, waits for them, and re-layouts, on_device(): lax.dot_general(applied_block, orbital_block, (((1,), (1,)), ((), ())), p...  10.3 us
    dot_general x1, matrix products, on_device(): lax.dot_general(orbital_block, orbital_block, (((1,), (1,)), ((), ())), p...  10.1 us
  transfers between devices with their start and end apart: 10, of which 8 were waited for; matrix products, arithmetic and copies ran while one was open for 3% of the time, Pallas kernels for 0%

commit v1 on v0

v1 whole, which is shorter than its diff:
```python
import functools

import jax
import jax.numpy as jnp
from jax import lax
from jax.experimental import pallas as pl
from jax.experimental.pallas import tpu as pltpu
from jax.sharding import PartitionSpec as P

SKEW = 12
FOLD = 32
BF = jnp.bfloat16
F32 = jnp.float32


def row_gap(rows, centre, total):
    gap = jnp.abs(rows - centre)
    return jnp.minimum(gap, total - gap)


def pack_kernel(ids_ref, first_ref, second_ref, third_ref, x_ref, o_ref, scr, *, share, patch, total_rows):
    count, window, rows, cells = x_ref.shape
    radius = window // 2
    base = ids_ref[0] * share + pl.program_id(0) * count
    z = lax.broadcasted_iota(jnp.int32, (rows, cells), 1).astype(F32)
    y = (lax.broadcasted_iota(jnp.int32, (rows, cells), 0) + ids_ref[1] * rows).astype(F32)

    def body(n, carry):
        i = base + n
        first = first_ref[i]
        off_z = z - third_ref[i].astype(F32)
        off_y = row_gap(y, second_ref[i].astype(F32), float(total_rows))
        distance = off_z * off_z + off_y * off_y
        packed = jnp.zeros((rows, cells), F32)
        for p in range(1, window - 1):
            off = p - patch - first
            limit = (radius * radius - off * off).astype(F32)
            kept = jnp.where(distance <= limit, x_ref[n, p].astype(F32), 0.0)
            packed = packed + pltpu.roll(kept, (SKEW * p) % cells, 1)
        scr[n] = packed
        return carry

    lax.fori_loop(0, count, body, 0, unroll=4)
    for r in range(rows):
        o_ref[r] = scr[:, r, :].astype(BF)


def pack_share(orbitals, firsts, seconds, thirds, share_id, row_group, share, patch, total_rows):
    _, window, rows, cells = orbitals.shape
    step = 16
    steps = share // step
    grid_spec = pltpu.PrefetchScalarGridSpec(
        num_scalar_prefetch=4,
        grid=(steps,),
        in_specs=[pl.BlockSpec((step, window, rows, cells), lambda s, ids, *_: (ids[0] * steps + s, 0, 0, 0))],
        out_specs=pl.BlockSpec((rows, step, cells), lambda s, *_: (0, s, 0)),
        scratch_shapes=[pltpu.VMEM((step, rows, cells), F32)],
    )
    return pl.pallas_call(
        functools.partial(pack_kernel, share=share, patch=patch, total_rows=total_rows),
        grid_spec=grid_spec,
        out_shape=jax.ShapeDtypeStruct((rows, share, cells), BF),
        compiler_params=pltpu.CompilerParams(vmem_limit_bytes=32 * 2**20),
        cost_estimate=pl.CostEstimate(flops=share * window * rows * cells * 8, bytes_accessed=share * window * rows * cells * 2, transcendentals=0),
    )(jnp.stack([share_id, row_group]), firsts, seconds, thirds, orbitals)


def merge_kernel(ids_ref, own_ref, near_ref, far_ref, diag_ref, centre_ref, o_ref):
    rows, share, cells = own_ref.shape
    parity = ids_ref[0] % 2
    o_ref[pl.ds(parity * rows, rows)] = own_ref[...] + far_ref[...]
    o_ref[pl.ds((1 - parity) * rows, rows)] = near_ref[...] + diag_ref[...]
    centres = centre_ref[pl.ds(pl.multiple_of(ids_ref[0] * share, share), share), :]
    lane = lax.broadcasted_iota(jnp.int32, (share, cells), 1)
    meta = jnp.where(lane == 0, centres[:, 0:1], jnp.where(lane == 1, centres[:, 1:2], centres[:, 2:3]))
    o_ref[2 * rows] = meta.astype(BF)


def merge_rows(ids, own, near, far, diag, centres):
    rows, share, cells = own.shape
    return pl.pallas_call(
        merge_kernel,
        in_specs=[pl.BlockSpec(memory_space=pltpu.SMEM)] + [pl.BlockSpec(memory_space=pltpu.VMEM)] * 5,
        out_specs=pl.BlockSpec(memory_space=pltpu.VMEM),
        out_shape=jax.ShapeDtypeStruct((2 * rows + 1, share, cells), BF),
        compiler_params=pltpu.CompilerParams(vmem_limit_bytes=32 * 2**20),
    )(ids, own, near, far, diag, centres)


def product_kernel(
    ids_ref, pairs_ref, row_third_ref,
    own_ref, near_ref, far_ref, diag_ref, low2_ref, low1_ref, up1_ref, up2_ref,
    v_own_ref, v_low_ref, v_up_ref,
    gram_ref, ham_ref,
    a_ref, b_ref, t_ref, v_ref, g_ref,
    *, patch, radius, total_rows,
):
    m = ids_ref[0]
    slots = own_ref.shape[0] - 1
    share, cells = own_ref.shape[1:]
    window = 3 * patch
    groups, _, rows, _ = v_own_ref.shape
    lane = lax.broadcasted_iota(jnp.int32, (share, cells), 1)

    for d, ref in enumerate((v_low_ref, v_own_ref, v_up_ref)):
        for group in range(groups):
            piece = jnp.bitwise_xor(group, m)
            for p in range(patch):
                v_ref[d, p, group * rows : (group + 1) * rows, :] = pltpu.roll(ref[piece, p], (FOLD * p) % cells, 1) if p else ref[piece, p]

    def centre_columns(ref):
        meta = ref[slots].astype(F32)
        return [jnp.broadcast_to(meta[:, c : c + 1], (share, cells)) for c in range(3)]

    def unpack(ref, planes, store):
        first, second, third = centre_columns(ref)
        for p in planes:
            z = jnp.bitwise_and(lane - FOLD * (p % patch), cells - 1).astype(F32)
            off_z = z - third
            off = float(p - patch) - first
            t_ref[p] = (float(radius * radius) - off * off - off_z * off_z).astype(BF)

        def body(s, carry):
            gaps = []
            for half in range(total_rows // slots):
                y = (s + half * slots).astype(F32)
                gap = row_gap(jnp.full((share, cells), y, F32), second, float(total_rows))
                gaps.append((gap * gap).astype(BF))
            packed = ref[s]
            parts = [{} for _ in gaps]
            for p in planes:
                moved = pltpu.roll(packed, ((FOLD - SKEW) * p) % cells, 1)
                limit = t_ref[p]
                for half, gap in enumerate(gaps):
                    before = parts[half].get(p // patch)
                    if before is None:
                        before = jnp.zeros_like(moved)
                    parts[half][p // patch] = jnp.where(gap <= limit, moved, before)
            for half in range(len(gaps)):
                column = pl.ds(pl.multiple_of((s + half * slots) * cells, cells), cells)
                for q, value in parts[half].items():
                    store(q, column, value)
            return carry

        lax.fori_loop(0, slots, body, 0)

    every = range(1, window - 1)
    for hop, ref in ((0, own_ref), (2, far_ref), (1, near_ref), (3, diag_ref)):
        who = pl.multiple_of(jnp.bitwise_xor(m, hop) * share, share)

        def store_row(q, column, value, who=who):
            a_ref[q, pl.ds(who, share), column] = value

        unpack(ref, every, store_row)

    def stencil(k, ref, planes):
        d = k - 2
        quads = sorted({p // patch for p in planes})

        def place(q):
            return q + d, (2 - q) * 2 * share

        def store_column(q, column, value):
            iq, at = place(q)
            b_ref[iq, at : at + share, column] = value

        unpack(ref, planes, store_column)
        third = centre_columns(ref)[2]
        for p in range(patch):
            z = jnp.bitwise_and(lane - FOLD * p, cells - 1).astype(F32)
            g_ref[p] = (jnp.abs(z - third) <= float(FOLD // 2 - 1)).astype(F32)

        def body(y, carry):
            here = pl.ds(pl.multiple_of(y * cells, cells), cells)
            after = pl.ds(pl.multiple_of(jnp.bitwise_and(y + 1, total_rows - 1) * cells, cells), cells)
            before = pl.ds(pl.multiple_of(jnp.bitwise_and(y - 1, total_rows - 1) * cells, cells), cells)
            part = 16
            for c in range(0, share, part):
                mine = [g_ref[p, c : c + part, :] > 0.5 for p in range(patch)]
                centre, up, down = {}, {}, {}
                for q in quads:
                    iq, at = place(q)
                    centre[q] = b_ref[iq, at + c : at + c + part, here].astype(F32)
                    up[q] = pltpu.roll(centre[q], FOLD, 1)
                    down[q] = pltpu.roll(centre[q], cells - FOLD, 1)
                zero = jnp.zeros((part, cells), F32)
                for q in quads:
                    iq, at = place(q)
                    below = jnp.where(mine[0], up.get(q - 1, zero), up[q])
                    above = jnp.where(mine[patch - 1], down.get(q + 1, zero), down[q])
                    beside = above + below
                    beside = beside + b_ref[iq, at + c : at + c + part, after].astype(F32)
                    beside = beside + b_ref[iq, at + c : at + c + part, before].astype(F32)
                    beside = beside + pltpu.roll(centre[q], cells - 1, 1) + pltpu.roll(centre[q], 1, 1)
                    v = [v_ref[iq, p, pl.ds(y, 1), :] for p in range(patch)]
                    v = [jnp.broadcast_to(row, (part, cells)) for row in v]
                    field = v[patch - 1]
                    for p in range(patch - 1):
                        field = jnp.where(mine[p], v[p], field)
                    applied = 0.5 * (6.0 * centre[q] - beside) + field * centre[q]
                    b_ref[iq, at + share + c : at + share + c + part, here] = applied.astype(BF)
            return carry

        lax.fori_loop(0, total_rows, body, 0)

    stencil(2, own_ref, every)
    stencil(1, low1_ref, range(patch, window - 1))
    stencil(3, up1_ref, range(1, 2 * patch))
    stencil(0, low2_ref, range(2 * patch, window - 1))
    stencil(4, up2_ref, range(1, patch))

    sums = {}
    both = 2 * share
    for q in range(3):
        product = lax.dot_general(b_ref[q], a_ref[q], (((1,), (1,)), ((), ())), preferred_element_type=F32)
        for s in range(3):
            k = q + s
            piece = product[s * both : (s + 1) * both]
            sums[k] = piece if k not in sums else sums[k] + piece

    half_rows = a_ref.shape[1] // pairs_ref.shape[0]
    column_block = (m * share) // half_rows
    row_third = row_third_ref[...]
    row_block = lax.broadcasted_iota(jnp.int32, (1, a_ref.shape[1]), 1) // half_rows
    for k, ref in enumerate((low2_ref, low1_ref, own_ref, up1_ref, up2_ref)):
        column_third = ref[slots].astype(F32)[:, 2:3]
        near = jnp.abs(row_third - column_third) <= float(FOLD // 2)
        weight = jnp.zeros((1, a_ref.shape[1]), F32)
        for g in range(pairs_ref.shape[0]):
            weight = jnp.where(row_block == g, pairs_ref[g, k, column_block].astype(F32), weight)
        weight = jnp.where(near, weight, 0.0)
        gram_ref[k] = sums[k][:share] * weight
        ham_ref[k] = sums[k][share:] * weight


def product(ids, pairs, row_third, packs, fields, patch, radius, total_rows, orbs):
    slots, share, cells = packs[0].shape
    reach = 2 * 2 + 1
    long = total_rows * cells
    vm = pl.BlockSpec(memory_space=pltpu.VMEM)
    sm = pl.BlockSpec(memory_space=pltpu.SMEM)
    out = jax.ShapeDtypeStruct((reach, share, orbs), F32)
    return pl.pallas_call(
        functools.partial(product_kernel, patch=patch, radius=radius, total_rows=total_rows),
        in_specs=[sm, sm, vm] + [vm] * 11,
        out_specs=[vm, vm],
        out_shape=[out, out],
        scratch_shapes=[
            pltpu.VMEM((3, orbs, long), BF),
            pltpu.VMEM((3, 6 * share, long), BF),
            pltpu.VMEM((3 * patch, share, cells), BF),
            pltpu.VMEM((3, patch, total_rows, cells), F32),
            pltpu.VMEM((patch, share, cells), F32),
        ],
        compiler_params=pltpu.CompilerParams(vmem_limit_bytes=56 * 2**20),
    )(ids, pairs, row_third, *packs, *fields)


def hop(x, k):
    return lax.ppermute(x, "mat", [(i, i ^ k) for i in range(lax.axis_size("mat"))])


def along(x, distance):
    size = lax.axis_size("dom")
    return lax.ppermute(x, "dom", [((i - distance) % size, i) for i in range(size)])


def on_device(orbitals, potential, centre_first, centre_second, centre_third, correlation_pairs):
    orbs, window, rows, cells = orbitals.shape
    patch = potential.shape[0]
    parts = lax.axis_size("mat")
    share = orbs // parts
    total_rows = rows * parts
    m = lax.axis_index("mat")
    ids = m[None]

    field = jnp.stack([potential] + [hop(potential, k) for k in range(1, parts)])
    field_low, field_up = along(field, 1), along(field, -1)

    def pack(k):
        return pack_share(orbitals, centre_first, centre_second, centre_third, m ^ k, m, share, patch, total_rows)

    arrived = {k: hop(pack(k), k) for k in (3, 2, 1)}
    centres = jnp.stack([centre_first, centre_second, centre_third], axis=1).astype(F32)
    merged = merge_rows(ids, pack(0), arrived[1], arrived[2], arrived[3], centres)

    low2, low1, up1, up2 = (along(merged, d) for d in (2, 1, -1, -2))
    far = hop(merged, 2)
    near = hop(merged, 1)
    diag = hop(far, 1)
    return tuple(
        product(
            ids, correlation_pairs, centre_third.astype(F32)[None, :],
            (merged, near, far, diag, low2, low1, up1, up2),
            (field, field_low, field_up),
            patch, window // 2, total_rows, orbs,
        )
    )


def solution(mesh):
    return jax.shard_map(
        on_device,
        mesh=mesh,
        in_specs=(
            P("dom", None, "mat", None),
            P("dom", "mat", None),
            P("dom"),
            P("dom"),
            P("dom"),
            P("dom", None, None),
        ),
        out_specs=(P(None, "mat", "dom"), P(None, "mat", "dom")),
        check_vma=False,
    )
```

time: 410 us -> 114 us (0.28)
  waiting for transfers between devices: 266 us -> 13.2 us
  Pallas kernels: 0 us -> 61.4 us
  other arithmetic: 50 us -> 0.91 us
  local copies, waits for them, and re-layouts: 41.1 us -> 14.9 us
  matrix products: 21.5 us -> 0 us
  between operations: 14.2 us -> 0.88 us
    ppermute x8 -> x15, waiting for transfers between devices: 207 us -> 13.2 us  [the longest x6 7.8 us: along(): lax.ppermute(x, 'dom', [((i - distance) % size, i) for i in range(size)])]
    pallas_call x0 -> x6, Pallas kernels: none -> 61.4 us  [the longest x1 49.6 us: product(): pl.pallas_call(functools.partial(product_kernel, patch=patch, radius=radi...]
    reduce_scatter x2 -> x0, waiting for transfers between devices: 58.8 us -> none  [the longest x1 35.8 us: on_device(): lax.psum_scatter(gram_full, 'mat', scatter_dimension=1, tiled=True)]
    another operation x2 -> x5, other arithmetic: 25.1 us -> 0.31 us  [the longest x4 0.3 us: pack_share(): jnp.stack([share_id, row_group])]
    dot_general x4 -> x0, matrix products: 21.5 us -> none  [the longest x1 10.1 us: on_device(): lax.dot_general(orbital_block, orbital_block, (((1,), (1,)), ((), ())), p...]
    dot_general x2 -> x0, local copies, waits for them, and re-layouts: 20.6 us -> none  [the longest x1 10.3 us: on_device(): lax.dot_general(orbital_block, orbital_block, (((1,), (1,)), ((), ())), p...]
    slice x4 -> x0, local copies, waits for them, and re-layouts: 20.4 us -> none  [the longest x2 13.7 us: on_device(): applied_block = slot_stack[1].reshape(3 * block_orbs, -1)]
    unnamed x4 -> x47, local copies, waits for them, and re-layouts: 0.01 us -> 14.8 us
  transfers between devices with their start and end apart: 10 -> 15, of which waited for: 8 -> 5; matrix products, arithmetic and copies ran while one was open for 3% -> 1% of each run, Pallas kernels for 0% -> 8%
where the time goes in v1:
time: 114 us; the launch traced here: 112 us
  Pallas kernels  61.4 us (54%)
  starting transfers between devices  20.5 us (18%)
  local copies, waits for them, and re-layouts  14.9 us (13%)
  waiting for transfers between devices  13.2 us (12%)
    pallas_call x1, Pallas kernels, product(): pl.pallas_call(functools.partial(product_kernel, patch=patch, radius=radi...  49.6 us
    unnamed x47, local copies, waits for them, and re-layouts  14.8 us
    ppermute x6, starting transfers between devices, along(): lax.ppermute(x, 'dom', [((i - distance) % size, i) for i in range(size)])  13.1 us
    pallas_call x4, Pallas kernels, pack_share(): pl.pallas_call(functools.partial(pack_kernel, share=share, patch=patch, t...  11.7 us
    ppermute x6, waiting for transfers between devices, along(): lax.ppermute(x, 'dom', [((i - distance) % size, i) for i in range(size)])  7.8 us
    ppermute x9, starting transfers between devices, hop(): lax.ppermute(x, 'mat', [(i, i ^ k) for i in range(lax.axis_size('mat'))])  7.38 us
    ppermute x9, waiting for transfers between devices, hop(): lax.ppermute(x, 'mat', [(i, i ^ k) for i in range(lax.axis_size('mat'))])  5.38 us
  transfers between devices with their start and end apart: 15, of which 5 were waited for; matrix products, arithmetic and copies ran while one was open for 1% of the time, Pallas kernels for 8%

profile of v1, /device:TPU:0, one launch (start us, length us, event | category | flops | bytes accessed | tf_op | source)
XLA Modules:
  0.0 111.7 jit_solution(16833151606559660012)
XLA Ops:
  0.7 2.8 %copy-done = bf16[256,12,8,128]{3,2,1,0:T(8,128)(2,1)S(1)} copy-done((bf16[256,12,8,128]{3,2,1,0:T(8,128)(2,1)S(1)}, bf16[256,12,8,128]{3,2,1,0:T(8,128)(2,1)}, u32[]{:S(2)}) %copy-start) | copy-done | bytes 6291480
  3.5 0.7 copy-done.5
  4.2 0.7 copy-done.7
  5.6 2.9 %shard_map.79 = bf16[8,64,128]{2,1,0:T(8,128)(2,1)S(1)} custom-call(s32[2]{0:T(128)S(1)} %pad_add_fusion.2.ids_ref, s32[256]{0:T(256)S(1)} %copy-done.7, s32[256]{0:T(256)S(1)} %copy-done.9, s32[256]{0:T(256)S(1)} %copy-done.5, bf16[256,12,8,128]{3,2,1,0:T(8,128)(2,1)S(1)} %copy-done), custom_call_target="tpu_custom_call" | custom-call | flops 6291456 | bytes 1572864 | tf_op jit(solution)/shard_map/pallas_call | solution.py:59
  8.5 3.0 %collective-permute-start.1 = (bf16[8,64,128]{2,1,0:T(8,128)(2,1)S(1)}, bf16[8,64,128]{2,1,0:T(8,128)(2,1)S(1)}, u32[]{:S(2)}, u32[]{:S(2)}) collective-permute-start(bf16[8,64,128]{2,1,0:T(8,128)(2,1)S(1)} %shard_map.79), channel_id=1, source_target_pairs={{0,2},{1,3},{2,0},{3,1},{4,6},{5,7},{6,4},{7,5},{8,10},{9,11},{10,... | collective-permute-start | bytes 393224 | tf_op jit(solution)/shard_map/ppermute | solution.py:260
  11.6 2.8 %copy-done.1 = bf16[256,12,8,128]{3,2,1,0:T(8,128)(2,1)S(1)} copy-done((bf16[256,12,8,128]{3,2,1,0:T(8,128)(2,1)S(1)}, bf16[256,12,8,128]{3,2,1,0:T(8,128)(2,1)}, u32[]{:S(2)}) %copy-start.1) | copy-done | bytes 6291480
  14.4 2.9 %shard_map.80 = bf16[8,64,128]{2,1,0:T(8,128)(2,1)S(1)} custom-call(s32[2]{0:T(128)S(1)} %pad_add_fusion.3.ids_ref, s32[256]{0:T(256)S(1)} %copy-done.8, s32[256]{0:T(256)S(1)} %copy-done.10, s32[256]{0:T(256)S(1)} %copy-done.6, bf16[256,12,8,128]{3,2,1,0:T(8,128)(2,1)S(1)} %copy-done.1), custom_call_target="tpu_custom_call" | custom-call | flops 6291456 | bytes 1572864 | tf_op jit(solution)/shard_map/pallas_call | solution.py:59
  17.5 2.8 %copy-done.2 = bf16[256,12,8,128]{3,2,1,0:T(8,128)(2,1)S(1)} copy-done((bf16[256,12,8,128]{3,2,1,0:T(8,128)(2,1)S(1)}, bf16[256,12,8,128]{3,2,1,0:T(8,128)(2,1)}, u32[]{:S(2)}) %copy-start.2) | copy-done | bytes 6291480
  20.2 2.9 %shard_map.78 = bf16[8,64,128]{2,1,0:T(8,128)(2,1)S(1)} custom-call(s32[2]{0:T(128)S(1)} %pad_add_fusion.1.ids_ref, s32[256]{0:T(256)S(1)} %copy-done.8, s32[256]{0:T(256)S(1)} %copy-done.10, s32[256]{0:T(256)S(1)} %copy-done.6, bf16[256,12,8,128]{3,2,1,0:T(8,128)(2,1)S(1)} %copy-done.2), custom_call_target="tpu_custom_call" | custom-call | flops 6291456 | bytes 1572864 | tf_op jit(solution)/shard_map/pallas_call | solution.py:59
  23.6 2.8 %copy-done.3 = bf16[256,12,8,128]{3,2,1,0:T(8,128)(2,1)S(1)} copy-done((bf16[256,12,8,128]{3,2,1,0:T(8,128)(2,1)S(1)}, bf16[256,12,8,128]{3,2,1,0:T(8,128)(2,1)}, u32[]{:S(2)}) %copy-start.3) | copy-done | bytes 6291480
  26.4 2.9 %shard_map.77.own_ref = bf16[8,64,128]{2,1,0:T(8,128)(2,1)S(1)} custom-call(s32[2]{0:T(128)S(1)} %pad_add_fusion.ids_ref, s32[256]{0:T(256)S(1)} %copy-done.8, s32[256]{0:T(256)S(1)} %copy-done.10, s32[256]{0:T(256)S(1)} %copy-done.6, bf16[256,12,8,128]{3,2,1,0:T(8,128)(2,1)S(1)} %copy-done.3), custom_call_target="tpu_custom_call" | custom-call | flops 6291456 | bytes 1572864 | tf_op jit(solution)/shard_map/pallas_call | solution.py:59
  29.4 4.2 %collective-permute-start.9 = (bf16[17,64,128]{2,1,0:T(8,128)(2,1)S(1)}, bf16[17,64,128]{2,1,0:T(8,128)(2,1)S(1)}, u32[]{:S(2)}, u32[]{:S(2)}) collective-permute-start(bf16[17,64,128]{2,1,0:T(8,128)(2,1)S(1)} %shard_map.81.own_ref), channel_id=1, source_target_pairs={{8,0},{12,4},{16,8},{20,12},{24,16},{28,20},{0,24},{4,28},{9,1},{1... | collective-permute-start | bytes 835592 | tf_op jit(solution)/shard_map/ppermute | solution.py:265
  33.6 1.5 %collective-permute-start.4 = (bf16[17,64,128]{2,1,0:T(8,128)(2,1)S(1)}, bf16[17,64,128]{2,1,0:T(8,128)(2,1)S(1)}, u32[]{:S(2)}, u32[]{:S(2)}) collective-permute-start(bf16[17,64,128]{2,1,0:T(8,128)(2,1)S(1)} %shard_map.81.own_ref), channel_id=1, source_target_pairs={{0,2},{1,3},{2,0},{3,1},{4,6},{5,7},{6,4},{7,5},{8,10},{9,11},{10,... | collective-permute-start | bytes 835592 | tf_op jit(solution)/shard_map/ppermute | solution.py:260
  35.7 1.5 %collective-permute-start.11 = (f32[4,8,128]{2,1,0:T(8,128)S(1)}, f32[4,8,128]{2,1,0:T(8,128)S(1)}, u32[]{:S(2)}, u32[]{:S(2)}) collective-permute-start(f32[4,8,128]{2,1,0:T(8,128)S(1)} %copy-done.21), channel_id=1, source_target_pairs={{0,2},{1,3},{2,0},{3,1},{4,6},{5,7},{6,4},{7,5},{8,10},{9,11},{10,... | collective-permute-start | bytes 49160 | tf_op jit(solution)/shard_map/ppermute | solution.py:260
  37.2 4.2 %collective-permute-done.12 = f32[4,8,128]{2,1,0:T(8,128)S(1)} collective-permute-done((f32[4,8,128]{2,1,0:T(8,128)S(1)}, f32[4,8,128]{2,1,0:T(8,128)S(1)}, u32[]{:S(2)}, u32[]{:S(2)}) %collective-permute-start.12) | collective-permute-done | bytes 16416 | tf_op jit(solution)/shard_map/ppermute | solution.py:260
  41.4 1.2 %collective-permute-done.11 = f32[4,8,128]{2,1,0:T(8,128)S(1)} collective-permute-done((f32[4,8,128]{2,1,0:T(8,128)S(1)}, f32[4,8,128]{2,1,0:T(8,128)S(1)}, u32[]{:S(2)}, u32[]{:S(2)}) %collective-permute-start.11) | collective-permute-done | bytes 16416 | tf_op jit(solution)/shard_map/ppermute | solution.py:260
  42.6 1.5 %collective-permute-start.14 = (f32[4,4,8,128]{3,2,1,0:T(8,128)S(1)}, f32[4,4,8,128]{3,2,1,0:T(8,128)S(1)}, u32[]{:S(2)}, u32[]{:S(2)}) collective-permute-start(f32[4,4,8,128]{3,2,1,0:T(8,128)S(1)} %pad_maximum_fusion.v_own_ref), channel_id=1, source_target_pairs={{4,0},{8,4},{12,8},{16,12},{20,16},{24,20},{28,24},{0,28},{5,1},{9... | collective-permute-start | bytes 196616 | tf_op jit(solution)/shard_map/ppermute | solution.py:265
  44.7 4.1 %collective-permute-start.8 = (bf16[17,64,128]{2,1,0:T(8,128)(2,1)S(1)}, bf16[17,64,128]{2,1,0:T(8,128)(2,1)S(1)}, u32[]{:S(2)}, u32[]{:S(2)}) collective-permute-start(bf16[17,64,128]{2,1,0:T(8,128)(2,1)S(1)} %shard_map.81.own_ref), channel_id=1, source_target_pairs={{4,0},{8,4},{12,8},{16,12},{20,16},{24,20},{28,24},{0,28},{5,1},{9... | collective-permute-start | bytes 835592 | tf_op jit(solution)/shard_map/ppermute | solution.py:265
  49.5 1.7 %collective-permute-done.13.v_low_ref = f32[4,4,8,128]{3,2,1,0:T(8,128)S(1)} collective-permute-done((f32[4,4,8,128]{3,2,1,0:T(8,128)S(1)}, f32[4,4,8,128]{3,2,1,0:T(8,128)S(1)}, u32[]{:S(2)}, u32[]{:S(2)}) %collective-permute-start.13) | collective-permute-done | bytes 65568 | tf_op jit(solution)/shard_map/ppermute | solution.py:265
  51.1 2.1 %collective-permute-start.6 = (bf16[17,64,128]{2,1,0:T(8,128)(2,1)S(1)}, bf16[17,64,128]{2,1,0:T(8,128)(2,1)S(1)}, u32[]{:S(2)}, u32[]{:S(2)}) collective-permute-start(bf16[17,64,128]{2,1,0:T(8,128)(2,1)S(1)} %shard_map.81.own_ref), channel_id=1, source_target_pairs={{24,0},{28,4},{0,8},{4,12},{8,16},{12,20},{16,24},{20,28},{25,1},{... | collective-permute-start | bytes 835592 | tf_op jit(solution)/shard_map/ppermute | solution.py:265
  54.3 0.7 copy.16.pairs_ref
  55.0 4.9 %collective-permute-done.8.up1_ref = bf16[17,64,128]{2,1,0:T(8,128)(2,1)S(1)} collective-permute-done((bf16[17,64,128]{2,1,0:T(8,128)(2,1)S(1)}, bf16[17,64,128]{2,1,0:T(8,128)(2,1)S(1)}, u32[]{:S(2)}, u32[]{:S(2)}) %collective-permute-start.8) | collective-permute-done | bytes 278560 | tf_op jit(solution)/shard_map/ppermute | solution.py:265
  59.9 1.2 %collective-permute-done.7.low1_ref = bf16[17,64,128]{2,1,0:T(8,128)(2,1)S(1)} collective-permute-done((bf16[17,64,128]{2,1,0:T(8,128)(2,1)S(1)}, bf16[17,64,128]{2,1,0:T(8,128)(2,1)S(1)}, u32[]{:S(2)}, u32[]{:S(2)}) %collective-permute-start.7) | collective-permute-done | bytes 278560 | tf_op jit(solution)/shard_map/ppermute | solution.py:265
  62.1 49.6 %shard_map.82 = (f32[5,64,256]{2,1,0:T(8,128)}, f32[5,64,256]{2,1,0:T(8,128)}) custom-call(s32[1]{0:T(128)} %bitcast.ids_ref, s32[2,5,2]{2,1,0:T(8,128)} %copy.16.pairs_ref, f32[1,256]{1,0:T(1,128)} %bitcast.19, bf16[17,64,128]{2,1,0:T(8,128)(2,1)} %copy-done.4, bf16[17,64,128]{2,1,0:T(8,128)(2,1)} %copy-done.16, bf16[17,64,128]{2,1,0:T(8,128)(2,1)} %copy-done.12, ...), custom_call_target="tpu_custom_call" | custom-call | tf_op jit(solution)/shard_map/pallas_call | solution.py:243
  (67 shorter events, 5.5 us)
Async XLA Ops:
  0.6 10.9 %copy-start.6 = (s32[256]{0:T(256)S(1)}, s32[256]{0:T(256)}, u32[]{:S(2)}) copy-start(s32[256]{0:T(256)} %third_ref.7) | copy-start | bytes 3076
  0.6 10.9 %copy-start.10 = (s32[256]{0:T(256)S(1)}, s32[256]{0:T(256)}, u32[]{:S(2)}) copy-start(s32[256]{0:T(256)} %second_ref.7) | copy-start | bytes 3076
  0.7 10.9 %copy-start.8 = (s32[256]{0:T(256)S(1)}, s32[256]{0:T(256)}, u32[]{:S(2)}) copy-start(s32[256]{0:T(256)} %first_ref.7) | copy-start | bytes 3076
  8.5 20.8 %collective-permute-start.1 = (bf16[8,64,128]{2,1,0:T(8,128)(2,1)S(1)}, bf16[8,64,128]{2,1,0:T(8,128)(2,1)S(1)}, u32[]{:S(2)}, u32[]{:S(2)}) collective-permute-start(bf16[8,64,128]{2,1,0:T(8,128)(2,1)S(1)} %shard_map.79), channel_id=1, source_target_pairs={{0,2},{1,3},{2,0},{3,1},{4,6},{5,7},{6,4},{7,5},{8,10},{9,11},{10,... | collective-permute-start | bytes 393224 | tf_op jit(solution)/shard_map/ppermute | solution.py:260
  17.3 12.0 %collective-permute-start.2 = (bf16[8,64,128]{2,1,0:T(8,128)(2,1)S(1)}, bf16[8,64,128]{2,1,0:T(8,128)(2,1)S(1)}, u32[]{:S(2)}, u32[]{:S(2)}) collective-permute-start(bf16[8,64,128]{2,1,0:T(8,128)(2,1)S(1)} %shard_map.80), channel_id=1, source_target_pairs={{0,3},{1,2},{2,1},{3,0},{4,7},{5,6},{6,5},{7,4},{8,11},{9,10},{10,... | collective-permute-start | bytes 393224 | tf_op jit(solution)/shard_map/ppermute | solution.py:260
  20.2 14.9 %copy-start.21 = (f32[4,8,128]{2,1,0:T(8,128)S(1)}, f32[4,8,128]{2,1,0:T(8,128)}, u32[]{:S(2)}) copy-start(f32[4,8,128]{2,1,0:T(8,128)} %param.7) | copy-start | bytes 49156
  20.2 34.1 %copy-start.22 = (s32[2,5,2]{1,2,0:T(2,128)S(1)}, s32[2,5,2]{1,2,0:T(2,128)}, u32[]{:S(2)}) copy-start(s32[2,5,2]{1,2,0:T(2,128)} %param.11) | copy-start | bytes 244
  23.2 6.1 %collective-permute-start = (bf16[8,64,128]{2,1,0:T(8,128)(2,1)S(1)}, bf16[8,64,128]{2,1,0:T(8,128)(2,1)S(1)}, u32[]{:S(2)}, u32[]{:S(2)}) collective-permute-start(bf16[8,64,128]{2,1,0:T(8,128)(2,1)S(1)} %shard_map.78), channel_id=1, source_target_pairs={{0,1},{1,0},{2,3},{3,2},{4,5},{5,4},{6,7},{7,6},{8,9},{9,8},{10,11... | collective-permute-start | bytes 393224 | tf_op jit(solution)/shard_map/ppermute | solution.py:260
  29.4 31.8 %copy-start.4 = (bf16[17,64,128]{2,1,0:T(8,128)(2,1)}, bf16[17,64,128]{2,1,0:T(8,128)(2,1)S(1)}, u32[]{:S(2)}) copy-start(bf16[17,64,128]{2,1,0:T(8,128)(2,1)S(1)} %shard_map.81.own_ref) | copy-start | bytes 835588
  29.4 23.8 %collective-permute-start.9 = (bf16[17,64,128]{2,1,0:T(8,128)(2,1)S(1)}, bf16[17,64,128]{2,1,0:T(8,128)(2,1)S(1)}, u32[]{:S(2)}, u32[]{:S(2)}) collective-permute-start(bf16[17,64,128]{2,1,0:T(8,128)(2,1)S(1)} %shard_map.81.own_ref), channel_id=1, source_target_pairs={{8,0},{12,4},{16,8},{20,12},{24,16},{28,20},{0,24},{4,28},{9,1},{1... | collective-permute-start | bytes 835592 | tf_op jit(solution)/shard_map/ppermute | solution.py:265
  33.6 19.6 %collective-permute-start.4 = (bf16[17,64,128]{2,1,0:T(8,128)(2,1)S(1)}, bf16[17,64,128]{2,1,0:T(8,128)(2,1)S(1)}, u32[]{:S(2)}, u32[]{:S(2)}) collective-permute-start(bf16[17,64,128]{2,1,0:T(8,128)(2,1)S(1)} %shard_map.81.own_ref), channel_id=1, source_target_pairs={{0,2},{1,3},{2,0},{3,1},{4,6},{5,7},{6,4},{7,5},{8,10},{9,11},{10,... | collective-permute-start | bytes 835592 | tf_op jit(solution)/shard_map/ppermute | solution.py:260
  35.1 2.1 %collective-permute-start.10 = (f32[4,8,128]{2,1,0:T(8,128)S(1)}, f32[4,8,128]{2,1,0:T(8,128)S(1)}, u32[]{:S(2)}, u32[]{:S(2)}) collective-permute-start(f32[4,8,128]{2,1,0:T(8,128)S(1)} %copy-done.21), channel_id=1, source_target_pairs={{0,1},{1,0},{2,3},{3,2},{4,5},{5,4},{6,7},{7,6},{8,9},{9,8},{10,11... | collective-permute-start | bytes 49160 | tf_op jit(solution)/shard_map/ppermute | solution.py:260
  35.1 6.3 %collective-permute-start.12 = (f32[4,8,128]{2,1,0:T(8,128)S(1)}, f32[4,8,128]{2,1,0:T(8,128)S(1)}, u32[]{:S(2)}, u32[]{:S(2)}) collective-permute-start(f32[4,8,128]{2,1,0:T(8,128)S(1)} %copy-done.21), channel_id=1, source_target_pairs={{0,3},{1,2},{2,1},{3,0},{4,7},{5,6},{6,5},{7,4},{8,11},{9,10},{10,... | collective-permute-start | bytes 49160 | tf_op jit(solution)/shard_map/ppermute | solution.py:260
  35.7 6.9 %collective-permute-start.11 = (f32[4,8,128]{2,1,0:T(8,128)S(1)}, f32[4,8,128]{2,1,0:T(8,128)S(1)}, u32[]{:S(2)}, u32[]{:S(2)}) collective-permute-start(f32[4,8,128]{2,1,0:T(8,128)S(1)} %copy-done.21), channel_id=1, source_target_pairs={{0,2},{1,3},{2,0},{3,1},{4,6},{5,7},{6,4},{7,5},{8,10},{9,11},{10,... | collective-permute-start | bytes 49160 | tf_op jit(solution)/shard_map/ppermute | solution.py:260
  42.6 18.6 %copy-start.18 = (f32[4,4,8,128]{3,2,1,0:T(8,128)}, f32[4,4,8,128]{3,2,1,0:T(8,128)S(1)}, u32[]{:S(2)}) copy-start(f32[4,4,8,128]{3,2,1,0:T(8,128)S(1)} %pad_maximum_fusion.v_own_ref) | copy-start | bytes 196612
  42.6 6.2 %collective-permute-start.14 = (f32[4,4,8,128]{3,2,1,0:T(8,128)S(1)}, f32[4,4,8,128]{3,2,1,0:T(8,128)S(1)}, u32[]{:S(2)}, u32[]{:S(2)}) collective-permute-start(f32[4,4,8,128]{3,2,1,0:T(8,128)S(1)} %pad_maximum_fusion.v_own_ref), channel_id=1, source_target_pairs={{4,0},{8,4},{12,8},{16,12},{20,16},{24,20},{28,24},{0,28},{5,1},{9... | collective-permute-start | bytes 196616 | tf_op jit(solution)/shard_map/ppermute | solution.py:265
  44.1 7.1 %collective-permute-start.13 = (f32[4,4,8,128]{3,2,1,0:T(8,128)S(1)}, f32[4,4,8,128]{3,2,1,0:T(8,128)S(1)}, u32[]{:S(2)}, u32[]{:S(2)}) collective-permute-start(f32[4,4,8,128]{3,2,1,0:T(8,128)S(1)} %pad_maximum_fusion.v_own_ref), channel_id=1, source_target_pairs={{28,0},{0,4},{4,8},{8,12},{12,16},{16,20},{20,24},{24,28},{29,1},{... | collective-permute-start | bytes 196616 | tf_op jit(solution)/shard_map/ppermute | solution.py:265
  44.7 15.2 %collective-permute-start.8 = (bf16[17,64,128]{2,1,0:T(8,128)(2,1)S(1)}, bf16[17,64,128]{2,1,0:T(8,128)(2,1)S(1)}, u32[]{:S(2)}, u32[]{:S(2)}) collective-permute-start(bf16[17,64,128]{2,1,0:T(8,128)(2,1)S(1)} %shard_map.81.own_ref), channel_id=1, source_target_pairs={{4,0},{8,4},{12,8},{16,12},{20,16},{24,20},{28,24},{0,28},{5,1},{9... | collective-permute-start | bytes 835592 | tf_op jit(solution)/shard_map/ppermute | solution.py:265
  48.8 12.4 %copy-start.19 = (f32[4,4,8,128]{3,2,1,0:T(8,128)}, f32[4,4,8,128]{3,2,1,0:T(8,128)S(1)}, u32[]{:S(2)}) copy-start(f32[4,4,8,128]{3,2,1,0:T(8,128)S(1)} %collective-permute-done.14.v_up_ref) | copy-start | bytes 196612
  48.8 12.3 %collective-permute-start.7 = (bf16[17,64,128]{2,1,0:T(8,128)(2,1)S(1)}, bf16[17,64,128]{2,1,0:T(8,128)(2,1)S(1)}, u32[]{:S(2)}, u32[]{:S(2)}) collective-permute-start(bf16[17,64,128]{2,1,0:T(8,128)(2,1)S(1)} %shard_map.81.own_ref), channel_id=1, source_target_pairs={{28,0},{0,4},{4,8},{8,12},{12,16},{16,20},{20,24},{24,28},{29,1},{... | collective-permute-start | bytes 835592 | tf_op jit(solution)/shard_map/ppermute | solution.py:265
  51.1 10.1 %copy-start.20 = (f32[4,4,8,128]{3,2,1,0:T(8,128)}, f32[4,4,8,128]{3,2,1,0:T(8,128)S(1)}, u32[]{:S(2)}) copy-start(f32[4,4,8,128]{3,2,1,0:T(8,128)S(1)} %collective-permute-done.13.v_low_ref) | copy-start | bytes 196612
  51.1 10.0 %collective-permute-start.6 = (bf16[17,64,128]{2,1,0:T(8,128)(2,1)S(1)}, bf16[17,64,128]{2,1,0:T(8,128)(2,1)S(1)}, u32[]{:S(2)}, u32[]{:S(2)}) collective-permute-start(bf16[17,64,128]{2,1,0:T(8,128)(2,1)S(1)} %shard_map.81.own_ref), channel_id=1, source_target_pairs={{24,0},{28,4},{0,8},{4,12},{8,16},{12,20},{16,24},{20,28},{25,1},{... | collective-permute-start | bytes 835592 | tf_op jit(solution)/shard_map/ppermute | solution.py:265
  53.2 7.9 %collective-permute-start.3 = (bf16[17,64,128]{2,1,0:T(8,128)(2,1)S(1)}, bf16[17,64,128]{2,1,0:T(8,128)(2,1)S(1)}, u32[]{:S(2)}, u32[]{:S(2)}) collective-permute-start(bf16[17,64,128]{2,1,0:T(8,128)(2,1)S(1)} %shard_map.81.own_ref), channel_id=1, source_target_pairs={{0,1},{1,0},{2,3},{3,2},{4,5},{5,4},{6,7},{7,6},{8,9},{9,8},{10,11... | collective-permute-start | bytes 835592 | tf_op jit(solution)/shard_map/ppermute | solution.py:260
  53.3 7.9 %collective-permute-start.5 = (bf16[17,64,128]{2,1,0:T(8,128)(2,1)S(1)}, bf16[17,64,128]{2,1,0:T(8,128)(2,1)S(1)}, u32[]{:S(2)}, u32[]{:S(2)}) collective-permute-start(bf16[17,64,128]{2,1,0:T(8,128)(2,1)S(1)} %collective-permute-done.4.far_ref), channel_id=1, source_target_pairs={{0,1},{1,0},{2,3},{3,2},{4,5},{5,4},{6,7},{7,6},{8,9},{9,8},{10,11... | collective-permute-start | bytes 835592 | tf_op jit(solution)/shard_map/ppermute | solution.py:260
  (14 other events, 33.8 us)

commit v2 on v0

v2 whole, which is shorter than its diff:
```python
import functools

import jax
import jax.numpy as jnp
from jax import lax
from jax.experimental import pallas as pl
from jax.experimental.pallas import tpu as pltpu
from jax.sharding import PartitionSpec as P

STEP = 29
SKEW = STEP + 64
NEAR = 14
BF = jnp.bfloat16
F32 = jnp.float32
I32 = jnp.int32


def iota(shape, axis):
    return lax.broadcasted_iota(I32, shape, axis)


def pack_kernel(ids_ref, first_ref, second_ref, third_ref, x_ref, *rest, patch, rows, total_rows):
    *o_refs, landed, arrived, kept, moves, limits, scr = rest
    parts = len(o_refs)
    share, cells = o_refs[0].shape[1:]
    count = scr.shape[0]
    window = 3 * patch
    pairs = window // 2
    radius = window // 2
    thirds = pairs // 2
    m = ids_ref[0]

    def start_of(j, c):
        return pl.multiple_of(jnp.bitwise_xor(m, parts - 1 - j) * share + c * count, count)

    steps = [(j, c) for j in range(parts) for c in range(share // count)]
    copies = []
    for n, (j, c) in enumerate(steps):
        copies.append(pltpu.make_async_copy(x_ref.at[pl.ds(start_of(j, c), count)], landed.at[n], arrived.at[n]))
        copies[-1].start()

    source, target = iota((2 * cells, 2 * cells), 0), iota((2 * cells, 2 * cells), 1)
    to = jnp.bitwise_and(source + SKEW * (source // cells * pairs + target // cells), cells - 1)
    moves[...] = (to == jnp.bitwise_and(target, cells - 1)).astype(F32).astype(BF)
    plane = iota((2 * rows, cells), 0) // rows
    for a in range(pairs):
        p = plane + 2 * a
        inside = (p >= 1) & (p <= window - 2)
        for first in range(patch):
            off = p - patch - first
            limits[first, a] = jnp.where(inside, radius * radius - off * off, -1).astype(F32).astype(BF)
    z = iota((rows, cells), 1).astype(F32)
    y = (iota((rows, cells), 0) + m * rows).astype(F32)

    for step, (j, c) in enumerate(steps):
        base = start_of(j, c)
        copies[step].wait()

        def body(n, carry, base=base, step=step):
            i = base + n
            first = first_ref[i]
            off_z = z - third_ref[i].astype(F32)
            off_y = jnp.abs(y - second_ref[i].astype(F32))
            off_y = jnp.minimum(off_y, float(total_rows) - off_y)
            distance = off_z * off_z + off_y * off_y
            distance = jnp.concatenate([distance, distance], axis=0).astype(BF)
            at = pl.ds(pl.multiple_of(n * 2 * rows, 2 * rows), 2 * rows)
            for half in range(2):
                total = None
                for a in range(half * thirds, (half + 1) * thirds):
                    x = landed[step, n, 2 * a * rows : 2 * (a + 1) * rows, :]
                    x = jnp.where(distance <= limits[first, a], x, jnp.zeros_like(x))
                    turn = 2 * SKEW * (a - half * thirds) % cells
                    total = x if total is None else total + pltpu.roll(x, turn, 1)
                kept[at, half * cells : (half + 1) * cells] = total
            return carry

        lax.fori_loop(0, count, body, 0, unroll=8)
        moved = jnp.dot(kept[...], moves[...], preferred_element_type=F32).reshape(count, 2 * rows, 2 * cells)
        scr[...] = moved[:, :rows, :cells] + moved[:, rows:, cells:]
        for r in range(rows):
            o_refs[j][r, c * count : (c + 1) * count, :] = scr[:, r, :].astype(BF)


def pack(ids, firsts, seconds, thirds, orbitals, parts, patch):
    orbs, window, rows, cells = orbitals.shape
    share = orbs // parts
    count = share // 2
    steps = orbs // count
    sm = pl.BlockSpec(memory_space=pltpu.SMEM)
    return pl.pallas_call(
        functools.partial(pack_kernel, patch=patch, rows=rows, total_rows=rows * parts),
        in_specs=[sm] * 4 + [pl.BlockSpec(memory_space=pl.ANY)],
        out_specs=[pl.BlockSpec(memory_space=pltpu.VMEM)] * parts,
        out_shape=[jax.ShapeDtypeStruct((rows, share, cells), BF)] * parts,
        scratch_shapes=[
            pltpu.VMEM((steps, count, window * rows, cells), BF),
            pltpu.SemaphoreType.DMA((steps,)),
            pltpu.VMEM((count * 2 * rows, 2 * cells), BF),
            pltpu.VMEM((2 * cells, 2 * cells), BF),
            pltpu.VMEM((patch, window // 2, 2 * rows, cells), BF),
            pltpu.VMEM((count, rows, cells), F32),
        ],
        compiler_params=pltpu.CompilerParams(vmem_limit_bytes=58 * 2**20),
        cost_estimate=pl.CostEstimate(flops=orbitals.size * 128, bytes_accessed=orbitals.size * 2, transcendentals=0),
    )(ids, firsts, seconds, thirds, orbitals.reshape(orbs, window * rows, cells))


def merge_kernel(ids_ref, own_ref, near_ref, far_ref, diag_ref, centre_ref, *rest, patch):
    *field_refs, o_ref, v_ref = rest
    rows, share, cells = own_ref.shape
    m = ids_ref[0]
    parity = m % 2
    o_ref[pl.ds(parity * rows, rows)] = own_ref[...] + far_ref[...]
    o_ref[pl.ds((1 - parity) * rows, rows)] = near_ref[...] + diag_ref[...]
    centres = centre_ref[pl.ds(pl.multiple_of(m * share, share), share), :]
    lane = iota((share, cells), 1)
    meta = jnp.where(lane == 0, centres[:, 0:1], jnp.where(lane == 1, centres[:, 1:2], centres[:, 2:3]))
    o_ref[2 * rows] = meta.astype(BF)
    for hop, ref in enumerate(field_refs):
        at = pl.ds(pl.multiple_of(jnp.bitwise_xor(m, hop) * rows, rows), rows)
        for p in range(3 * patch):
            v_ref[p, at, :] = pltpu.roll(ref[p], STEP * p % cells, 1) if p else ref[p]


def merge_rows(ids, packs, centres, fields):
    rows, share, cells = packs[0].shape
    window = fields[0].shape[0]
    return pl.pallas_call(
        functools.partial(merge_kernel, patch=window // 3),
        in_specs=[pl.BlockSpec(memory_space=pltpu.SMEM)] + [pl.BlockSpec(memory_space=pltpu.VMEM)] * (5 + len(fields)),
        out_specs=[pl.BlockSpec(memory_space=pltpu.VMEM)] * 2,
        out_shape=[
            jax.ShapeDtypeStruct((2 * rows + 1, share, cells), BF),
            jax.ShapeDtypeStruct((window, rows * len(fields), cells), F32),
        ],
        compiler_params=pltpu.CompilerParams(vmem_limit_bytes=16 * 2**20),
    )(ids, *packs, centres, *fields)


class Source:
    def __init__(self, ref, hop, patch, total_rows):
        self.ref, self.hop, self.patch, self.total_rows = ref, hop, patch, total_rows
        self.slots = ref.shape[0] - 1
        self.share, self.cells = ref.shape[1:]
        meta = ref[self.slots].astype(F32)
        shape = (self.share, self.cells)
        self.first, self.second, self.third = (jnp.broadcast_to(meta[:, c : c + 1], shape) for c in range(3))
        self.start = iota(shape, 1) - self.third.astype(I32) + self.cells // 2
        self.row = self.second.astype(I32)

    def off(self, p):
        place = STEP * (p + self.patch * self.hop)
        return (jnp.bitwise_and(self.start - place, self.cells - 1) - self.cells // 2).astype(F32)

    def limit(self, p):
        off_z, off_x = self.off(p), float(p - self.patch) - self.first
        radius = 3 * self.patch // 2
        return float(radius * radius) - off_x * off_x - off_z * off_z

    def limits(self, plane_sets, out_ref):
        every = {p: self.limit(p) for p in sorted(set().union(*plane_sets))}
        for n, planes in enumerate(plane_sets):
            for odd in range(2):
                value = jnp.full((self.share, self.cells), -1.0, F32)
                for p in planes:
                    if p % 2 == odd:
                        value = jnp.maximum(value, every[p])
                out_ref[n, odd] = value.astype(BF)

    def gap(self, s):
        ahead = s - self.row
        off = jnp.bitwise_and(ahead + self.slots // 2, self.slots - 1) - self.slots // 2
        low = jnp.bitwise_and(ahead + self.slots // 2, self.total_rows - 1) < self.slots
        off = off.astype(F32)
        return (off * off).astype(BF), low.astype(F32)

    def packed(self, s):
        value = self.ref[s]
        turn = STEP * self.patch * self.hop
        even = pltpu.roll(value, turn % self.cells, 1) if turn % self.cells else value
        return even, pltpu.roll(value, (turn + self.cells // 2) % self.cells, 1)


def inside(gap, limit_ref, n, even, odd):
    zero = jnp.zeros_like(even)
    return jnp.where(gap <= limit_ref[n, 0], even, jnp.where(gap <= limit_ref[n, 1], odd, zero))


def planes_of(quads, allowed, patch, shift):
    return [[p for p in range(patch * q + shift, patch * (q + 1) + shift) if p in allowed] for q in quads]


def spread_rows(source, limit_ref, quads, store):
    def body(s, carry):
        even, odd = source.packed(s)
        gap, low = source.gap(s)
        is_low = low.astype(BF) > 0.5
        zero = jnp.zeros_like(even)
        for n, q in enumerate(quads):
            value = inside(gap, limit_ref, n, even, odd)
            store(q, s, jnp.where(is_low, value, zero))
            store(q, s + source.slots, jnp.where(is_low, zero, value))
        return carry

    lax.fori_loop(0, source.slots, body, 0, unroll=4)


def stencil_moves(cells):
    source, target = iota((2 * cells, 2 * cells), 0), iota((2 * cells, 2 * cells), 1)
    ahead = jnp.bitwise_and(target - source, cells - 1)
    same = source // cells == target // cells
    beside = (same & ((ahead == 1) | (ahead == cells - 1))) | (~same & (ahead == 0))
    value = jnp.where(same & (ahead == 0), 3.0, 0.0)
    return jnp.where(beside, -0.5, value).astype(F32).astype(BF)


def columns(source, allowed, limit_ref, group_ref, value_ref, plane_ref, moves_ref, v_ref, kinetic_ref, store):
    patch, cells, share, slots = source.patch, source.cells, source.share, source.slots
    shift = -patch * source.hop
    quads = sorted({(p - shift) // patch for p in allowed})
    sets = planes_of(quads, allowed, patch, shift) + planes_of(quads, allowed, patch, shift - 1) + planes_of(quads, allowed, patch, shift + 1)
    source.limits(sets, limit_ref)
    count = len(quads)
    for n, q in enumerate(quads):
        group = jnp.zeros((share, cells), F32)
        for g in range(1, patch):
            group = jnp.where(jnp.abs(source.off(patch * q + shift + g)) <= float(NEAR), float(g), group)
        group_ref[n] = group

    def place(n, pair):
        return pl.ds(pl.multiple_of((n * (slots // 2) + pair) * share, share), share)

    def first_pass(pair, carry):
        for half in range(2):
            s = 2 * pair + half
            even, odd = source.packed(s)
            gap, _ = source.gap(s)
            for n in range(count):
                at = place(n, pair)
                value_ref[at, half * cells : (half + 1) * cells] = inside(gap, limit_ref, n, even, odd)
                before = inside(gap, limit_ref, count + n, even, odd)
                plane_ref[at, half * cells : (half + 1) * cells] = pltpu.roll(before, STEP, 1)
                after = inside(gap, limit_ref, 2 * count + n, even, odd)
                plane_ref[at, (2 + half) * cells : (3 + half) * cells] = pltpu.roll(after, cells - STEP, 1)
        return carry

    lax.fori_loop(0, slots // 2, first_pass, 0, unroll=4)
    total = count * slots // 2 * share
    kinetic_ref[:total] = jnp.dot(value_ref[:total], moves_ref[...], preferred_element_type=F32)

    def second_pass(pair, carry):
        for half in range(2):
            s = 2 * pair + half
            _, low = source.gap(s)
            low_wide = low > 0.5
            low_packed = low.astype(BF) > 0.5
            neighbour = jnp.bitwise_and(pair + 2 * half - 1, slots // 2 - 1)
            here = slice(half * cells, (half + 1) * cells)
            there = slice((1 - half) * cells, (2 - half) * cells)
            for n, q in enumerate(quads):
                at = place(n, pair)
                value = value_ref[at, here]
                group = group_ref[n]
                field = None
                for g in range(patch):
                    rows = [v_ref[patch * q + g, pl.ds(y, 1), :] for y in (s, s + slots)]
                    row = jnp.where(low_wide, *rows)
                    field = row if g == 0 else jnp.where(group == float(g), row, field)
                beside = plane_ref[at, here].astype(F32) + plane_ref[at, slice((2 + half) * cells, (3 + half) * cells)].astype(F32)
                beside = beside + value_ref[place(n, neighbour), there].astype(F32)
                applied = kinetic_ref[at, here] - 0.5 * beside + field * value.astype(F32)
                applied = applied.astype(BF)
                zero = jnp.zeros_like(value)
                store(q, 0, s, jnp.where(low_packed, value, zero))
                store(q, 0, s + slots, jnp.where(low_packed, zero, value))
                store(q, 1, s, jnp.where(low_packed, applied, zero))
                store(q, 1, s + slots, jnp.where(low_packed, zero, applied))
        return carry

    lax.fori_loop(0, slots // 2, second_pass, 0, unroll=2)


def row_of(y, cells):
    return pl.ds(pl.multiple_of(y * cells, cells), cells)


def product_of(b, a):
    return lax.dot_general(b, a, (((1,), (1,)), ((), ())), preferred_element_type=F32)


def own_kernel(own_ref, v_ref, b_ref, limit_ref, group_ref, value_ref, plane_ref, moves_ref, kinetic_ref, *, patch, total_rows):
    share, cells = own_ref.shape[1:]
    moves_ref[...] = stencil_moves(cells)

    def store_column(q, applied, y, value):
        b_ref[q, applied * share : (applied + 1) * share, row_of(y, cells)] = value

    source = Source(own_ref, 0, patch, total_rows)
    every = range(1, 3 * patch - 1)
    columns(source, every, limit_ref, group_ref, value_ref, plane_ref, moves_ref, v_ref, kinetic_ref, store_column)


def rows_kernel(ids_ref, own_ref, near_ref, far_ref, diag_ref, b_ref, a_ref, sum_ref, limit_ref, *, patch, total_rows):
    m = ids_ref[0]
    share, cells = own_ref.shape[1:]
    every = range(1, 3 * patch - 1)
    for hop, ref in enumerate((own_ref, near_ref, far_ref, diag_ref)):
        who = pl.ds(pl.multiple_of(jnp.bitwise_xor(m, hop) * share, share), share)
        source = Source(ref, 0, patch, total_rows)
        source.limits(planes_of(range(3), every, patch, 0), limit_ref)

        def store_row(q, y, value, who=who):
            a_ref[q, who, row_of(y, cells)] = value

        spread_rows(source, limit_ref, range(3), store_row)
    total = product_of(b_ref[0], a_ref[0])
    for q in range(1, 3):
        total = total + product_of(b_ref[q], a_ref[q])
    sum_ref[...] = total


def others_kernel(
    ids_ref, pairs_ref, row_third_ref, own_ref, low2_ref, low1_ref, up1_ref, up2_ref, a_ref, v_ref, sum_ref,
    gram_ref, ham_ref,
    b_ref, limit_ref, group_ref, value_ref, plane_ref, moves_ref, kinetic_ref,
    *, patch, total_rows,
):
    m = ids_ref[0]
    slots = own_ref.shape[0] - 1
    share, cells = own_ref.shape[1:]
    both = 2 * share
    window = 3 * patch
    moves_ref[...] = stencil_moves(cells)
    spots = {}
    for hop, ref, allowed in (
        (-1, low1_ref, range(patch, window - 1)),
        (1, up1_ref, range(1, 2 * patch)),
        (-2, low2_ref, range(2 * patch, window - 1)),
        (2, up2_ref, range(1, patch)),
    ):
        def store_column(q, applied, y, value, hop=hop):
            taken = sorted({q - 2, q - 1, q} - {0}).index(hop)
            spots[hop, q] = taken
            at = taken * both + applied * share
            b_ref[q, at : at + share, row_of(y, cells)] = value

        source = Source(ref, hop, patch, total_rows)
        columns(source, allowed, limit_ref, group_ref, value_ref, plane_ref, moves_ref, v_ref, kinetic_ref, store_column)

    sums = {0: sum_ref[...]}
    for q in range(3):
        product = product_of(b_ref[q], a_ref[q])
        for (hop, at_q), taken in spots.items():
            if at_q == q:
                piece = product[taken * both : (taken + 1) * both]
                sums[hop] = piece if hop not in sums else sums[hop] + piece

    orbs = a_ref.shape[1]
    half_rows = orbs // pairs_ref.shape[0]
    column_block = (m * share) // half_rows
    row_third = row_third_ref[...]
    row_block = iota((1, orbs), 1) // half_rows
    for k, ref in enumerate((low2_ref, low1_ref, own_ref, up1_ref, up2_ref)):
        column_third = ref[slots].astype(F32)[:, 2:3]
        weight = jnp.zeros((1, orbs), F32)
        for g in range(pairs_ref.shape[0]):
            weight = jnp.where(row_block == g, pairs_ref[g, k, column_block].astype(F32), weight)
        weight = jnp.where(jnp.abs(row_third - column_third) <= float(NEAR), weight, 0.0)
        gram_ref[k] = sums[k - 2][:share] * weight
        ham_ref[k] = sums[k - 2][share:] * weight


def products(ids, pairs, row_third, rows, others, v, total_rows, orbs):
    slots, share, cells = rows[0].shape
    patch = v.shape[0] // 3
    slots -= 1
    long = total_rows * cells
    vm = pl.BlockSpec(memory_space=pltpu.VMEM)
    sm = pl.BlockSpec(memory_space=pltpu.SMEM)
    params = pltpu.CompilerParams(vmem_limit_bytes=26 * 2**20)
    cost = pl.CostEstimate(flops=3 * 10**9, bytes_accessed=10 * 10**6, transcendentals=0)
    sizes = dict(patch=patch, total_rows=total_rows)

    def scratch(quads):
        tall = quads * slots // 2 * share
        return [
            pltpu.VMEM((3 * quads, 2, share, cells), BF),
            pltpu.VMEM((quads, share, cells), F32),
            pltpu.VMEM((tall, 2 * cells), BF),
            pltpu.VMEM((tall, 4 * cells), BF),
            pltpu.VMEM((2 * cells, 2 * cells), BF),
            pltpu.VMEM((tall, 2 * cells), F32),
        ]

    b = pl.pallas_call(
        functools.partial(own_kernel, **sizes),
        in_specs=[vm] * 2,
        out_specs=vm,
        out_shape=jax.ShapeDtypeStruct((3, 2 * share, long), BF),
        scratch_shapes=scratch(3),
        compiler_params=params,
        cost_estimate=cost,
    )(rows[0], v)
    a, own_sum = pl.pallas_call(
        functools.partial(rows_kernel, **sizes),
        in_specs=[sm] + [vm] * 5,
        out_specs=[vm] * 2,
        out_shape=[jax.ShapeDtypeStruct((3, orbs, long), BF), jax.ShapeDtypeStruct((2 * share, orbs), F32)],
        scratch_shapes=[pltpu.VMEM((3, 2, share, cells), BF)],
        compiler_params=params,
        cost_estimate=cost,
    )(ids, *rows, b)
    out = jax.ShapeDtypeStruct((5, share, orbs), F32)
    return pl.pallas_call(
        functools.partial(others_kernel, **sizes),
        in_specs=[sm, sm] + [vm] * 9,
        out_specs=[vm, vm],
        out_shape=[out, out],
        scratch_shapes=[pltpu.VMEM((3, 4 * share, long), BF)] + scratch(2),
        compiler_params=params,
        cost_estimate=cost,
    )(ids, pairs, row_third, rows[0], *others, a, v, own_sum)


def hop(x, k):
    return lax.ppermute(x, "mat", [(i, i ^ k) for i in range(lax.axis_size("mat"))])


def along(x, distance):
    size = lax.axis_size("dom")
    return lax.ppermute(x, "dom", [((i - distance) % size, i) for i in range(size)])


def on_device(orbitals, potential, centre_first, centre_second, centre_third, correlation_pairs):
    orbs, window, rows, cells = orbitals.shape
    patch = potential.shape[0]
    parts = lax.axis_size("mat")
    ids = lax.axis_index("mat")[None]

    field = jnp.concatenate([along(potential, 1), potential, along(potential, -1)], axis=0)
    fields = [field] + [hop(field, k) for k in range(1, parts)]

    diag, far, near, own = pack(ids, centre_first, centre_second, centre_third, orbitals, parts, patch)
    centres = jnp.stack([centre_first, centre_second, centre_third], axis=1).astype(F32)
    merged, v = merge_rows(ids, (own, hop(near, 1), hop(far, 2), hop(diag, 3)), centres, fields)

    others = [along(merged, d) for d in (2, 1, -1, -2)]
    far = hop(merged, 2)
    near = hop(merged, 1)
    diag = hop(far, 1)
    row_third = centre_third.astype(F32)[None, :]
    return tuple(products(ids, correlation_pairs, row_third, (merged, near, far, diag), others, v, rows * parts, orbs))


def solution(mesh):
    return jax.shard_map(
        on_device,
        mesh=mesh,
        in_specs=(
            P("dom", None, "mat", None),
            P("dom", "mat", None),
            P("dom"),
            P("dom"),
            P("dom"),
            P("dom", None, None),
        ),
        out_specs=(P(None, "mat", "dom"), P(None, "mat", "dom")),
        check_vma=False,
    )
```

time: 410 us -> 69.2 us (0.17)
  waiting for transfers between devices: 266 us -> 14.5 us
  other arithmetic: 50 us -> 0.01 us
  local copies, waits for them, and re-layouts: 41.1 us -> 1.88 us
  Pallas kernels: 0 us -> 32.8 us
  matrix products: 21.5 us -> 0 us
  between operations: 14.2 us -> 0.76 us
    ppermute x8 -> x15, waiting for transfers between devices: 207 us -> 14.5 us  [the longest x9 7.5 us: hop(): lax.ppermute(x, 'mat', [(i, i ^ k) for i in range(lax.axis_size('mat'))])]
    reduce_scatter x2 -> x0, waiting for transfers between devices: 58.8 us -> none  [the longest x1 35.8 us: on_device(): lax.psum_scatter(gram_full, 'mat', scatter_dimension=1, tiled=True)]
    pallas_call x0 -> x5, Pallas kernels: none -> 32.8 us  [the longest x1 13.8 us: products(): pl.pallas_call(functools.partial(others_kernel, **sizes), in_specs=[sm, s...]
    another operation x2 -> x0, other arithmetic: 25.1 us -> none  [on_device(): paired = jnp.stack([masked, applied])]
    dot_general x4 -> x0, matrix products: 21.5 us -> none  [the longest x1 10.1 us: on_device(): lax.dot_general(orbital_block, orbital_block, (((1,), (1,)), ((), ())), p...]
    dot_general x2 -> x0, local copies, waits for them, and re-layouts: 20.6 us -> none  [the longest x1 10.3 us: on_device(): lax.dot_general(orbital_block, orbital_block, (((1,), (1,)), ((), ())), p...]
    slice x4 -> x0, local copies, waits for them, and re-layouts: 20.4 us -> none  [the longest x2 13.7 us: on_device(): applied_block = slot_stack[1].reshape(3 * block_orbs, -1)]
    concatenate x3 -> x0, other arithmetic: 13.1 us -> none  [the longest x1 9.87 us: on_device(): slot_stack = jnp.concatenate([received[0], middle, received[1]], axis=1)]
  transfers between devices with their start and end apart: 10 -> 15, of which waited for: 8 -> 5; matrix products, arithmetic and copies ran while one was open for 3% -> 1% of each run, Pallas kernels for 0% -> 27%
where the time goes in v2:
time: 69.2 us; the launch traced here: 68.9 us
  Pallas kernels  32.8 us (47%)
  starting transfers between devices  18.9 us (27%)
  waiting for transfers between devices  14.5 us (21%)
  local copies, waits for them, and re-layouts  1.88 us (3%)
  between operations  0.76 us (1%)
    pallas_call x1, Pallas kernels, products(): pl.pallas_call(functools.partial(others_kernel, **sizes), in_specs=[sm, s...  13.8 us
    ppermute x6, starting transfers between devices, along(): lax.ppermute(x, 'dom', [((i - distance) % size, i) for i in range(size)])  13.1 us
    pallas_call x1, Pallas kernels, pack(): pl.pallas_call(functools.partial(pack_kernel, patch=patch, rows=rows, tot...  8.81 us
    ppermute x9, waiting for transfers between devices, hop(): lax.ppermute(x, 'mat', [(i, i ^ k) for i in range(lax.axis_size('mat'))])  7.5 us
    ppermute x6, waiting for transfers between devices, along(): lax.ppermute(x, 'dom', [((i - distance) % size, i) for i in range(size)])  7.02 us
    pallas_call x1, Pallas kernels, products(): pl.pallas_call(functools.partial(rows_kernel, **sizes), in_specs=[sm] + [...  5.91 us
    ppermute x9, starting transfers between devices, hop(): lax.ppermute(x, 'mat', [(i, i ^ k) for i in range(lax.axis_size('mat'))])  5.83 us
    pallas_call x1, Pallas kernels, products(): pl.pallas_call(functools.partial(own_kernel, **sizes), in_specs=[vm] * 2,...  4.21 us
  transfers between devices with their start and end apart: 15, of which 5 were waited for; matrix products, arithmetic and copies ran while one was open for 1% of the time, Pallas kernels for 27%

profile of v2, /device:TPU:0, one launch (start us, length us, event | category | flops | bytes accessed | tf_op | source)
XLA Modules:
  0.0 68.9 jit_solution(7546909337901456120)
XLA Ops:
  0.7 3.0 %collective-permute-start.3 = (f32[4,8,128]{2,1,0:T(8,128)}, f32[4,8,128]{2,1,0:T(8,128)S(1)}, u32[]{:S(2)}, u32[]{:S(2)}) collective-permute-start(f32[4,8,128]{2,1,0:T(8,128)} %param.7), channel_id=1, source_target_pairs={{28,0},{0,4},{4,8},{8,12},{12,16},{16,20},{20,24},{24,28},{29,1},{... | collective-permute-start | bytes 49160 | tf_op jit(solution)/shard_map/ppermute | solution.py:432
  3.7 3.1 %collective-permute-start.4 = (f32[4,8,128]{2,1,0:T(8,128)}, f32[4,8,128]{2,1,0:T(8,128)S(1)}, u32[]{:S(2)}, u32[]{:S(2)}) collective-permute-start(f32[4,8,128]{2,1,0:T(8,128)} %param.7), channel_id=1, source_target_pairs={{4,0},{8,4},{12,8},{16,12},{20,16},{24,20},{28,24},{0,28},{5,1},{9... | collective-permute-start | bytes 49160 | tf_op jit(solution)/shard_map/ppermute | solution.py:432
  6.8 1.9 %collective-permute-done.3 = f32[4,8,128]{2,1,0:T(8,128)S(1)} collective-permute-done((f32[4,8,128]{2,1,0:T(8,128)}, f32[4,8,128]{2,1,0:T(8,128)S(1)}, u32[]{:S(2)}, u32[]{:S(2)}) %collective-permute-start.3) | collective-permute-done | bytes 16416 | tf_op jit(solution)/shard_map/ppermute | solution.py:432
  8.7 0.7 %constant_dynamic-update-slice_fusion.1 = f32[12,8,128]{2,1,0:T(8,128)S(1)} fusion(f32[12,8,128]{2,1,0:T(8,128)S(1)} %constant_dynamic-update-slice_fusion.2, f32[4,8,128]{2,1,0:T(8,128)} %param.7), kind=kLoop, calls=%fused_computation.1 | loop fusion | bytes 32768
  9.4 8.8 %shard_map.77 = (bf16[8,64,128]{2,1,0:T(8,128)(2,1)}, bf16[8,64,128]{2,1,0:T(8,128)(2,1)}, bf16[8,64,128]{2,1,0:T(8,128)(2,1)}, bf16[8,64,128]{2,1,0:T(8,128)(2,1)}) custom-call(s32[1]{0:T(128)} %bitcast.ids_ref, s32[256]{0:T(256)} %first_ref.1, s32[256]{0:T(256)} %second_ref.1, s32[256]{0:T(256)} %third_ref.1, bf16[256,96,128]{2,1,0:T(8,128)(2,1)} %bitcast.7), custom_call_target="tpu_custom_call" | custom-call | flops 402653184 | bytes 6291456 | tf_op jit(solution)/shard_map/pallas_call | solution.py:91
  18.2 0.6 collective-permute-start
  18.8 1.7 %collective-permute-start.1 = (bf16[8,64,128]{2,1,0:T(8,128)(2,1)}, bf16[8,64,128]{2,1,0:T(8,128)(2,1)S(1)}, u32[]{:S(2)}, u32[]{:S(2)}) collective-permute-start(bf16[8,64,128]{2,1,0:T(8,128)(2,1)} %get-tuple-element.12), channel_id=1, source_target_pairs={{0,2},{1,3},{2,0},{3,1},{4,6},{5,7},{6,4},{7,5},{8,10},{9,11},{10,... | collective-permute-start | bytes 393224 | tf_op jit(solution)/shard_map/ppermute | solution.py:427
  20.4 1.4 %collective-permute-start.6 = (f32[12,8,128]{2,1,0:T(8,128)S(1)}, f32[12,8,128]{2,1,0:T(8,128)S(1)}, u32[]{:S(2)}, u32[]{:S(2)}) collective-permute-start(f32[12,8,128]{2,1,0:T(8,128)S(1)} %constant_dynamic-update-slice_fusion.rest_0_), channel_id=1, source_target_pairs={{0,2},{1,3},{2,0},{3,1},{4,6},{5,7},{6,4},{7,5},{8,10},{9,11},{10,... | collective-permute-start | bytes 147464 | tf_op jit(solution)/shard_map/ppermute | solution.py:427
  21.9 0.4 collective-permute-start.7
  22.3 0.1 copy.15.centre_ref
  22.4 6.4 %collective-permute-done.6.rest_2_ = f32[12,8,128]{2,1,0:T(8,128)S(1)} collective-permute-done((f32[12,8,128]{2,1,0:T(8,128)S(1)}, f32[12,8,128]{2,1,0:T(8,128)S(1)}, u32[]{:S(2)}, u32[]{:S(2)}) %collective-permute-start.6) | collective-permute-done | bytes 49184 | tf_op jit(solution)/shard_map/ppermute | solution.py:427
  28.9 0.9 %copy-done = bf16[8,64,128]{2,1,0:T(8,128)(2,1)S(1)} copy-done((bf16[8,64,128]{2,1,0:T(8,128)(2,1)S(1)}, bf16[8,64,128]{2,1,0:T(8,128)(2,1)}, u32[]{:S(2)}) %copy-start) | copy-done | bytes 131096
  29.8 0.2 shard_map.78
  29.9 1.7 %collective-permute-start.13 = (bf16[17,64,128]{2,1,0:T(8,128)(2,1)S(1)}, bf16[17,64,128]{2,1,0:T(8,128)(2,1)S(1)}, u32[]{:S(2)}, u32[]{:S(2)}) collective-permute-start(bf16[17,64,128]{2,1,0:T(8,128)(2,1)S(1)} %get-tuple-element.14.own_ref), channel_id=1, source_target_pairs={{0,2},{1,3},{2,0},{3,1},{4,6},{5,7},{6,4},{7,5},{8,10},{9,11},{10,... | collective-permute-start | bytes 835592 | tf_op jit(solution)/shard_map/ppermute | solution.py:427
  31.7 0.1 copy.16.pairs_ref
  31.8 4.0 %collective-permute-start.10 = (bf16[17,64,128]{2,1,0:T(8,128)(2,1)S(1)}, bf16[17,64,128]{2,1,0:T(8,128)(2,1)S(1)}, u32[]{:S(2)}, u32[]{:S(2)}) collective-permute-start(bf16[17,64,128]{2,1,0:T(8,128)(2,1)S(1)} %get-tuple-element.14.own_ref), channel_id=1, source_target_pairs={{4,0},{8,4},{12,8},{16,12},{20,16},{24,20},{28,24},{0,28},{5,1},{9... | collective-permute-start | bytes 835592 | tf_op jit(solution)/shard_map/ppermute | solution.py:432
  35.8 2.0 %collective-permute-start.8 = (bf16[17,64,128]{2,1,0:T(8,128)(2,1)S(1)}, bf16[17,64,128]{2,1,0:T(8,128)(2,1)S(1)}, u32[]{:S(2)}, u32[]{:S(2)}) collective-permute-start(bf16[17,64,128]{2,1,0:T(8,128)(2,1)S(1)} %get-tuple-element.14.own_ref), channel_id=1, source_target_pairs={{24,0},{28,4},{0,8},{4,12},{8,16},{12,20},{16,24},{20,28},{25,1},{... | collective-permute-start | bytes 835592 | tf_op jit(solution)/shard_map/ppermute | solution.py:432
  37.8 1.1 %collective-permute-done.13.far_ref = bf16[17,64,128]{2,1,0:T(8,128)(2,1)S(1)} collective-permute-done((bf16[17,64,128]{2,1,0:T(8,128)(2,1)S(1)}, bf16[17,64,128]{2,1,0:T(8,128)(2,1)S(1)}, u32[]{:S(2)}, u32[]{:S(2)}) %collective-permute-start.13) | collective-permute-done | bytes 278560 | tf_op jit(solution)/shard_map/ppermute | solution.py:427
  38.9 4.2 %shard_map.79.b_ref = bf16[3,128,4096]{2,1,0:T(8,128)(2,1)S(1)} custom-call(bf16[17,64,128]{2,1,0:T(8,128)(2,1)S(1)} %get-tuple-element.14.own_ref, f32[12,32,128]{2,1,0:T(8,128)S(1)} %get-tuple-element.15.v_ref), custom_call_target="tpu_custom_call" | custom-call | flops 3000000000 | bytes 10000000 | tf_op jit(solution)/shard_map/pallas_call | solution.py:396
  43.1 0.9 %collective-permute-start.9 = (bf16[17,64,128]{2,1,0:T(8,128)(2,1)S(1)}, bf16[17,64,128]{2,1,0:T(8,128)(2,1)S(1)}, u32[]{:S(2)}, u32[]{:S(2)}) collective-permute-start(bf16[17,64,128]{2,1,0:T(8,128)(2,1)S(1)} %get-tuple-element.14.own_ref), channel_id=1, source_target_pairs={{28,0},{0,4},{4,8},{8,12},{12,16},{16,20},{20,24},{24,28},{29,1},{... | collective-permute-start | bytes 835592 | tf_op jit(solution)/shard_map/ppermute | solution.py:432
  44.0 5.9 %shard_map.80 = (bf16[3,256,4096]{2,1,0:T(8,128)(2,1)S(1)}, f32[128,256]{1,0:T(8,128)S(1)}) custom-call(s32[1]{0:T(128)} %bitcast.ids_ref, bf16[17,64,128]{2,1,0:T(8,128)(2,1)S(1)} %get-tuple-element.14.own_ref, bf16[17,64,128]{2,1,0:T(8,128)(2,1)S(1)} %collective-permute-done.12.near_ref, bf16[17,64,128]{2,1,0:T(8,128)(2,1)S(1)} %collective-permute-done.13.far_ref, ...), custom_call_target="tpu_custom_call" | custom-call | flops 3000000000 | bytes 10000000 | tf_op jit(solution)/shard_map/pallas_call | solution.py:405
  50.0 4.8 %collective-permute-done.8.low2_ref = bf16[17,64,128]{2,1,0:T(8,128)(2,1)S(1)} collective-permute-done((bf16[17,64,128]{2,1,0:T(8,128)(2,1)S(1)}, bf16[17,64,128]{2,1,0:T(8,128)(2,1)S(1)}, u32[]{:S(2)}, u32[]{:S(2)}) %collective-permute-start.8) | collective-permute-done | bytes 278560 | tf_op jit(solution)/shard_map/ppermute | solution.py:432
  54.7 0.4 collective-permute-done.9.low1_ref
  55.1 13.8 %shard_map.81 = (f32[5,64,256]{2,1,0:T(8,128)}, f32[5,64,256]{2,1,0:T(8,128)}) custom-call(s32[1]{0:T(128)} %bitcast.ids_ref, s32[2,5,2]{2,1,0:T(8,128)S(1)} %copy.16.pairs_ref, f32[1,256]{1,0:T(1,128)S(1)} %bitcast.6, bf16[17,64,128]{2,1,0:T(8,128)(2,1)S(1)} %get-tuple-element.14.own_ref, bf16[17,64,128]{2,1,0:T(8,128)(2,1)S(1)} %collective-permute-done.8.low2_ref, ...), custom_call_target="tpu_custom_call" | custom-call | flops 3000000000 | bytes 10000000 | tf_op jit(solution)/shard_map/pallas_call | solution.py:415
  (28 shorter events, 0.1 us)
Async XLA Ops:
  0.6 21.7 %copy-start.1 = (s32[256]{0:T(256)S(1)}, s32[256]{0:T(256)}, u32[]{:S(2)}) copy-start(s32[256]{0:T(256)} %third_ref.1) | copy-start | bytes 3076
  0.6 21.6 %copy-start.2 = (s32[256]{0:T(256)S(1)}, s32[256]{0:T(256)}, u32[]{:S(2)}) copy-start(s32[256]{0:T(256)} %first_ref.1) | copy-start | bytes 3076
  0.7 21.6 %copy-start.3 = (s32[256]{0:T(256)S(1)}, s32[256]{0:T(256)}, u32[]{:S(2)}) copy-start(s32[256]{0:T(256)} %second_ref.1) | copy-start | bytes 3076
  0.7 31.0 %copy-start.4 = (s32[2,5,2]{1,2,0:T(2,128)S(1)}, s32[2,5,2]{1,2,0:T(2,128)}, u32[]{:S(2)}) copy-start(s32[2,5,2]{1,2,0:T(2,128)} %param.11) | copy-start | bytes 244
  0.7 8.0 %collective-permute-start.3 = (f32[4,8,128]{2,1,0:T(8,128)}, f32[4,8,128]{2,1,0:T(8,128)S(1)}, u32[]{:S(2)}, u32[]{:S(2)}) collective-permute-start(f32[4,8,128]{2,1,0:T(8,128)} %param.7), channel_id=1, source_target_pairs={{28,0},{0,4},{4,8},{8,12},{12,16},{16,20},{20,24},{24,28},{29,1},{... | collective-permute-start | bytes 49160 | tf_op jit(solution)/shard_map/ppermute | solution.py:432
  3.7 5.7 %collective-permute-start.4 = (f32[4,8,128]{2,1,0:T(8,128)}, f32[4,8,128]{2,1,0:T(8,128)S(1)}, u32[]{:S(2)}, u32[]{:S(2)}) collective-permute-start(f32[4,8,128]{2,1,0:T(8,128)} %param.7), channel_id=1, source_target_pairs={{4,0},{8,4},{12,8},{16,12},{20,16},{24,20},{28,24},{0,28},{5,1},{9... | collective-permute-start | bytes 49160 | tf_op jit(solution)/shard_map/ppermute | solution.py:432
  9.4 12.5 %collective-permute-start.5 = (f32[12,8,128]{2,1,0:T(8,128)S(1)}, f32[12,8,128]{2,1,0:T(8,128)S(1)}, u32[]{:S(2)}, u32[]{:S(2)}) collective-permute-start(f32[12,8,128]{2,1,0:T(8,128)S(1)} %constant_dynamic-update-slice_fusion.rest_0_), channel_id=1, source_target_pairs={{0,1},{1,0},{2,3},{3,2},{4,5},{5,4},{6,7},{7,6},{8,9},{9,8},{10,11... | collective-permute-start | bytes 147464 | tf_op jit(solution)/shard_map/ppermute | solution.py:427
  18.2 10.7 %collective-permute-start = (bf16[8,64,128]{2,1,0:T(8,128)(2,1)}, bf16[8,64,128]{2,1,0:T(8,128)(2,1)S(1)}, u32[]{:S(2)}, u32[]{:S(2)}) collective-permute-start(bf16[8,64,128]{2,1,0:T(8,128)(2,1)} %get-tuple-element.11), channel_id=1, source_target_pairs={{0,1},{1,0},{2,3},{3,2},{4,5},{5,4},{6,7},{7,6},{8,9},{9,8},{10,11... | collective-permute-start | bytes 393224 | tf_op jit(solution)/shard_map/ppermute | solution.py:427
  18.8 10.1 %collective-permute-start.1 = (bf16[8,64,128]{2,1,0:T(8,128)(2,1)}, bf16[8,64,128]{2,1,0:T(8,128)(2,1)S(1)}, u32[]{:S(2)}, u32[]{:S(2)}) collective-permute-start(bf16[8,64,128]{2,1,0:T(8,128)(2,1)} %get-tuple-element.12), channel_id=1, source_target_pairs={{0,2},{1,3},{2,0},{3,1},{4,6},{5,7},{6,4},{7,5},{8,10},{9,11},{10,... | collective-permute-start | bytes 393224 | tf_op jit(solution)/shard_map/ppermute | solution.py:427
  20.4 8.4 %collective-permute-start.2 = (bf16[8,64,128]{2,1,0:T(8,128)(2,1)}, bf16[8,64,128]{2,1,0:T(8,128)(2,1)S(1)}, u32[]{:S(2)}, u32[]{:S(2)}) collective-permute-start(bf16[8,64,128]{2,1,0:T(8,128)(2,1)} %get-tuple-element.13), channel_id=1, source_target_pairs={{0,3},{1,2},{2,1},{3,0},{4,7},{5,6},{6,5},{7,4},{8,11},{9,10},{10,... | collective-permute-start | bytes 393224 | tf_op jit(solution)/shard_map/ppermute | solution.py:427
  20.4 8.4 %collective-permute-start.6 = (f32[12,8,128]{2,1,0:T(8,128)S(1)}, f32[12,8,128]{2,1,0:T(8,128)S(1)}, u32[]{:S(2)}, u32[]{:S(2)}) collective-permute-start(f32[12,8,128]{2,1,0:T(8,128)S(1)} %constant_dynamic-update-slice_fusion.rest_0_), channel_id=1, source_target_pairs={{0,2},{1,3},{2,0},{3,1},{4,6},{5,7},{6,4},{7,5},{8,10},{9,11},{10,... | collective-permute-start | bytes 147464 | tf_op jit(solution)/shard_map/ppermute | solution.py:427
  21.9 7.0 %collective-permute-start.7 = (f32[12,8,128]{2,1,0:T(8,128)S(1)}, f32[12,8,128]{2,1,0:T(8,128)S(1)}, u32[]{:S(2)}, u32[]{:S(2)}) collective-permute-start(f32[12,8,128]{2,1,0:T(8,128)S(1)} %constant_dynamic-update-slice_fusion.rest_0_), channel_id=1, source_target_pairs={{0,3},{1,2},{2,1},{3,0},{4,7},{5,6},{6,5},{7,4},{8,11},{9,10},{10,... | collective-permute-start | bytes 147464 | tf_op jit(solution)/shard_map/ppermute | solution.py:427
  28.9 0.9 %copy-start = (bf16[8,64,128]{2,1,0:T(8,128)(2,1)S(1)}, bf16[8,64,128]{2,1,0:T(8,128)(2,1)}, u32[]{:S(2)}) copy-start(bf16[8,64,128]{2,1,0:T(8,128)(2,1)} %get-tuple-element.10.own_ref) | copy-start | bytes 393220
  29.9 9.0 %collective-permute-start.13 = (bf16[17,64,128]{2,1,0:T(8,128)(2,1)S(1)}, bf16[17,64,128]{2,1,0:T(8,128)(2,1)S(1)}, u32[]{:S(2)}, u32[]{:S(2)}) collective-permute-start(bf16[17,64,128]{2,1,0:T(8,128)(2,1)S(1)} %get-tuple-element.14.own_ref), channel_id=1, source_target_pairs={{0,2},{1,3},{2,0},{3,1},{4,6},{5,7},{6,4},{7,5},{8,10},{9,11},{10,... | collective-permute-start | bytes 835592 | tf_op jit(solution)/shard_map/ppermute | solution.py:427
  31.8 11.4 %collective-permute-start.12 = (bf16[17,64,128]{2,1,0:T(8,128)(2,1)S(1)}, bf16[17,64,128]{2,1,0:T(8,128)(2,1)S(1)}, u32[]{:S(2)}, u32[]{:S(2)}) collective-permute-start(bf16[17,64,128]{2,1,0:T(8,128)(2,1)S(1)} %get-tuple-element.14.own_ref), channel_id=1, source_target_pairs={{0,1},{1,0},{2,3},{3,2},{4,5},{5,4},{6,7},{7,6},{8,9},{9,8},{10,11... | collective-permute-start | bytes 835592 | tf_op jit(solution)/shard_map/ppermute | solution.py:427
  31.8 18.1 %collective-permute-start.10 = (bf16[17,64,128]{2,1,0:T(8,128)(2,1)S(1)}, bf16[17,64,128]{2,1,0:T(8,128)(2,1)S(1)}, u32[]{:S(2)}, u32[]{:S(2)}) collective-permute-start(bf16[17,64,128]{2,1,0:T(8,128)(2,1)S(1)} %get-tuple-element.14.own_ref), channel_id=1, source_target_pairs={{4,0},{8,4},{12,8},{16,12},{20,16},{24,20},{28,24},{0,28},{5,1},{9... | collective-permute-start | bytes 835592 | tf_op jit(solution)/shard_map/ppermute | solution.py:432
  35.8 14.2 %collective-permute-start.11 = (bf16[17,64,128]{2,1,0:T(8,128)(2,1)S(1)}, bf16[17,64,128]{2,1,0:T(8,128)(2,1)S(1)}, u32[]{:S(2)}, u32[]{:S(2)}) collective-permute-start(bf16[17,64,128]{2,1,0:T(8,128)(2,1)S(1)} %get-tuple-element.14.own_ref), channel_id=1, source_target_pairs={{8,0},{12,4},{16,8},{20,12},{24,16},{28,20},{0,24},{4,28},{9,1},{1... | collective-permute-start | bytes 835592 | tf_op jit(solution)/shard_map/ppermute | solution.py:432
  35.8 18.9 %collective-permute-start.8 = (bf16[17,64,128]{2,1,0:T(8,128)(2,1)S(1)}, bf16[17,64,128]{2,1,0:T(8,128)(2,1)S(1)}, u32[]{:S(2)}, u32[]{:S(2)}) collective-permute-start(bf16[17,64,128]{2,1,0:T(8,128)(2,1)S(1)} %get-tuple-element.14.own_ref), channel_id=1, source_target_pairs={{24,0},{28,4},{0,8},{4,12},{8,16},{12,20},{16,24},{20,28},{25,1},{... | collective-permute-start | bytes 835592 | tf_op jit(solution)/shard_map/ppermute | solution.py:432
  38.9 5.1 %collective-permute-start.14 = (bf16[17,64,128]{2,1,0:T(8,128)(2,1)S(1)}, bf16[17,64,128]{2,1,0:T(8,128)(2,1)S(1)}, u32[]{:S(2)}, u32[]{:S(2)}) collective-permute-start(bf16[17,64,128]{2,1,0:T(8,128)(2,1)S(1)} %collective-permute-done.13.far_ref), channel_id=1, source_target_pairs={{0,1},{1,0},{2,3},{3,2},{4,5},{5,4},{6,7},{7,6},{8,9},{9,8},{10,11... | collective-permute-start | bytes 835592 | tf_op jit(solution)/shard_map/ppermute | solution.py:427
  43.1 12.0 %collective-permute-start.9 = (bf16[17,64,128]{2,1,0:T(8,128)(2,1)S(1)}, bf16[17,64,128]{2,1,0:T(8,128)(2,1)S(1)}, u32[]{:S(2)}, u32[]{:S(2)}) collective-permute-start(bf16[17,64,128]{2,1,0:T(8,128)(2,1)S(1)} %get-tuple-element.14.own_ref), channel_id=1, source_target_pairs={{28,0},{0,4},{4,8},{8,12},{12,16},{16,20},{20,24},{24,28},{29,1},{... | collective-permute-start | bytes 835592 | tf_op jit(solution)/shard_map/ppermute | solution.py:432

commit v3 on v2

v3 whole, which is shorter than its diff:
```python
import functools

import jax
import jax.numpy as jnp
from jax import lax
from jax.experimental import pallas as pl
from jax.experimental.pallas import tpu as pltpu
from jax.sharding import PartitionSpec as P

STEP = 29
SKEW = STEP + 64
NEAR = 14
PAIR_SKEW, PAIR_ROW = 22, 32
P_STEP, P_UNROLL = 16, 1
A_PART, A_STEP, A_UNROLL = 16, 8, 1
S_PART, S_UNROLL = 32, 16
BF = jnp.bfloat16
F32 = jnp.float32
I32 = jnp.int32


def iota(shape, axis):
    return lax.broadcasted_iota(I32, shape, axis)


def half_of(m, own):
    return jnp.bitwise_xor(m // 2, 1 - own)


def pack_kernel(ids_ref, centre_in, x_ref, *rest, patch, rows, total_rows):
    *o_refs, landed, arrived, limits, scr, centre_ref, told = rest
    _, half, cells = o_refs[0].shape
    steps, count = landed.shape[:2]
    window = 3 * patch
    pairs = window // 2
    radius = window // 2
    m = ids_ref[0]

    def start_of(step):
        return pl.multiple_of(half_of(m, step * count // half) * half + step * count % half, count)

    copies = []
    for step in range(steps):
        copies.append(pltpu.make_async_copy(x_ref.at[pl.ds(start_of(step), count)], landed.at[step], arrived.at[step]))
        copies[-1].start()
    centre_copy = pltpu.make_async_copy(centre_in, centre_ref, told.at[0])
    centre_copy.start()

    plane = iota((2 * rows, cells), 0) // rows
    for a in range(pairs):
        p = plane + 2 * a
        inside = (p >= 1) & (p <= window - 2)
        for first in range(patch):
            off = p - patch - first
            limits[first, a] = jnp.where(inside, radius * radius - off * off, -1).astype(F32).astype(BF)
    z = iota((rows, cells), 1).astype(F32)
    y = (iota((rows, cells), 0) + m * rows).astype(F32)

    centre_copy.wait()
    for step in range(steps):
        copies[step].wait()

        def body(n, carry, base=start_of(step), step=step):
            found = []
            for i in range(P_STEP):
                at = n * P_STEP + i
                first = centre_ref[0, base + at]
                off_z = z - centre_ref[2, base + at].astype(F32)
                off_y = jnp.abs(y - centre_ref[1, base + at].astype(F32))
                off_y = jnp.minimum(off_y, float(total_rows) - off_y)
                distance = off_z * off_z + off_y * off_y
                distance = jnp.concatenate([distance, distance], axis=0).astype(BF)
                total = None
                for a in range(pairs):
                    x = landed[step, at, 2 * a * rows : 2 * (a + 1) * rows, :]
                    x = jnp.where(distance <= limits[first, a], x, jnp.zeros_like(x))
                    turn = 2 * SKEW * a % cells
                    total = x if total is None else total + pltpu.roll(x, turn, 1)
                odd = pltpu.roll(total, SKEW, 1)
                found.append((at, total.astype(F32)[:rows] + odd.astype(F32)[rows:]))
            for at, value in found:
                scr[at] = value
            return carry

        lax.fori_loop(0, count // P_STEP, body, 0, unroll=P_UNROLL)
        for r in range(rows):
            at = step * count % half
            o_refs[step * count // half][r, at : at + count, :] = scr[:, r, :].astype(BF)


def pack(ids, centres, orbitals, parts, patch):
    orbs, window, rows, cells = orbitals.shape
    steps = 8
    count = orbs // steps
    sm = pl.BlockSpec(memory_space=pltpu.SMEM)
    return pl.pallas_call(
        functools.partial(pack_kernel, patch=patch, rows=rows, total_rows=rows * parts),
        in_specs=[sm] + [pl.BlockSpec(memory_space=pl.ANY)] * 2,
        out_specs=[pl.BlockSpec(memory_space=pltpu.VMEM)] * 2,
        out_shape=[jax.ShapeDtypeStruct((rows, orbs // 2, cells), BF)] * 2,
        scratch_shapes=[
            pltpu.VMEM((steps, count, window * rows, cells), BF),
            pltpu.SemaphoreType.DMA((steps,)),
            pltpu.VMEM((patch, window // 2, 2 * rows, cells), BF),
            pltpu.VMEM((count, rows, cells), F32),
            pltpu.SMEM(centres.shape, I32),
            pltpu.SemaphoreType.DMA((1,)),
        ],
        compiler_params=pltpu.CompilerParams(vmem_limit_bytes=53 * 2**20),
        cost_estimate=pl.CostEstimate(flops=orbitals.size * 256, bytes_accessed=orbitals.size * 2, transcendentals=0),
    )(ids, centres, orbitals.reshape(orbs, window * rows, cells))


def merge_kernel(ids_ref, centre_ref, *refs, chips, own_only, patch):
    m = ids_ref[0]
    parity = m % 2
    o_refs = refs[4 * chips :]
    share = o_refs[0].shape[1]
    for chip in range(chips):
        own_ref, near_ref, far_ref, diag_ref = refs[4 * chip : 4 * chip + 4]
        rows, half, cells = own_ref.shape
        for n in [None] if own_only else range(half // share):
            o_ref = o_refs[0] if own_only else o_refs[chip * half // share + n]
            start = parity * share if own_only else n * share
            source = pl.ds(pl.multiple_of(start, share), share)
            centres = centre_ref[pl.ds(pl.multiple_of(half_of(m, 1 - chip) * half + start, share), share), :]
            lane = iota((share, cells), 1)
            meta = jnp.where(lane == 0, centres[:, 0:1], jnp.where(lane == 1, centres[:, 1:2], centres[:, 2:3]))
            o_ref[pl.ds(parity * rows, rows)] = own_ref[:, source, :] + far_ref[:, source, :]
            o_ref[pl.ds((1 - parity) * rows, rows)] = near_ref[:, source, :] + diag_ref[:, source, :]
            o_ref[2 * rows] = meta.astype(BF)
    if own_only:
        o_ref, low_ref, up_ref, gap_ref = o_refs
        source = Source(o_ref, 0, patch, 4 * rows, SKEW)
        source.gaps(gap_ref)
        tighten(source, gap_ref, range(2 * patch, 3 * patch - 1), low_ref)
        tighten(source, gap_ref, range(1, patch), up_ref)


def merge_rows(ids, centres, share, patch, own_only, *packs):
    rows, half, cells = packs[0][0].shape
    units = [2 * rows + 1, rows // 2 + 1, rows // 2 + 1] if own_only else [2 * rows + 1] * (len(packs) * half // share)
    return pl.pallas_call(
        functools.partial(merge_kernel, chips=len(packs), own_only=own_only, patch=patch),
        in_specs=[pl.BlockSpec(memory_space=pltpu.SMEM)] + [pl.BlockSpec(memory_space=pltpu.VMEM)] * (1 + 4 * len(packs)),
        out_specs=[pl.BlockSpec(memory_space=pltpu.VMEM)] * len(units),
        out_shape=[jax.ShapeDtypeStruct((n, share, cells), BF) for n in units],
        scratch_shapes=[pltpu.VMEM((2, 2 * rows, share, cells), BF)] if own_only else [],
        compiler_params=pltpu.CompilerParams(vmem_limit_bytes=16 * 2**20),
    )(ids, centres, *(array for pack in packs for array in pack))


class Source:
    def __init__(self, ref, hop, patch, total_rows, step=STEP):
        self.ref, self.hop, self.patch, self.total_rows, self.step = ref, hop, patch, total_rows, step
        self.slots = total_rows // 2
        units, self.share, self.cells = ref.shape
        meta = ref[units - 1].astype(F32)
        shape = (self.share, self.cells)
        self.first, self.second, self.third = (jnp.broadcast_to(meta[:, c : c + 1], shape) for c in range(3))
        self.start = iota(shape, 1) - self.third.astype(I32) + self.cells // 2

    def off(self, p):
        place = self.step * (p + self.patch * self.hop)
        return (jnp.bitwise_and(self.start - place, self.cells - 1) - self.cells // 2).astype(F32)

    def limit(self, p):
        off_z, off_x = self.off(p), float(p - self.patch) - self.first
        radius = 3 * self.patch // 2
        return float(radius * radius) - off_x * off_x - off_z * off_z

    def limits(self, plane_sets, out_ref):
        every = {p: self.limit(p) for p in sorted(set().union(*plane_sets))}
        for n, planes in enumerate(plane_sets):
            for odd in range(2):
                value = jnp.full((self.share, self.cells), -1.0, F32)
                for p in planes:
                    if p % 2 == odd:
                        value = jnp.maximum(value, every[p])
                out_ref[n, odd] = value.astype(BF)

    def gaps(self, gap_ref):
        row = self.second.astype(I32)
        for s in range(self.slots):
            ahead = s - row + self.slots // 2
            off = (jnp.bitwise_and(ahead, self.slots - 1) - self.slots // 2).astype(F32)
            gap_ref[0, s] = (off * off).astype(BF)
            gap_ref[1, s] = (jnp.bitwise_and(ahead, self.total_rows - 1) < self.slots).astype(F32).astype(BF)

    def packed(self, s, part):
        value = self.ref[s, part, :]
        turn = STEP * self.patch * self.hop
        even = pltpu.roll(value, turn % self.cells, 1) if turn % self.cells else value
        return even, pltpu.roll(value, (turn + self.cells // 2) % self.cells, 1)

    def parts(self, size):
        return [slice(c, c + size) for c in range(0, self.share, size)]


def tighten(source, gap_ref, planes, o_ref):
    half = source.slots // 2
    cells = source.cells
    limits = {p: source.limit(p).astype(BF) for p in planes}
    turn = (PAIR_SKEW - SKEW) % cells
    rows = []
    for r in range(half):
        total = None
        for later in range(2):
            s = r + half * later
            value, gap = source.ref[s], gap_ref[0, s]
            some = None
            for p in reversed(planes):
                piece = jnp.where(gap <= limits[p], value, jnp.zeros_like(value))
                some = piece if some is None else piece + pltpu.roll(some, turn, 1)
            total = total + pltpu.roll(some, PAIR_ROW, 1) if later else some
        rows.append(total + pltpu.roll(total, cells // 2, 1))
    lane = iota((source.share, cells), 1)
    for u in range(half // 2):
        o_ref[u] = jnp.where(lane < cells // 2, rows[u], rows[u + half // 2])
    o_ref[half // 2] = source.ref[source.ref.shape[0] - 1]


def loosen_kernel(low_ref, up_ref, low_out_ref, up_out_ref, gap_ref, *, patch, total_rows):
    for ref, o_ref, planes in ((low_ref, low_out_ref, range(2 * patch, 3 * patch - 1)), (up_ref, up_out_ref, range(1, patch))):
        source = Source(ref, 0, patch, total_rows, SKEW)
        source.gaps(gap_ref)
        cells, half = source.cells, source.slots // 2
        limits = {p: source.limit(p).astype(BF) for p in planes}
        lane = iota((source.share, cells), 1)
        for u in range(half // 2):
            value = ref[u]
            turned = pltpu.roll(value, cells // 2, 1)
            for group in range(2):
                both = jnp.where(lane < cells // 2, *((value, turned) if group == 0 else (turned, value)))
                for later in range(2):
                    s = u + half // 2 * group + half * later
                    gap = gap_ref[0, s]
                    total = jnp.zeros_like(value)
                    for p in planes:
                        turn = (SKEW - PAIR_SKEW) * (p - planes[0]) - PAIR_ROW * later
                        total = jnp.where(gap <= limits[p], pltpu.roll(both, turn % cells, 1) if turn else both, total)
                    o_ref[s] = total
        o_ref[source.slots] = ref[half // 2]


def loosen(low, up, patch, total_rows):
    slots = total_rows // 2
    vm = pl.BlockSpec(memory_space=pltpu.VMEM)
    return pl.pallas_call(
        functools.partial(loosen_kernel, patch=patch, total_rows=total_rows),
        in_specs=[vm] * 2,
        out_specs=[vm] * 2,
        out_shape=[jax.ShapeDtypeStruct((slots + 1, *low.shape[1:]), BF)] * 2,
        scratch_shapes=[pltpu.VMEM((2, slots, *low.shape[1:]), BF)],
        compiler_params=pltpu.CompilerParams(vmem_limit_bytes=16 * 2**20),
        cost_estimate=pl.CostEstimate(flops=10**6, bytes_accessed=10**4, transcendentals=0),
    )(low, up)


def inside(gap, limit_ref, n, part, even, odd):
    zero = jnp.zeros_like(even)
    return jnp.where(gap <= limit_ref[n, 0, part, :], even, jnp.where(gap <= limit_ref[n, 1, part, :], odd, zero))


def planes_of(quads, allowed, patch, shift):
    return [[p for p in range(patch * q + shift, patch * (q + 1) + shift) if p in allowed] for q in quads]


def spread_rows(source, limit_ref, gap_ref, quads, store):
    def body(n, carry):
        for part in source.parts(A_PART):
            found = []
            for step in range(A_STEP):
                s = n * A_STEP + step
                even, odd = source.packed(s, part)
                gap = gap_ref[0, s, part, :]
                is_low = gap_ref[1, s, part, :] > 0.5
                zero = jnp.zeros_like(even)
                for n_q, q in enumerate(quads):
                    value = inside(gap, limit_ref, n_q, part, even, odd)
                    found.append((q, s, part, jnp.where(is_low, value, zero)))
                    found.append((q, s + source.slots, part, jnp.where(is_low, zero, value)))
            for item in found:
                store(*item)
        return carry

    lax.fori_loop(0, source.slots // A_STEP, body, 0, unroll=A_UNROLL)


def columns(source, allowed, limit_ref, gap_ref, group_ref, v_ref, store):
    patch, cells, share, slots = source.patch, source.cells, source.share, source.slots
    shift = -patch * source.hop
    quads = sorted({(p - shift) // patch for p in allowed})
    sets = planes_of(quads, allowed, patch, shift) + planes_of(quads, allowed, patch, shift - 1) + planes_of(quads, allowed, patch, shift + 1)
    source.limits(sets, limit_ref)
    source.gaps(gap_ref)
    count = len(quads)
    for n, q in enumerate(quads):
        group = jnp.zeros((share, cells), F32)
        for g in range(1, patch):
            group = jnp.where(jnp.abs(source.off(patch * q + shift + g)) <= float(NEAR), float(g), group)
        group_ref[n] = group

    for part in source.parts(S_PART):

        def look(s, part=part):
            even, odd = source.packed(s, part)
            gap = gap_ref[0, s, part, :]
            return even, odd, [inside(gap, limit_ref, n, part, even, odd) for n in range(count)]

        def wide(values):
            return [value.astype(F32) for value in values]

        def body(s, carry, part=part):
            before, even, odd, now = carry
            next_even, next_odd, after = look(jnp.bitwise_and(s + 1, slots - 1))
            gap = gap_ref[0, s, part, :]
            low = gap_ref[1, s, part, :]
            low_packed = low > 0.5
            low_wide = low.astype(F32) > 0.5
            found = []
            for n, q in enumerate(quads):
                value = now[n]
                below = pltpu.roll(inside(gap, limit_ref, count + n, part, even, odd), STEP, 1)
                above = pltpu.roll(inside(gap, limit_ref, 2 * count + n, part, even, odd), cells - STEP, 1)
                beside = below.astype(F32) + above.astype(F32)
                beside = beside + (before[n].astype(F32) + after[n].astype(F32))
                beside = beside + (pltpu.roll(value, 1, 1).astype(F32) + pltpu.roll(value, cells - 1, 1).astype(F32))
                group = group_ref[n, part, :]
                field = None
                for g in range(patch):
                    row = jnp.where(low_wide, *(v_ref[patch * q + g, pl.ds(y, 1), :] for y in (s, s + slots)))
                    field = row if g == 0 else jnp.where(group == float(g), row, field)
                centre = value.astype(F32)
                applied = (0.5 * (6.0 * centre - beside) + field * centre).astype(BF)
                zero = jnp.zeros_like(value)
                found.append((q, 0, s, part, jnp.where(low_packed, value, zero)))
                found.append((q, 0, s + slots, part, jnp.where(low_packed, zero, value)))
                found.append((q, 1, s, part, jnp.where(low_packed, applied, zero)))
                found.append((q, 1, s + slots, part, jnp.where(low_packed, zero, applied)))
            for item in found:
                store(*item)
            return now, next_even, next_odd, after

        lax.fori_loop(0, slots, body, (look(slots - 1)[2], *look(0)), unroll=S_UNROLL)


def row_of(y, cells):
    return pl.ds(pl.multiple_of(y * cells, cells), cells)


def product_of(b, a):
    return lax.dot_general(b, a, (((1,), (1,)), ((), ())), preferred_element_type=F32)


def own_kernel(ids_ref, own_ref, *rest, patch, total_rows, parts):
    field_refs, (b_ref, v_ref, limit_ref, gap_ref, group_ref) = rest[:parts], rest[parts:]
    m = ids_ref[0]
    share, cells = own_ref.shape[1:]
    rows = total_rows // parts
    for hop, ref in enumerate(field_refs):
        to = pl.ds(pl.multiple_of(jnp.bitwise_xor(m, hop) * rows, rows), rows)
        for p in range(3 * patch):
            v_ref[p, to, :] = pltpu.roll(ref[p], STEP * p % cells, 1) if p else ref[p]

    def store_column(q, applied, y, part, value):
        at = applied * share
        b_ref[q, at + part.start : at + part.stop, row_of(y, cells)] = value

    source = Source(own_ref, 0, patch, total_rows)
    every = range(1, 3 * patch - 1)
    columns(source, every, limit_ref, gap_ref, group_ref, v_ref, store_column)


def rows_kernel(ids_ref, *refs, patch, total_rows, parts):
    row_refs, (b_ref, a_ref, sum_ref, limit_ref, gap_ref) = refs[:parts], refs[parts:]
    share, cells = row_refs[0].shape[1:]
    every = range(1, 3 * patch - 1)
    for n, ref in enumerate(row_refs):
        who = jnp.bitwise_xor(jnp.bitwise_and(ids_ref[0], 2), n) * share
        source = Source(ref, 0, patch, total_rows)
        source.limits(planes_of(range(3), every, patch, 0), limit_ref)
        source.gaps(gap_ref)

        def store_row(q, y, part, value, who=who):
            size = part.stop - part.start
            a_ref[q, pl.ds(pl.multiple_of(who + part.start, size), size), row_of(y, cells)] = value

        spread_rows(source, limit_ref, gap_ref, range(3), store_row)
    total = product_of(b_ref[0], a_ref[0])
    for q in range(1, 3):
        total = total + product_of(b_ref[q], a_ref[q])
    sum_ref[...] = total


def others_kernel(
    ids_ref, pairs_ref, row_third_ref, own_ref, low2_ref, low1_ref, up1_ref, up2_ref, a_ref, v_ref, sum_ref,
    gram_ref, ham_ref,
    b_ref, limit_ref, gap_ref, group_ref,
    *, patch, total_rows,
):
    m = ids_ref[0]
    slots = total_rows // 2
    share, cells = own_ref.shape[1:]
    both = 2 * share
    window = 3 * patch
    spots = {}
    for hop, ref, allowed in (
        (-1, low1_ref, range(patch, window - 1)),
        (1, up1_ref, range(1, 2 * patch)),
        (-2, low2_ref, range(2 * patch, window - 1)),
        (2, up2_ref, range(1, patch)),
    ):
        def store_column(q, applied, y, part, value, hop=hop):
            taken = sorted({q - 2, q - 1, q} - {0}).index(hop)
            spots[hop, q] = taken
            at = taken * both + applied * share
            b_ref[q, at + part.start : at + part.stop, row_of(y, cells)] = value

        source = Source(ref, hop, patch, total_rows)
        columns(source, allowed, limit_ref, gap_ref, group_ref, v_ref, store_column)

    sums = {0: sum_ref[...]}
    for q in range(3):
        product = product_of(b_ref[q], a_ref[q])
        for (hop, at_q), taken in spots.items():
            if at_q == q:
                piece = product[taken * both : (taken + 1) * both]
                sums[hop] = piece if hop not in sums else sums[hop] + piece

    orbs = a_ref.shape[1]
    half_rows = orbs // pairs_ref.shape[0]
    column_block = (m * share) // half_rows
    row_third = row_third_ref[...]
    row_block = iota((1, orbs), 1) // half_rows
    for k, ref in enumerate((low2_ref, low1_ref, own_ref, up1_ref, up2_ref)):
        column_third = ref[slots].astype(F32)[:, 2:3]
        weight = jnp.zeros((1, orbs), F32)
        for g in range(pairs_ref.shape[0]):
            weight = jnp.where(row_block == g, pairs_ref[g, k, column_block].astype(F32), weight)
        weight = jnp.where(jnp.abs(row_third - column_third) <= float(NEAR), weight, 0.0)
        gram_ref[k] = sums[k - 2][:share] * weight
        ham_ref[k] = sums[k - 2][share:] * weight


def products(ids, pairs, row_third, own, rows, others, fields, patch, total_rows, orbs):
    share, cells = rows[0].shape[1:]
    slots = total_rows // 2
    long = total_rows * cells
    vm = pl.BlockSpec(memory_space=pltpu.VMEM)
    sm = pl.BlockSpec(memory_space=pltpu.SMEM)
    params = pltpu.CompilerParams(vmem_limit_bytes=26 * 2**20)
    cost = pl.CostEstimate(flops=10**6, bytes_accessed=10**4, transcendentals=0)
    sizes = dict(patch=patch, total_rows=total_rows)

    def scratch(quads):
        return [
            pltpu.VMEM((3 * quads, 2, share, cells), BF),
            pltpu.VMEM((2, slots, share, cells), BF),
            pltpu.VMEM((quads, share, cells), F32),
        ]

    b, v = pl.pallas_call(
        functools.partial(own_kernel, **sizes, parts=len(rows)),
        in_specs=[sm] + [vm] * (1 + len(fields)),
        out_specs=[vm] * 2,
        out_shape=[jax.ShapeDtypeStruct((3, 2 * share, long), BF), jax.ShapeDtypeStruct((3 * patch, total_rows, cells), F32)],
        scratch_shapes=scratch(3),
        compiler_params=params,
        cost_estimate=cost,
    )(ids, own, *fields)
    a, own_sum = pl.pallas_call(
        functools.partial(rows_kernel, **sizes, parts=len(rows)),
        in_specs=[sm] + [vm] * (len(rows) + 1),
        out_specs=[vm] * 2,
        out_shape=[jax.ShapeDtypeStruct((3, orbs, long), BF), jax.ShapeDtypeStruct((2 * share, orbs), F32)],
        scratch_shapes=[pltpu.VMEM((3, 2, share, cells), BF), pltpu.VMEM((2, slots, share, cells), BF)],
        compiler_params=params,
        cost_estimate=cost,
    )(ids, *rows, b)
    out = jax.ShapeDtypeStruct((5, share, orbs), F32)
    return pl.pallas_call(
        functools.partial(others_kernel, **sizes),
        in_specs=[sm, sm] + [vm] * 9,
        out_specs=[vm, vm],
        out_shape=[out, out],
        scratch_shapes=[pltpu.VMEM((3, 4 * share, long), BF)] + scratch(2),
        compiler_params=params,
        cost_estimate=cost,
    )(ids, pairs, row_third, own, *others, a, v, own_sum)


def hop(x, k):
    return lax.ppermute(x, "mat", [(i, i ^ k) for i in range(lax.axis_size("mat"))])


def along(x, distance):
    size = lax.axis_size("dom")
    return lax.ppermute(x, "dom", [((i - distance) % size, i) for i in range(size)])


def on_device(orbitals, potential, centre_first, centre_second, centre_third, correlation_pairs):
    orbs, window, rows, cells = orbitals.shape
    patch = potential.shape[0]
    parts = lax.axis_size("mat")
    ids = lax.axis_index("mat")[None]

    centres = jnp.stack([centre_first, centre_second, centre_third])
    away, home = pack(ids, centres, orbitals, parts, patch)
    before, after = along(potential, 1), along(potential, -1)
    away, home, before, after = lax.optimization_barrier((away, home, before, after))
    far_home, far_away = hop(away, 2), hop(home, 2)
    near_home, near_away = hop(home, 1), hop(away, 1)
    field = jnp.concatenate([before, potential, after], axis=0)
    far_field = hop(field, 2)
    far_home, far_field = lax.optimization_barrier((far_home, far_field))
    centres = centres.T.astype(F32)
    share = orbs // parts
    homes = (home, near_home, far_home, hop(far_home, 1))
    merged, low2, up2 = merge_rows(ids, centres, share, patch, True, homes)
    low2, low1, up1, up2 = along(low2, 2), along(merged, 1), along(merged, -1), along(up2, -2)
    far_away, low2, up2 = lax.optimization_barrier((far_away, low2, up2))
    fields = (field, hop(field, 1), far_field, hop(far_field, 1))
    every = merge_rows(ids, centres, share, patch, False, homes, (away, near_away, far_away, hop(far_away, 1)))
    low2, up2 = loosen(low2, up2, patch, rows * parts)
    others = (low2, low1, up1, up2)
    row_third = centre_third.astype(F32)[None, :]
    return tuple(products(ids, correlation_pairs, row_third, merged, every, others, fields, patch, rows * parts, orbs))


def solution(mesh):
    return jax.shard_map(
        on_device,
        mesh=mesh,
        in_specs=(
            P("dom", None, "mat", None),
            P("dom", "mat", None),
            P("dom"),
            P("dom"),
            P("dom"),
            P("dom", None, None),
        ),
        out_specs=(P(None, "mat", "dom"), P(None, "mat", "dom")),
        check_vma=False,
    )
```

time: 69.2 us -> 56.7 us (0.82)
  waiting for transfers between devices: 14.5 us -> 10.1 us
  Pallas kernels: 32.8 us -> 28.4 us
  starting transfers between devices: 18.9 us -> 16.3 us
  local copies, waits for them, and re-layouts: 1.88 us -> 0.25 us
  other arithmetic: 0.01 us -> 0.72 us
    ppermute x6, waiting for transfers between devices: 7.02 us -> 1.22 us  [along(): lax.ppermute(x, 'dom', [((i - distance) % size, i) for i in range(size)])]
    pallas_call x1, Pallas kernels: 13.8 us -> 9.91 us  [products(): pl.pallas_call(functools.partial(others_kernel, **sizes), in_specs=[sm, s...]
    pallas_call x1, Pallas kernels: 8.81 us -> 6.69 us  [pack(): pl.pallas_call(functools.partial(pack_kernel, patch=patch, rows=rows, tot...]
    unnamed x13 -> x9, local copies, waits for them, and re-layouts: 1.74 us -> 0.12 us
    ppermute x9, starting transfers between devices: 5.83 us -> 4.3 us  [hop(): lax.ppermute(x, 'mat', [(i, i ^ k) for i in range(lax.axis_size('mat'))])]
    pallas_call x3 -> x5, Pallas kernels: 10.3 us -> 11.8 us  [the longest x1 6.24 us: products(): pl.pallas_call(functools.partial(rows_kernel, **sizes, parts=len(rows)),...]
    ppermute x9, waiting for transfers between devices: 7.5 us -> 8.88 us  [hop(): lax.ppermute(x, 'mat', [(i, i ^ k) for i in range(lax.axis_size('mat'))])]
    ppermute x6, starting transfers between devices: 13.1 us -> 12 us  [along(): lax.ppermute(x, 'dom', [((i - distance) % size, i) for i in range(size)])]
  transfers between devices with their start and end apart: 15 -> 15, of which waited for: 5 -> 5; matrix products, arithmetic and copies ran while one was open for 1% -> 2% of each run, Pallas kernels for 27% -> 33%
where the time goes in v3:
time: 56.7 us; the launch traced here: 56.6 us
  Pallas kernels  28.4 us (50%)
  starting transfers between devices  16.3 us (29%)
  waiting for transfers between devices  10.1 us (18%)
  between operations  0.8 us (1%)
  other arithmetic  0.72 us (1%)
    ppermute x6, starting transfers between devices, along(): lax.ppermute(x, 'dom', [((i - distance) % size, i) for i in range(size)])  12 us
    pallas_call x1, Pallas kernels, products(): pl.pallas_call(functools.partial(others_kernel, **sizes), in_specs=[sm, s...  9.91 us
    ppermute x9, waiting for transfers between devices, hop(): lax.ppermute(x, 'mat', [(i, i ^ k) for i in range(lax.axis_size('mat'))])  8.88 us
    pallas_call x1, Pallas kernels, pack(): pl.pallas_call(functools.partial(pack_kernel, patch=patch, rows=rows, tot...  6.69 us
    pallas_call x1, Pallas kernels, products(): pl.pallas_call(functools.partial(rows_kernel, **sizes, parts=len(rows)),...  6.24 us
    ppermute x9, starting transfers between devices, hop(): lax.ppermute(x, 'mat', [(i, i ^ k) for i in range(lax.axis_size('mat'))])  4.3 us
    pallas_call x1, Pallas kernels, products(): pl.pallas_call(functools.partial(own_kernel, **sizes, parts=len(rows)), i...  3.03 us
    pallas_call x2, Pallas kernels, merge_rows(): pl.pallas_call(functools.partial(merge_kernel, chips=len(packs), own_only...  1.36 us
  transfers between devices with their start and end apart: 15, of which 5 were waited for; matrix products, arithmetic and copies ran while one was open for 2% of the time, Pallas kernels for 33%

profile of v3, /device:TPU:0, one launch (start us, length us, event | category | flops | bytes accessed | tf_op | source)
XLA Modules:
  0.0 56.6 jit_solution(17195194436841279475)
XLA Ops:
  0.7 3.0 %collective-permute-start = (f32[4,8,128]{2,1,0:T(8,128)}, f32[4,8,128]{2,1,0:T(8,128)S(1)}, u32[]{:S(2)}, u32[]{:S(2)}) collective-permute-start(f32[4,8,128]{2,1,0:T(8,128)} %param.7), channel_id=1, source_target_pairs={{28,0},{0,4},{4,8},{8,12},{12,16},{16,20},{20,24},{24,28},{29,1},{... | collective-permute-start | bytes 49160 | tf_op jit(solution)/shard_map/ppermute | solution.py:499
  3.7 3.1 %collective-permute-start.1 = (f32[4,8,128]{2,1,0:T(8,128)}, f32[4,8,128]{2,1,0:T(8,128)S(1)}, u32[]{:S(2)}, u32[]{:S(2)}) collective-permute-start(f32[4,8,128]{2,1,0:T(8,128)} %param.7), channel_id=1, source_target_pairs={{4,0},{8,4},{12,8},{16,12},{20,16},{24,20},{28,24},{0,28},{5,1},{9... | collective-permute-start | bytes 49160 | tf_op jit(solution)/shard_map/ppermute | solution.py:499
  6.8 0.7 %pad_add_fusion = (s32[3,256]{1,0:T(4,128)S(1)}, f32[3,256]{1,0:T(4,128)S(1)}) fusion(s32[1,256]{1,0:T(1,128)} %bitcast.11, s32[1,256]{1,0:T(1,128)} %bitcast.12, s32[1,256]{1,0:T(1,128)} %bitcast.13), kind=kLoop, calls=%fused_computation.3 | loop fusion | flops 2304 | bytes 9216 | tf_op jit(solution)/shard_map/stack | solution.py:508
  7.5 6.7 %shard_map.77 = (bf16[8,128,128]{2,1,0:T(8,128)(2,1)S(1)}, bf16[8,128,128]{2,1,0:T(8,128)(2,1)S(1)}) custom-call(s32[1]{0:T(128)} %bitcast.ids_ref, s32[3,256]{1,0:T(4,128)S(1)} %get-tuple-element.50.centre_in, bf16[256,96,128]{2,1,0:T(8,128)(2,1)} %bitcast.10), custom_call_target="tpu_custom_call" | custom-call | flops 805306368 | bytes 6291456 | tf_op jit(solution)/shard_map/pallas_call | solution.py:96
  14.2 1.7 %collective-permute-start.3 = (bf16[8,128,128]{2,1,0:T(8,128)(2,1)S(1)}, bf16[8,128,128]{2,1,0:T(8,128)(2,1)S(1)}, u32[]{:S(2)}, u32[]{:S(2)}) collective-permute-start(bf16[8,128,128]{2,1,0:T(8,128)(2,1)S(1)} %get-tuple-element.29.refs_4_), channel_id=1, source_target_pairs={{0,2},{1,3},{2,0},{3,1},{4,6},{5,7},{6,4},{7,5},{8,10},{9,11},{10,... | collective-permute-start | bytes 786440 | tf_op jit(solution)/shard_map/ppermute | solution.py:494
  15.9 0.5 collective-permute-start.4
  16.4 6.7 %collective-permute-done.4.rest_2_ = f32[12,8,128]{2,1,0:T(8,128)S(1)} collective-permute-done((f32[12,8,128]{2,1,0:T(8,128)S(1)}, f32[12,8,128]{2,1,0:T(8,128)S(1)}, u32[]{:S(2)}, u32[]{:S(2)}) %collective-permute-start.4) | collective-permute-done | bytes 49184 | tf_op jit(solution)/shard_map/ppermute | solution.py:494
  23.1 1.5 %collective-permute-start.6 = (bf16[8,128,128]{2,1,0:T(8,128)(2,1)S(1)}, bf16[8,128,128]{2,1,0:T(8,128)(2,1)S(1)}, u32[]{:S(2)}, u32[]{:S(2)}) collective-permute-start(bf16[8,128,128]{2,1,0:T(8,128)(2,1)S(1)} %get-tuple-element.28.refs_0_), channel_id=1, source_target_pairs={{0,2},{1,3},{2,0},{3,1},{4,6},{5,7},{6,4},{7,5},{8,10},{9,11},{10,... | collective-permute-start | bytes 786440 | tf_op jit(solution)/shard_map/ppermute | solution.py:494
  24.6 0.1 copy.15
  24.8 1.1 %shard_map.78 = (bf16[17,64,128]{2,1,0:T(8,128)(2,1)S(1)}, bf16[5,64,128]{2,1,0:T(8,128)(2,1)S(1)}, bf16[5,64,128]{2,1,0:T(8,128)(2,1)S(1)}) custom-call(s32[1]{0:T(128)} %bitcast.ids_ref, f32[256,3]{1,0:T(8,128)S(1)} %bitcast.7, bf16[8,128,128]{2,1,0:T(8,128)(2,1)S(1)} %get-tuple-element.28.refs_0_, ...), custom_call_target="tpu_custom_call" | custom-call | tf_op jit(solution)/shard_map/pallas_call | solution.py:143
  25.9 3.8 %collective-permute-start.8 = (bf16[5,64,128]{2,1,0:T(8,128)(2,1)S(1)}, bf16[5,64,128]{2,1,0:T(8,128)(2,1)S(1)}, u32[]{:S(2)}, u32[]{:S(2)}) collective-permute-start(bf16[5,64,128]{2,1,0:T(8,128)(2,1)S(1)} %get-tuple-element.35), channel_id=1, source_target_pairs={{8,0},{12,4},{16,8},{20,12},{24,16},{28,20},{0,24},{4,28},{9,1},{1... | collective-permute-start | bytes 245768 | tf_op jit(solution)/shard_map/ppermute | solution.py:499
  29.8 2.0 %collective-permute-start.9 = (bf16[17,64,128]{2,1,0:T(8,128)(2,1)S(1)}, bf16[17,64,128]{2,1,0:T(8,128)(2,1)S(1)}, u32[]{:S(2)}, u32[]{:S(2)}) collective-permute-start(bf16[17,64,128]{2,1,0:T(8,128)(2,1)S(1)} %get-tuple-element.33.own_ref), channel_id=1, source_target_pairs={{28,0},{0,4},{4,8},{8,12},{12,16},{16,20},{20,24},{24,28},{29,1},{... | collective-permute-start | bytes 835592 | tf_op jit(solution)/shard_map/ppermute | solution.py:499
  31.8 0.1 collective-permute-done.6.refs_6_
  31.9 1.2 %collective-permute-done.7.low_ref = bf16[5,64,128]{2,1,0:T(8,128)(2,1)S(1)} collective-permute-done((bf16[5,64,128]{2,1,0:T(8,128)(2,1)S(1)}, bf16[5,64,128]{2,1,0:T(8,128)(2,1)S(1)}, u32[]{:S(2)}, u32[]{:S(2)}) %collective-permute-start.7) | collective-permute-done | bytes 81952 | tf_op jit(solution)/shard_map/ppermute | solution.py:499
  33.1 0.5 collective-permute-start.13
  33.6 1.1 %collective-permute-done.13.rest_1_ = f32[12,8,128]{2,1,0:T(8,128)S(1)} collective-permute-done((f32[12,8,128]{2,1,0:T(8,128)S(1)}, f32[12,8,128]{2,1,0:T(8,128)S(1)}, u32[]{:S(2)}, u32[]{:S(2)}) %collective-permute-start.13) | collective-permute-done | bytes 49184 | tf_op jit(solution)/shard_map/ppermute | solution.py:494
  34.7 0.1 collective-permute-start.14
  34.8 0.1 copy.16.pairs_ref
  34.9 1.0 %collective-permute-done.14.rest_3_ = f32[12,8,128]{2,1,0:T(8,128)S(1)} collective-permute-done((f32[12,8,128]{2,1,0:T(8,128)S(1)}, f32[12,8,128]{2,1,0:T(8,128)S(1)}, u32[]{:S(2)}, u32[]{:S(2)}) %collective-permute-start.14) | collective-permute-done | bytes 49184 | tf_op jit(solution)/shard_map/ppermute | solution.py:494
  35.9 3.0 %shard_map.81 = (bf16[3,128,4096]{2,1,0:T(8,128)(2,1)S(1)}, f32[12,32,128]{2,1,0:T(8,128)S(1)}) custom-call(s32[1]{0:T(128)} %bitcast.ids_ref, bf16[17,64,128]{2,1,0:T(8,128)(2,1)S(1)} %get-tuple-element.33.own_ref, f32[12,8,128]{2,1,0:T(8,128)S(1)} %constant_dynamic-update-slice_fusion.rest_0_, f32[12,8,128]{2,1,0:T(8,128)S(1)} %collective-permute-done.13.rest_1_, ...), custom_call_target="tpu_custom_call" | custom-call | flops 1000000 | bytes 10000 | tf_op jit(solution)/shard_map/pallas_call | solution.py:463
  38.9 1.2 %shard_map.79 = (bf16[17,64,128]{2,1,0:T(8,128)(2,1)S(1)}, bf16[17,64,128]{2,1,0:T(8,128)(2,1)S(1)}) custom-call(bf16[5,64,128]{2,1,0:T(8,128)(2,1)S(1)} %collective-permute-done.7.low_ref, bf16[5,64,128]{2,1,0:T(8,128)(2,1)S(1)} %collective-permute-done.8.up_ref), custom_call_target="tpu_custom_call" | custom-call | flops 1000000 | bytes 10000 | tf_op jit(solution)/shard_map/pallas_call | solution.py:249
  40.1 0.3 shard_map.80
  40.4 6.2 %shard_map.82 = (bf16[3,256,4096]{2,1,0:T(8,128)(2,1)S(1)}, f32[128,256]{1,0:T(8,128)S(1)}) custom-call(s32[1]{0:T(128)} %bitcast.ids_ref, bf16[17,64,128]{2,1,0:T(8,128)(2,1)S(1)} %get-tuple-element.41.refs_0_, bf16[17,64,128]{2,1,0:T(8,128)(2,1)S(1)} %get-tuple-element.42.refs_1_, bf16[17,64,128]{2,1,0:T(8,128)(2,1)S(1)} %get-tuple-element.43.refs_2_, ...), custom_call_target="tpu_custom_call" | custom-call | flops 1000000 | bytes 10000 | tf_op jit(solution)/shard_map/pallas_call | solution.py:472
  46.7 9.9 %shard_map.83 = (f32[5,64,256]{2,1,0:T(8,128)}, f32[5,64,256]{2,1,0:T(8,128)}) custom-call(s32[1]{0:T(128)} %bitcast.ids_ref, s32[2,5,2]{2,1,0:T(8,128)S(1)} %copy.16.pairs_ref, f32[1,256]{1,0:T(1,128)S(1)} %bitcast.9, bf16[17,64,128]{2,1,0:T(8,128)(2,1)S(1)} %get-tuple-element.33.own_ref, bf16[17,64,128]{2,1,0:T(8,128)(2,1)S(1)} %get-tuple-element.38.low2_ref, ...), custom_call_target="tpu_custom_call" | custom-call | flops 1000000 | bytes 10000 | tf_op jit(solution)/shard_map/pallas_call | solution.py:482
  (26 shorter events, 0.1 us)
Async XLA Ops:
  0.6 15.3 %copy-start = (f32[4,8,128]{2,1,0:T(8,128)S(1)}, f32[4,8,128]{2,1,0:T(8,128)}, u32[]{:S(2)}) copy-start(f32[4,8,128]{2,1,0:T(8,128)} %param.7) | copy-start | bytes 49156
  0.6 34.2 %copy-start.1 = (s32[256]{0:T(256)S(1)}, s32[256]{0:T(256)}, u32[]{:S(2)}) copy-start(s32[256]{0:T(256)} %param.10) | copy-start | bytes 3076
  0.7 34.2 %copy-start.2 = (s32[2,5,2]{1,2,0:T(2,128)S(1)}, s32[2,5,2]{1,2,0:T(2,128)}, u32[]{:S(2)}) copy-start(s32[2,5,2]{1,2,0:T(2,128)} %param.11) | copy-start | bytes 244
  0.7 13.5 %collective-permute-start = (f32[4,8,128]{2,1,0:T(8,128)}, f32[4,8,128]{2,1,0:T(8,128)S(1)}, u32[]{:S(2)}, u32[]{:S(2)}) collective-permute-start(f32[4,8,128]{2,1,0:T(8,128)} %param.7), channel_id=1, source_target_pairs={{28,0},{0,4},{4,8},{8,12},{12,16},{16,20},{20,24},{24,28},{29,1},{... | collective-permute-start | bytes 49160 | tf_op jit(solution)/shard_map/ppermute | solution.py:499
  3.7 10.5 %collective-permute-start.1 = (f32[4,8,128]{2,1,0:T(8,128)}, f32[4,8,128]{2,1,0:T(8,128)S(1)}, u32[]{:S(2)}, u32[]{:S(2)}) collective-permute-start(f32[4,8,128]{2,1,0:T(8,128)} %param.7), channel_id=1, source_target_pairs={{4,0},{8,4},{12,8},{16,12},{20,16},{24,20},{28,24},{0,28},{5,1},{9... | collective-permute-start | bytes 49160 | tf_op jit(solution)/shard_map/ppermute | solution.py:499
  14.2 8.9 %collective-permute-start.3 = (bf16[8,128,128]{2,1,0:T(8,128)(2,1)S(1)}, bf16[8,128,128]{2,1,0:T(8,128)(2,1)S(1)}, u32[]{:S(2)}, u32[]{:S(2)}) collective-permute-start(bf16[8,128,128]{2,1,0:T(8,128)(2,1)S(1)} %get-tuple-element.29.refs_4_), channel_id=1, source_target_pairs={{0,2},{1,3},{2,0},{3,1},{4,6},{5,7},{6,4},{7,5},{8,10},{9,11},{10,... | collective-permute-start | bytes 786440 | tf_op jit(solution)/shard_map/ppermute | solution.py:494
  15.9 7.2 %collective-permute-start.4 = (f32[12,8,128]{2,1,0:T(8,128)S(1)}, f32[12,8,128]{2,1,0:T(8,128)S(1)}, u32[]{:S(2)}, u32[]{:S(2)}) collective-permute-start(f32[12,8,128]{2,1,0:T(8,128)S(1)} %constant_dynamic-update-slice_fusion.rest_0_), channel_id=1, source_target_pairs={{0,2},{1,3},{2,0},{3,1},{4,6},{5,7},{6,4},{7,5},{8,10},{9,11},{10,... | collective-permute-start | bytes 147464 | tf_op jit(solution)/shard_map/ppermute | solution.py:494
  16.4 8.4 %collective-permute-start.2 = (bf16[8,128,128]{2,1,0:T(8,128)(2,1)S(1)}, bf16[8,128,128]{2,1,0:T(8,128)(2,1)S(1)}, u32[]{:S(2)}, u32[]{:S(2)}) collective-permute-start(bf16[8,128,128]{2,1,0:T(8,128)(2,1)S(1)} %get-tuple-element.28.refs_0_), channel_id=1, source_target_pairs={{0,1},{1,0},{2,3},{3,2},{4,5},{5,4},{6,7},{7,6},{8,9},{9,8},{10,11... | collective-permute-start | bytes 786440 | tf_op jit(solution)/shard_map/ppermute | solution.py:494
  23.1 1.6 %collective-permute-start.5 = (bf16[8,128,128]{2,1,0:T(8,128)(2,1)S(1)}, bf16[8,128,128]{2,1,0:T(8,128)(2,1)S(1)}, u32[]{:S(2)}, u32[]{:S(2)}) collective-permute-start(bf16[8,128,128]{2,1,0:T(8,128)(2,1)S(1)} %collective-permute-done.3.refs_2_), channel_id=1, source_target_pairs={{0,1},{1,0},{2,3},{3,2},{4,5},{5,4},{6,7},{7,6},{8,9},{9,8},{10,11... | collective-permute-start | bytes 786440 | tf_op jit(solution)/shard_map/ppermute | solution.py:494
  23.1 8.7 %collective-permute-start.6 = (bf16[8,128,128]{2,1,0:T(8,128)(2,1)S(1)}, bf16[8,128,128]{2,1,0:T(8,128)(2,1)S(1)}, u32[]{:S(2)}, u32[]{:S(2)}) collective-permute-start(bf16[8,128,128]{2,1,0:T(8,128)(2,1)S(1)} %get-tuple-element.28.refs_0_), channel_id=1, source_target_pairs={{0,2},{1,3},{2,0},{3,1},{4,6},{5,7},{6,4},{7,5},{8,10},{9,11},{10,... | collective-permute-start | bytes 786440 | tf_op jit(solution)/shard_map/ppermute | solution.py:494
  25.9 7.2 %collective-permute-start.7 = (bf16[5,64,128]{2,1,0:T(8,128)(2,1)S(1)}, bf16[5,64,128]{2,1,0:T(8,128)(2,1)S(1)}, u32[]{:S(2)}, u32[]{:S(2)}) collective-permute-start(bf16[5,64,128]{2,1,0:T(8,128)(2,1)S(1)} %get-tuple-element.34), channel_id=1, source_target_pairs={{24,0},{28,4},{0,8},{4,12},{8,16},{12,20},{16,24},{20,28},{25,1},{... | collective-permute-start | bytes 245768 | tf_op jit(solution)/shard_map/ppermute | solution.py:499
  25.9 7.1 %collective-permute-start.8 = (bf16[5,64,128]{2,1,0:T(8,128)(2,1)S(1)}, bf16[5,64,128]{2,1,0:T(8,128)(2,1)S(1)}, u32[]{:S(2)}, u32[]{:S(2)}) collective-permute-start(bf16[5,64,128]{2,1,0:T(8,128)(2,1)S(1)} %get-tuple-element.35), channel_id=1, source_target_pairs={{8,0},{12,4},{16,8},{20,12},{24,16},{28,20},{0,24},{4,28},{9,1},{1... | collective-permute-start | bytes 245768 | tf_op jit(solution)/shard_map/ppermute | solution.py:499
  29.8 16.9 %collective-permute-start.10 = (bf16[17,64,128]{2,1,0:T(8,128)(2,1)S(1)}, bf16[17,64,128]{2,1,0:T(8,128)(2,1)S(1)}, u32[]{:S(2)}, u32[]{:S(2)}) collective-permute-start(bf16[17,64,128]{2,1,0:T(8,128)(2,1)S(1)} %get-tuple-element.33.own_ref), channel_id=1, source_target_pairs={{4,0},{8,4},{12,8},{16,12},{20,16},{24,20},{28,24},{0,28},{5,1},{9... | collective-permute-start | bytes 835592 | tf_op jit(solution)/shard_map/ppermute | solution.py:499
  29.8 16.9 %collective-permute-start.9 = (bf16[17,64,128]{2,1,0:T(8,128)(2,1)S(1)}, bf16[17,64,128]{2,1,0:T(8,128)(2,1)S(1)}, u32[]{:S(2)}, u32[]{:S(2)}) collective-permute-start(bf16[17,64,128]{2,1,0:T(8,128)(2,1)S(1)} %get-tuple-element.33.own_ref), channel_id=1, source_target_pairs={{28,0},{0,4},{4,8},{8,12},{12,16},{16,20},{20,24},{24,28},{29,1},{... | collective-permute-start | bytes 835592 | tf_op jit(solution)/shard_map/ppermute | solution.py:499
  31.9 8.3 %collective-permute-start.11 = (bf16[8,128,128]{2,1,0:T(8,128)(2,1)S(1)}, bf16[8,128,128]{2,1,0:T(8,128)(2,1)S(1)}, u32[]{:S(2)}, u32[]{:S(2)}) collective-permute-start(bf16[8,128,128]{2,1,0:T(8,128)(2,1)S(1)} %get-tuple-element.29.refs_4_), channel_id=1, source_target_pairs={{0,1},{1,0},{2,3},{3,2},{4,5},{5,4},{6,7},{7,6},{8,9},{9,8},{10,11... | collective-permute-start | bytes 786440 | tf_op jit(solution)/shard_map/ppermute | solution.py:494
  33.1 7.1 %collective-permute-start.12 = (bf16[8,128,128]{2,1,0:T(8,128)(2,1)S(1)}, bf16[8,128,128]{2,1,0:T(8,128)(2,1)S(1)}, u32[]{:S(2)}, u32[]{:S(2)}) collective-permute-start(bf16[8,128,128]{2,1,0:T(8,128)(2,1)S(1)} %collective-permute-done.6.refs_6_), channel_id=1, source_target_pairs={{0,1},{1,0},{2,3},{3,2},{4,5},{5,4},{6,7},{7,6},{8,9},{9,8},{10,11... | collective-permute-start | bytes 786440 | tf_op jit(solution)/shard_map/ppermute | solution.py:494
  33.1 1.6 %collective-permute-start.13 = (f32[12,8,128]{2,1,0:T(8,128)S(1)}, f32[12,8,128]{2,1,0:T(8,128)S(1)}, u32[]{:S(2)}, u32[]{:S(2)}) collective-permute-start(f32[12,8,128]{2,1,0:T(8,128)S(1)} %constant_dynamic-update-slice_fusion.rest_0_), channel_id=1, source_target_pairs={{0,1},{1,0},{2,3},{3,2},{4,5},{5,4},{6,7},{7,6},{8,9},{9,8},{10,11... | collective-permute-start | bytes 147464 | tf_op jit(solution)/shard_map/ppermute | solution.py:494
  34.7 1.2 %collective-permute-start.14 = (f32[12,8,128]{2,1,0:T(8,128)S(1)}, f32[12,8,128]{2,1,0:T(8,128)S(1)}, u32[]{:S(2)}, u32[]{:S(2)}) collective-permute-start(f32[12,8,128]{2,1,0:T(8,128)S(1)} %collective-permute-done.4.rest_2_), channel_id=1, source_target_pairs={{0,1},{1,0},{2,3},{3,2},{4,5},{5,4},{6,7},{7,6},{8,9},{9,8},{10,11... | collective-permute-start | bytes 147464 | tf_op jit(solution)/shard_map/ppermute | solution.py:494

commit v4 on v3

--- a/solution.py
+++ b/solution.py
@@ -27,9 +27,8 @@
     return jnp.bitwise_xor(m // 2, 1 - own)
 
 
-def pack_kernel(ids_ref, centre_in, x_ref, *rest, patch, rows, total_rows):
-    *o_refs, landed, arrived, limits, scr, centre_ref, told = rest
-    _, half, cells = o_refs[0].shape
+def pack_kernel(ids_ref, centre_in, x_ref, o_ref, landed, arrived, limits, scr, centre_ref, told, *, own, patch, rows, total_rows):
+    _, half, cells = o_ref.shape
     steps, count = landed.shape[:2]
     window = 3 * patch
     pairs = window // 2
@@ -37,7 +36,7 @@
     m = ids_ref[0]
 
     def start_of(step):
-        return pl.multiple_of(half_of(m, step * count // half) * half + step * count % half, count)
+        return pl.multiple_of(half_of(m, own) * half + step * count, count)
 
     copies = []
     for step in range(steps):
@@ -84,20 +83,19 @@
 
         lax.fori_loop(0, count // P_STEP, body, 0, unroll=P_UNROLL)
         for r in range(rows):
-            at = step * count % half
-            o_refs[step * count // half][r, at : at + count, :] = scr[:, r, :].astype(BF)
-
-
-def pack(ids, centres, orbitals, parts, patch):
+            o_ref[r, step * count : (step + 1) * count, :] = scr[:, r, :].astype(BF)
+
+
+def pack(ids, centres, orbitals, parts, patch, own):
     orbs, window, rows, cells = orbitals.shape
-    steps = 8
-    count = orbs // steps
+    half, steps = orbs // 2, 4
+    count = half // steps
     sm = pl.BlockSpec(memory_space=pltpu.SMEM)
     return pl.pallas_call(
-        functools.partial(pack_kernel, patch=patch, rows=rows, total_rows=rows * parts),
+        functools.partial(pack_kernel, own=own, patch=patch, rows=rows, total_rows=rows * parts),
         in_specs=[sm] + [pl.BlockSpec(memory_space=pl.ANY)] * 2,
-        out_specs=[pl.BlockSpec(memory_space=pltpu.VMEM)] * 2,
-        out_shape=[jax.ShapeDtypeStruct((rows, orbs // 2, cells), BF)] * 2,
+        out_specs=pl.BlockSpec(memory_space=pltpu.VMEM),
+        out_shape=jax.ShapeDtypeStruct((rows, half, cells), BF),
         scratch_shapes=[
             pltpu.VMEM((steps, count, window * rows, cells), BF),
             pltpu.SemaphoreType.DMA((steps,)),
@@ -107,7 +105,7 @@
             pltpu.SemaphoreType.DMA((1,)),
         ],
         compiler_params=pltpu.CompilerParams(vmem_limit_bytes=53 * 2**20),
-        cost_estimate=pl.CostEstimate(flops=orbitals.size * 256, bytes_accessed=orbitals.size * 2, transcendentals=0),
+        cost_estimate=pl.CostEstimate(flops=orbitals.size * 256, bytes_accessed=orbitals.size, transcendentals=0),
     )(ids, centres, orbitals.reshape(orbs, window * rows, cells))
 
 
@@ -506,21 +504,25 @@
     ids = lax.axis_index("mat")[None]
 
     centres = jnp.stack([centre_first, centre_second, centre_third])
-    away, home = pack(ids, centres, orbitals, parts, patch)
+    away = pack(ids, centres, orbitals, parts, patch, 0)
     before, after = along(potential, 1), along(potential, -1)
-    away, home, before, after = lax.optimization_barrier((away, home, before, after))
-    far_home, far_away = hop(away, 2), hop(home, 2)
+    away, before, after = lax.optimization_barrier((away, before, after))
+    far_home = hop(away, 2)
+    home = pack(ids, centres, orbitals, parts, patch, 1)
+    far_away = hop(home, 2)
     near_home, near_away = hop(home, 1), hop(away, 1)
     field = jnp.concatenate([before, potential, after], axis=0)
-    far_field = hop(field, 2)
-    far_home, far_field = lax.optimization_barrier((far_home, far_field))
+    far_field, near_field = hop(field, 2), hop(field, 1)
+    far_home, far_field, near_field, home = lax.optimization_barrier((far_home, far_field, near_field, home))
+    diag_home, diag_field = hop(far_home, 1), hop(far_field, 1)
+    diag_home, diag_field = lax.optimization_barrier((diag_home, diag_field))
+    fields = (field, near_field, far_field, diag_field)
     centres = centres.T.astype(F32)
     share = orbs // parts
-    homes = (home, near_home, far_home, hop(far_home, 1))
+    homes = (home, near_home, far_home, diag_home)
     merged, low2, up2 = merge_rows(ids, centres, share, patch, True, homes)
     low2, low1, up1, up2 = along(low2, 2), along(merged, 1), along(merged, -1), along(up2, -2)
     far_away, low2, up2 = lax.optimization_barrier((far_away, low2, up2))
-    fields = (field, hop(field, 1), far_field, hop(far_field, 1))
     every = merge_rows(ids, centres, share, patch, False, homes, (away, near_away, far_away, hop(far_away, 1)))
     low2, up2 = loosen(low2, up2, patch, rows * parts)
     others = (low2, low1, up1, up2)

time: 56.7 us -> 53.6 us (0.945)
  waiting for transfers between devices: 10.1 us -> 5.02 us
  Pallas kernels: 28.4 us -> 29.5 us
  starting transfers between devices: 16.3 us -> 17.1 us
    ppermute x9, waiting for transfers between devices: 8.88 us -> 3.9 us  [hop(): lax.ppermute(x, 'mat', [(i, i ^ k) for i in range(lax.axis_size('mat'))])]
    pallas_call x1 -> x2, Pallas kernels: 6.69 us -> 7.85 us  [pack(): pl.pallas_call(functools.partial(pack_kernel, own=own, patch=patch, rows=...]
    ppermute x6, starting transfers between devices: 12 us -> 12.9 us  [along(): lax.ppermute(x, 'dom', [((i - distance) % size, i) for i in range(size)])]
  transfers between devices with their start and end apart: 15 -> 15, of which waited for: 5 -> 3; matrix products, arithmetic and copies ran while one was open for 2% -> 2% of each run, Pallas kernels for 33% -> 37%
where the time goes in v4:
time: 53.6 us; the launch traced here: 53.4 us
  Pallas kernels  29.5 us (55%)
  starting transfers between devices  17.1 us (32%)
  waiting for transfers between devices  5.02 us (9%)
  between operations  0.8 us (1%)
  other arithmetic  0.72 us (1%)
    ppermute x6, starting transfers between devices, along(): lax.ppermute(x, 'dom', [((i - distance) % size, i) for i in range(size)])  12.9 us
    pallas_call x1, Pallas kernels, products(): pl.pallas_call(functools.partial(others_kernel, **sizes), in_specs=[sm, s...  9.9 us
    pallas_call x2, Pallas kernels, pack(): pl.pallas_call(functools.partial(pack_kernel, own=own, patch=patch, rows=...  7.85 us
    pallas_call x1, Pallas kernels, products(): pl.pallas_call(functools.partial(rows_kernel, **sizes, parts=len(rows)),...  6.24 us
    ppermute x9, starting transfers between devices, hop(): lax.ppermute(x, 'mat', [(i, i ^ k) for i in range(lax.axis_size('mat'))])  4.16 us
    ppermute x9, waiting for transfers between devices, hop(): lax.ppermute(x, 'mat', [(i, i ^ k) for i in range(lax.axis_size('mat'))])  3.9 us
    pallas_call x1, Pallas kernels, products(): pl.pallas_call(functools.partial(own_kernel, **sizes, parts=len(rows)), i...  3.03 us
    pallas_call x2, Pallas kernels, merge_rows(): pl.pallas_call(functools.partial(merge_kernel, chips=len(packs), own_only...  1.35 us
  transfers between devices with their start and end apart: 15, of which 3 were waited for; matrix products, arithmetic and copies ran while one was open for 2% of the time, Pallas kernels for 37%

profile of v4, /device:TPU:0, one launch (start us, length us, event | category | flops | bytes accessed | tf_op | source)
XLA Modules:
  0.0 53.4 jit_solution(16492017652557276246)
XLA Ops:
  0.6 3.0 %collective-permute-start = (f32[4,8,128]{2,1,0:T(8,128)}, f32[4,8,128]{2,1,0:T(8,128)S(1)}, u32[]{:S(2)}, u32[]{:S(2)}) collective-permute-start(f32[4,8,128]{2,1,0:T(8,128)} %param.7), channel_id=1, source_target_pairs={{28,0},{0,4},{4,8},{8,12},{12,16},{16,20},{20,24},{24,28},{29,1},{... | collective-permute-start | bytes 49160 | tf_op jit(solution)/shard_map/ppermute | solution.py:497
  3.7 3.1 %collective-permute-start.1 = (f32[4,8,128]{2,1,0:T(8,128)}, f32[4,8,128]{2,1,0:T(8,128)S(1)}, u32[]{:S(2)}, u32[]{:S(2)}) collective-permute-start(f32[4,8,128]{2,1,0:T(8,128)} %param.7), channel_id=1, source_target_pairs={{4,0},{8,4},{12,8},{16,12},{20,16},{24,20},{28,24},{0,28},{5,1},{9... | collective-permute-start | bytes 49160 | tf_op jit(solution)/shard_map/ppermute | solution.py:497
  6.8 0.7 %pad_add_fusion = (s32[3,256]{1,0:T(4,128)S(1)}, f32[3,256]{1,0:T(4,128)S(1)}) fusion(s32[1,256]{1,0:T(1,128)} %bitcast.12, s32[1,256]{1,0:T(1,128)} %bitcast.13, s32[1,256]{1,0:T(1,128)} %bitcast.14), kind=kLoop, calls=%fused_computation.3 | loop fusion | flops 2304 | bytes 9216 | tf_op jit(solution)/shard_map/stack | solution.py:506
  7.5 3.9 %shard_map.77.refs_4_ = bf16[8,128,128]{2,1,0:T(8,128)(2,1)S(1)} custom-call(s32[1]{0:T(128)} %bitcast.ids_ref, s32[3,256]{1,0:T(4,128)S(1)} %get-tuple-element.52.centre_in, bf16[256,96,128]{2,1,0:T(8,128)(2,1)} %bitcast.10), custom_call_target="tpu_custom_call" | custom-call | flops 805306368 | bytes 3145728 | tf_op jit(solution)/shard_map/pallas_call | solution.py:94
  11.5 1.7 %collective-permute-start.2 = (bf16[8,128,128]{2,1,0:T(8,128)(2,1)S(1)}, bf16[8,128,128]{2,1,0:T(8,128)(2,1)S(1)}, u32[]{:S(2)}, u32[]{:S(2)}) collective-permute-start(bf16[8,128,128]{2,1,0:T(8,128)(2,1)S(1)} %shard_map.77.refs_4_), channel_id=1, source_target_pairs={{0,2},{1,3},{2,0},{3,1},{4,6},{5,7},{6,4},{7,5},{8,10},{9,11},{10,... | collective-permute-start | bytes 786440 | tf_op jit(solution)/shard_map/ppermute | solution.py:492
  13.1 0.5 collective-permute-start.3
  13.6 3.9 %shard_map.78.refs_0_ = bf16[8,128,128]{2,1,0:T(8,128)(2,1)S(1)} custom-call(s32[1]{0:T(128)} %bitcast.ids_ref, s32[3,256]{1,0:T(4,128)S(1)} %get-tuple-element.52.centre_in, bf16[256,96,128]{2,1,0:T(8,128)(2,1)} %bitcast.11), custom_call_target="tpu_custom_call" | custom-call | flops 805306368 | bytes 3145728 | tf_op jit(solution)/shard_map/pallas_call | solution.py:94
  17.6 2.8 %collective-permute-done.3.rest_2_ = f32[12,8,128]{2,1,0:T(8,128)S(1)} collective-permute-done((f32[12,8,128]{2,1,0:T(8,128)S(1)}, f32[12,8,128]{2,1,0:T(8,128)S(1)}, u32[]{:S(2)}, u32[]{:S(2)}) %collective-permute-start.3) | collective-permute-done | bytes 49184 | tf_op jit(solution)/shard_map/ppermute | solution.py:492
  20.4 0.5 collective-permute-start.5
  20.9 1.5 %collective-permute-start.8 = (bf16[8,128,128]{2,1,0:T(8,128)(2,1)S(1)}, bf16[8,128,128]{2,1,0:T(8,128)(2,1)S(1)}, u32[]{:S(2)}, u32[]{:S(2)}) collective-permute-start(bf16[8,128,128]{2,1,0:T(8,128)(2,1)S(1)} %shard_map.78.refs_0_), channel_id=1, source_target_pairs={{0,2},{1,3},{2,0},{3,1},{4,6},{5,7},{6,4},{7,5},{8,10},{9,11},{10,... | collective-permute-start | bytes 786440 | tf_op jit(solution)/shard_map/ppermute | solution.py:492
  22.4 0.1 copy.17
  22.5 1.1 %collective-permute-done.7.rest_3_ = f32[12,8,128]{2,1,0:T(8,128)S(1)} collective-permute-done((f32[12,8,128]{2,1,0:T(8,128)S(1)}, f32[12,8,128]{2,1,0:T(8,128)S(1)}, u32[]{:S(2)}, u32[]{:S(2)}) %collective-permute-start.7) | collective-permute-done | bytes 49184 | tf_op jit(solution)/shard_map/ppermute | solution.py:492
  23.6 1.1 %shard_map.79 = (bf16[17,64,128]{2,1,0:T(8,128)(2,1)S(1)}, bf16[5,64,128]{2,1,0:T(8,128)(2,1)S(1)}, bf16[5,64,128]{2,1,0:T(8,128)(2,1)S(1)}) custom-call(s32[1]{0:T(128)} %bitcast.ids_ref, f32[256,3]{1,0:T(8,128)S(1)} %bitcast.7, bf16[8,128,128]{2,1,0:T(8,128)(2,1)S(1)} %shard_map.78.refs_0_, bf16[8,128,128]{2,1,0:T(8,128)(2,1)S(1)} %collective-permute-done.5.refs_1_, ...), custom_call_target="tpu_custom_call" | custom-call | tf_op jit(solution)/shard_map/pallas_call | solution.py:141
  24.7 1.7 %collective-permute-start.10 = (bf16[5,64,128]{2,1,0:T(8,128)(2,1)S(1)}, bf16[5,64,128]{2,1,0:T(8,128)(2,1)S(1)}, u32[]{:S(2)}, u32[]{:S(2)}) collective-permute-start(bf16[5,64,128]{2,1,0:T(8,128)(2,1)S(1)} %get-tuple-element.36), channel_id=1, source_target_pairs={{8,0},{12,4},{16,8},{20,12},{24,16},{28,20},{0,24},{4,28},{9,1},{1... | collective-permute-start | bytes 245768 | tf_op jit(solution)/shard_map/ppermute | solution.py:497
  26.4 0.4 collective-permute-start.9
  26.8 0.2 collective-permute-start.11
  27.0 4.5 %collective-permute-start.12 = (bf16[17,64,128]{2,1,0:T(8,128)(2,1)S(1)}, bf16[17,64,128]{2,1,0:T(8,128)(2,1)S(1)}, u32[]{:S(2)}, u32[]{:S(2)}) collective-permute-start(bf16[17,64,128]{2,1,0:T(8,128)(2,1)S(1)} %get-tuple-element.34.own_ref), channel_id=1, source_target_pairs={{4,0},{8,4},{12,8},{16,12},{20,16},{24,20},{28,24},{0,28},{5,1},{9... | collective-permute-start | bytes 835592 | tf_op jit(solution)/shard_map/ppermute | solution.py:497
  31.5 1.1 %collective-permute-done.9.low_ref = bf16[5,64,128]{2,1,0:T(8,128)(2,1)S(1)} collective-permute-done((bf16[5,64,128]{2,1,0:T(8,128)(2,1)S(1)}, bf16[5,64,128]{2,1,0:T(8,128)(2,1)S(1)}, u32[]{:S(2)}, u32[]{:S(2)}) %collective-permute-start.9) | collective-permute-done | bytes 81952 | tf_op jit(solution)/shard_map/ppermute | solution.py:497
  32.6 0.1 copy.18.pairs_ref
  32.7 3.0 %shard_map.82 = (bf16[3,128,4096]{2,1,0:T(8,128)(2,1)S(1)}, f32[12,32,128]{2,1,0:T(8,128)S(1)}) custom-call(s32[1]{0:T(128)} %bitcast.ids_ref, bf16[17,64,128]{2,1,0:T(8,128)(2,1)S(1)} %get-tuple-element.34.own_ref, f32[12,8,128]{2,1,0:T(8,128)S(1)} %constant_dynamic-update-slice_fusion.rest_0_, f32[12,8,128]{2,1,0:T(8,128)S(1)} %collective-permute-done.4.rest_1_, ...), custom_call_target="tpu_custom_call" | custom-call | flops 1000000 | bytes 10000 | tf_op jit(solution)/shard_map/pallas_call | solution.py:461
  35.8 1.2 %shard_map.80 = (bf16[17,64,128]{2,1,0:T(8,128)(2,1)S(1)}, bf16[17,64,128]{2,1,0:T(8,128)(2,1)S(1)}) custom-call(bf16[5,64,128]{2,1,0:T(8,128)(2,1)S(1)} %collective-permute-done.9.low_ref, bf16[5,64,128]{2,1,0:T(8,128)(2,1)S(1)} %collective-permute-done.10.up_ref), custom_call_target="tpu_custom_call" | custom-call | flops 1000000 | bytes 10000 | tf_op jit(solution)/shard_map/pallas_call | solution.py:247
  37.0 0.3 shard_map.81
  37.2 6.2 %shard_map.83 = (bf16[3,256,4096]{2,1,0:T(8,128)(2,1)S(1)}, f32[128,256]{1,0:T(8,128)S(1)}) custom-call(s32[1]{0:T(128)} %bitcast.ids_ref, bf16[17,64,128]{2,1,0:T(8,128)(2,1)S(1)} %get-tuple-element.42.refs_0_, bf16[17,64,128]{2,1,0:T(8,128)(2,1)S(1)} %get-tuple-element.43.refs_1_, bf16[17,64,128]{2,1,0:T(8,128)(2,1)S(1)} %get-tuple-element.44.refs_2_, ...), custom_call_target="tpu_custom_call" | custom-call | flops 1000000 | bytes 10000 | tf_op jit(solution)/shard_map/pallas_call | solution.py:470
  43.5 9.9 %shard_map.84 = (f32[5,64,256]{2,1,0:T(8,128)}, f32[5,64,256]{2,1,0:T(8,128)}) custom-call(s32[1]{0:T(128)} %bitcast.ids_ref, s32[2,5,2]{2,1,0:T(8,128)S(1)} %copy.18.pairs_ref, f32[1,256]{1,0:T(1,128)S(1)} %bitcast.9, bf16[17,64,128]{2,1,0:T(8,128)(2,1)S(1)} %get-tuple-element.34.own_ref, bf16[17,64,128]{2,1,0:T(8,128)(2,1)S(1)} %get-tuple-element.39.low2_ref, ...), custom_call_target="tpu_custom_call" | custom-call | flops 1000000 | bytes 10000 | tf_op jit(solution)/shard_map/pallas_call | solution.py:480
  (27 shorter events, 0.1 us)
Async XLA Ops:
  0.6 12.5 %copy-start = (f32[4,8,128]{2,1,0:T(8,128)S(1)}, f32[4,8,128]{2,1,0:T(8,128)}, u32[]{:S(2)}) copy-start(f32[4,8,128]{2,1,0:T(8,128)} %param.7) | copy-start | bytes 49156
  0.6 10.8 %collective-permute-start = (f32[4,8,128]{2,1,0:T(8,128)}, f32[4,8,128]{2,1,0:T(8,128)S(1)}, u32[]{:S(2)}, u32[]{:S(2)}) collective-permute-start(f32[4,8,128]{2,1,0:T(8,128)} %param.7), channel_id=1, source_target_pairs={{28,0},{0,4},{4,8},{8,12},{12,16},{16,20},{20,24},{24,28},{29,1},{... | collective-permute-start | bytes 49160 | tf_op jit(solution)/shard_map/ppermute | solution.py:497
  3.7 7.8 %collective-permute-start.1 = (f32[4,8,128]{2,1,0:T(8,128)}, f32[4,8,128]{2,1,0:T(8,128)S(1)}, u32[]{:S(2)}, u32[]{:S(2)}) collective-permute-start(f32[4,8,128]{2,1,0:T(8,128)} %param.7), channel_id=1, source_target_pairs={{4,0},{8,4},{12,8},{16,12},{20,16},{24,20},{28,24},{0,28},{5,1},{9... | collective-permute-start | bytes 49160 | tf_op jit(solution)/shard_map/ppermute | solution.py:497
  7.5 25.1 %copy-start.1 = (s32[256]{0:T(256)S(1)}, s32[256]{0:T(256)}, u32[]{:S(2)}) copy-start(s32[256]{0:T(256)} %param.10) | copy-start | bytes 3076
  7.5 25.1 %copy-start.2 = (s32[2,5,2]{1,2,0:T(2,128)S(1)}, s32[2,5,2]{1,2,0:T(2,128)}, u32[]{:S(2)}) copy-start(s32[2,5,2]{1,2,0:T(2,128)} %param.11) | copy-start | bytes 244
  11.5 8.9 %collective-permute-start.2 = (bf16[8,128,128]{2,1,0:T(8,128)(2,1)S(1)}, bf16[8,128,128]{2,1,0:T(8,128)(2,1)S(1)}, u32[]{:S(2)}, u32[]{:S(2)}) collective-permute-start(bf16[8,128,128]{2,1,0:T(8,128)(2,1)S(1)} %shard_map.77.refs_4_), channel_id=1, source_target_pairs={{0,2},{1,3},{2,0},{3,1},{4,6},{5,7},{6,4},{7,5},{8,10},{9,11},{10,... | collective-permute-start | bytes 786440 | tf_op jit(solution)/shard_map/ppermute | solution.py:492
  13.1 7.2 %collective-permute-start.3 = (f32[12,8,128]{2,1,0:T(8,128)S(1)}, f32[12,8,128]{2,1,0:T(8,128)S(1)}, u32[]{:S(2)}, u32[]{:S(2)}) collective-permute-start(f32[12,8,128]{2,1,0:T(8,128)S(1)} %constant_dynamic-update-slice_fusion.rest_0_), channel_id=1, source_target_pairs={{0,2},{1,3},{2,0},{3,1},{4,6},{5,7},{6,4},{7,5},{8,10},{9,11},{10,... | collective-permute-start | bytes 147464 | tf_op jit(solution)/shard_map/ppermute | solution.py:492
  13.6 6.7 %collective-permute-start.4 = (f32[12,8,128]{2,1,0:T(8,128)S(1)}, f32[12,8,128]{2,1,0:T(8,128)S(1)}, u32[]{:S(2)}, u32[]{:S(2)}) collective-permute-start(f32[12,8,128]{2,1,0:T(8,128)S(1)} %constant_dynamic-update-slice_fusion.rest_0_), channel_id=1, source_target_pairs={{0,1},{1,0},{2,3},{3,2},{4,5},{5,4},{6,7},{7,6},{8,9},{9,8},{10,11... | collective-permute-start | bytes 147464 | tf_op jit(solution)/shard_map/ppermute | solution.py:492
  20.4 3.2 %collective-permute-start.6 = (bf16[8,128,128]{2,1,0:T(8,128)(2,1)S(1)}, bf16[8,128,128]{2,1,0:T(8,128)(2,1)S(1)}, u32[]{:S(2)}, u32[]{:S(2)}) collective-permute-start(bf16[8,128,128]{2,1,0:T(8,128)(2,1)S(1)} %collective-permute-done.2.refs_2_), channel_id=1, source_target_pairs={{0,1},{1,0},{2,3},{3,2},{4,5},{5,4},{6,7},{7,6},{8,9},{9,8},{10,11... | collective-permute-start | bytes 786440 | tf_op jit(solution)/shard_map/ppermute | solution.py:492
  20.4 3.2 %collective-permute-start.5 = (bf16[8,128,128]{2,1,0:T(8,128)(2,1)S(1)}, bf16[8,128,128]{2,1,0:T(8,128)(2,1)S(1)}, u32[]{:S(2)}, u32[]{:S(2)}) collective-permute-start(bf16[8,128,128]{2,1,0:T(8,128)(2,1)S(1)} %shard_map.78.refs_0_), channel_id=1, source_target_pairs={{0,1},{1,0},{2,3},{3,2},{4,5},{5,4},{6,7},{7,6},{8,9},{9,8},{10,11... | collective-permute-start | bytes 786440 | tf_op jit(solution)/shard_map/ppermute | solution.py:492
  20.9 10.6 %collective-permute-start.8 = (bf16[8,128,128]{2,1,0:T(8,128)(2,1)S(1)}, bf16[8,128,128]{2,1,0:T(8,128)(2,1)S(1)}, u32[]{:S(2)}, u32[]{:S(2)}) collective-permute-start(bf16[8,128,128]{2,1,0:T(8,128)(2,1)S(1)} %shard_map.78.refs_0_), channel_id=1, source_target_pairs={{0,2},{1,3},{2,0},{3,1},{4,6},{5,7},{6,4},{7,5},{8,10},{9,11},{10,... | collective-permute-start | bytes 786440 | tf_op jit(solution)/shard_map/ppermute | solution.py:492
  22.4 1.2 %collective-permute-start.7 = (f32[12,8,128]{2,1,0:T(8,128)S(1)}, f32[12,8,128]{2,1,0:T(8,128)S(1)}, u32[]{:S(2)}, u32[]{:S(2)}) collective-permute-start(f32[12,8,128]{2,1,0:T(8,128)S(1)} %collective-permute-done.3.rest_2_), channel_id=1, source_target_pairs={{0,1},{1,0},{2,3},{3,2},{4,5},{5,4},{6,7},{7,6},{8,9},{9,8},{10,11... | collective-permute-start | bytes 147464 | tf_op jit(solution)/shard_map/ppermute | solution.py:492
  24.7 6.8 %collective-permute-start.10 = (bf16[5,64,128]{2,1,0:T(8,128)(2,1)S(1)}, bf16[5,64,128]{2,1,0:T(8,128)(2,1)S(1)}, u32[]{:S(2)}, u32[]{:S(2)}) collective-permute-start(bf16[5,64,128]{2,1,0:T(8,128)(2,1)S(1)} %get-tuple-element.36), channel_id=1, source_target_pairs={{8,0},{12,4},{16,8},{20,12},{24,16},{28,20},{0,24},{4,28},{9,1},{1... | collective-permute-start | bytes 245768 | tf_op jit(solution)/shard_map/ppermute | solution.py:497
  26.4 6.2 %collective-permute-start.9 = (bf16[5,64,128]{2,1,0:T(8,128)(2,1)S(1)}, bf16[5,64,128]{2,1,0:T(8,128)(2,1)S(1)}, u32[]{:S(2)}, u32[]{:S(2)}) collective-permute-start(bf16[5,64,128]{2,1,0:T(8,128)(2,1)S(1)} %get-tuple-element.35), channel_id=1, source_target_pairs={{24,0},{28,4},{0,8},{4,12},{8,16},{12,20},{16,24},{20,28},{25,1},{... | collective-permute-start | bytes 245768 | tf_op jit(solution)/shard_map/ppermute | solution.py:497
  26.8 16.7 %collective-permute-start.11 = (bf16[17,64,128]{2,1,0:T(8,128)(2,1)S(1)}, bf16[17,64,128]{2,1,0:T(8,128)(2,1)S(1)}, u32[]{:S(2)}, u32[]{:S(2)}) collective-permute-start(bf16[17,64,128]{2,1,0:T(8,128)(2,1)S(1)} %get-tuple-element.34.own_ref), channel_id=1, source_target_pairs={{28,0},{0,4},{4,8},{8,12},{12,16},{16,20},{20,24},{24,28},{29,1},{... | collective-permute-start | bytes 835592 | tf_op jit(solution)/shard_map/ppermute | solution.py:497
  27.0 16.5 %collective-permute-start.12 = (bf16[17,64,128]{2,1,0:T(8,128)(2,1)S(1)}, bf16[17,64,128]{2,1,0:T(8,128)(2,1)S(1)}, u32[]{:S(2)}, u32[]{:S(2)}) collective-permute-start(bf16[17,64,128]{2,1,0:T(8,128)(2,1)S(1)} %get-tuple-element.34.own_ref), channel_id=1, source_target_pairs={{4,0},{8,4},{12,8},{16,12},{20,16},{24,20},{28,24},{0,28},{5,1},{9... | collective-permute-start | bytes 835592 | tf_op jit(solution)/shard_map/ppermute | solution.py:497
  31.5 5.4 %collective-permute-start.13 = (bf16[8,128,128]{2,1,0:T(8,128)(2,1)S(1)}, bf16[8,128,128]{2,1,0:T(8,128)(2,1)S(1)}, u32[]{:S(2)}, u32[]{:S(2)}) collective-permute-start(bf16[8,128,128]{2,1,0:T(8,128)(2,1)S(1)} %shard_map.77.refs_4_), channel_id=1, source_target_pairs={{0,1},{1,0},{2,3},{3,2},{4,5},{5,4},{6,7},{7,6},{8,9},{9,8},{10,11... | collective-permute-start | bytes 786440 | tf_op jit(solution)/shard_map/ppermute | solution.py:492
  32.6 4.3 %collective-permute-start.14 = (bf16[8,128,128]{2,1,0:T(8,128)(2,1)S(1)}, bf16[8,128,128]{2,1,0:T(8,128)(2,1)S(1)}, u32[]{:S(2)}, u32[]{:S(2)}) collective-permute-start(bf16[8,128,128]{2,1,0:T(8,128)(2,1)S(1)} %collective-permute-done.8.refs_6_), channel_id=1, source_target_pairs={{0,1},{1,0},{2,3},{3,2},{4,5},{5,4},{6,7},{7,6},{8,9},{9,8},{10,11... | collective-permute-start | bytes 786440 | tf_op jit(solution)/shard_map/ppermute | solution.py:492

commit v5 on v4

--- a/solution.py
+++ b/solution.py
@@ -371,7 +371,7 @@
 
 
 def rows_kernel(ids_ref, *refs, patch, total_rows, parts):
-    row_refs, (b_ref, a_ref, sum_ref, limit_ref, gap_ref) = refs[:parts], refs[parts:]
+    row_refs, (a_ref, limit_ref, gap_ref) = refs[:parts], refs[parts:]
     share, cells = row_refs[0].shape[1:]
     every = range(1, 3 * patch - 1)
     for n, ref in enumerate(row_refs):
@@ -385,14 +385,10 @@
             a_ref[q, pl.ds(pl.multiple_of(who + part.start, size), size), row_of(y, cells)] = value
 
         spread_rows(source, limit_ref, gap_ref, range(3), store_row)
-    total = product_of(b_ref[0], a_ref[0])
-    for q in range(1, 3):
-        total = total + product_of(b_ref[q], a_ref[q])
-    sum_ref[...] = total
 
 
 def others_kernel(
-    ids_ref, pairs_ref, row_third_ref, own_ref, low2_ref, low1_ref, up1_ref, up2_ref, a_ref, v_ref, sum_ref,
+    ids_ref, pairs_ref, row_third_ref, own_ref, low2_ref, low1_ref, up1_ref, up2_ref, a_ref, v_ref, own_b_ref,
     gram_ref, ham_ref,
     b_ref, limit_ref, gap_ref, group_ref,
     *, patch, total_rows,
@@ -418,13 +414,13 @@
         source = Source(ref, hop, patch, total_rows)
         columns(source, allowed, limit_ref, gap_ref, group_ref, v_ref, store_column)
 
-    sums = {0: sum_ref[...]}
+    sums = {}
     for q in range(3):
-        product = product_of(b_ref[q], a_ref[q])
-        for (hop, at_q), taken in spots.items():
-            if at_q == q:
-                piece = product[taken * both : (taken + 1) * both]
-                sums[hop] = piece if hop not in sums else sums[hop] + piece
+        product = product_of(jnp.concatenate([b_ref[q], own_b_ref[q]], axis=0), a_ref[q])
+        for hop in sorted({q - 2, q - 1, q}):
+            taken = spots.get((hop, q), 2)
+            piece = product[taken * both : (taken + 1) * both]
+            sums[hop] = piece if hop not in sums else sums[hop] + piece
 
     orbs = a_ref.shape[1]
     half_rows = orbs // pairs_ref.shape[0]
@@ -467,15 +463,15 @@
         compiler_params=params,
         cost_estimate=cost,
     )(ids, own, *fields)
-    a, own_sum = pl.pallas_call(
+    a = pl.pallas_call(
         functools.partial(rows_kernel, **sizes, parts=len(rows)),
-        in_specs=[sm] + [vm] * (len(rows) + 1),
-        out_specs=[vm] * 2,
-        out_shape=[jax.ShapeDtypeStruct((3, orbs, long), BF), jax.ShapeDtypeStruct((2 * share, orbs), F32)],
+        in_specs=[sm] + [vm] * len(rows),
+        out_specs=vm,
+        out_shape=jax.ShapeDtypeStruct((3, orbs, long), BF),
         scratch_shapes=[pltpu.VMEM((3, 2, share, cells), BF), pltpu.VMEM((2, slots, share, cells), BF)],
         compiler_params=params,
         cost_estimate=cost,
-    )(ids, *rows, b)
+    )(ids, *rows)
     out = jax.ShapeDtypeStruct((5, share, orbs), F32)
     return pl.pallas_call(
         functools.partial(others_kernel, **sizes),
@@ -485,7 +481,7 @@
         scratch_shapes=[pltpu.VMEM((3, 4 * share, long), BF)] + scratch(2),
         compiler_params=params,
         cost_estimate=cost,
-    )(ids, pairs, row_third, own, *others, a, v, own_sum)
+    )(ids, pairs, row_third, own, *others, a, v, b)
 
 
 def hop(x, k):

time: 53.6 us -> 52 us (0.970)
  Pallas kernels: 29.5 us -> 27.9 us
    pallas_call x1, Pallas kernels: 6.24 us -> 4.07 us  [products(): pl.pallas_call(functools.partial(rows_kernel, **sizes, parts=len(rows)),...]
    pallas_call x1, Pallas kernels: 9.9 us -> 10.5 us  [products(): pl.pallas_call(functools.partial(others_kernel, **sizes), in_specs=[sm, s...]
  transfers between devices with their start and end apart: 15 -> 15, of which waited for: 3 -> 3; matrix products, arithmetic and copies ran while one was open for 2% -> 2% of each run, Pallas kernels for 37% -> 34%
where the time goes in v5:
time: 52 us; the launch traced here: 51.8 us
  Pallas kernels  27.9 us (54%)
  starting transfers between devices  17.1 us (33%)
  waiting for transfers between devices  5.04 us (10%)
  between operations  0.8 us (2%)
  other arithmetic  0.72 us (1%)
    ppermute x6, starting transfers between devices, along(): lax.ppermute(x, 'dom', [((i - distance) % size, i) for i in range(size)])  12.9 us
    pallas_call x1, Pallas kernels, products(): pl.pallas_call(functools.partial(others_kernel, **sizes), in_specs=[sm, s...  10.5 us
    pallas_call x2, Pallas kernels, pack(): pl.pallas_call(functools.partial(pack_kernel, own=own, patch=patch, rows=...  7.84 us
    ppermute x9, starting transfers between devices, hop(): lax.ppermute(x, 'mat', [(i, i ^ k) for i in range(lax.axis_size('mat'))])  4.15 us
    pallas_call x1, Pallas kernels, products(): pl.pallas_call(functools.partial(rows_kernel, **sizes, parts=len(rows)),...  4.07 us
    ppermute x9, waiting for transfers between devices, hop(): lax.ppermute(x, 'mat', [(i, i ^ k) for i in range(lax.axis_size('mat'))])  3.91 us
    pallas_call x1, Pallas kernels, products(): pl.pallas_call(functools.partial(own_kernel, **sizes, parts=len(rows)), i...  3.03 us
    pallas_call x2, Pallas kernels, merge_rows(): pl.pallas_call(functools.partial(merge_kernel, chips=len(packs), own_only...  1.35 us
  transfers between devices with their start and end apart: 15, of which 3 were waited for; matrix products, arithmetic and copies ran while one was open for 2% of the time, Pallas kernels for 34%

profile of v5, /device:TPU:0, one launch (start us, length us, event | category | flops | bytes accessed | tf_op | source)
XLA Modules:
  0.0 51.8 jit_solution(12459476470558845233)
XLA Ops:
  0.6 3.0 %collective-permute-start = (f32[4,8,128]{2,1,0:T(8,128)}, f32[4,8,128]{2,1,0:T(8,128)S(1)}, u32[]{:S(2)}, u32[]{:S(2)}) collective-permute-start(f32[4,8,128]{2,1,0:T(8,128)} %param.7), channel_id=1, source_target_pairs={{28,0},{0,4},{4,8},{8,12},{12,16},{16,20},{20,24},{24,28},{29,1},{... | collective-permute-start | bytes 49160 | tf_op jit(solution)/shard_map/ppermute | solution.py:493
  3.7 3.1 %collective-permute-start.1 = (f32[4,8,128]{2,1,0:T(8,128)}, f32[4,8,128]{2,1,0:T(8,128)S(1)}, u32[]{:S(2)}, u32[]{:S(2)}) collective-permute-start(f32[4,8,128]{2,1,0:T(8,128)} %param.7), channel_id=1, source_target_pairs={{4,0},{8,4},{12,8},{16,12},{20,16},{24,20},{28,24},{0,28},{5,1},{9... | collective-permute-start | bytes 49160 | tf_op jit(solution)/shard_map/ppermute | solution.py:493
  6.8 0.7 %pad_add_fusion = (s32[3,256]{1,0:T(4,128)S(1)}, f32[3,256]{1,0:T(4,128)S(1)}) fusion(s32[1,256]{1,0:T(1,128)} %bitcast.12, s32[1,256]{1,0:T(1,128)} %bitcast.13, s32[1,256]{1,0:T(1,128)} %bitcast.14), kind=kLoop, calls=%fused_computation.3 | loop fusion | flops 2304 | bytes 9216 | tf_op jit(solution)/shard_map/stack | solution.py:502
  7.5 3.9 %shard_map.77.refs_4_ = bf16[8,128,128]{2,1,0:T(8,128)(2,1)S(1)} custom-call(s32[1]{0:T(128)} %bitcast.ids_ref, s32[3,256]{1,0:T(4,128)S(1)} %get-tuple-element.48.centre_in, bf16[256,96,128]{2,1,0:T(8,128)(2,1)} %bitcast.10), custom_call_target="tpu_custom_call" | custom-call | flops 805306368 | bytes 3145728 | tf_op jit(solution)/shard_map/pallas_call | solution.py:94
  11.5 1.6 %collective-permute-start.2 = (bf16[8,128,128]{2,1,0:T(8,128)(2,1)S(1)}, bf16[8,128,128]{2,1,0:T(8,128)(2,1)S(1)}, u32[]{:S(2)}, u32[]{:S(2)}) collective-permute-start(bf16[8,128,128]{2,1,0:T(8,128)(2,1)S(1)} %shard_map.77.refs_4_), channel_id=1, source_target_pairs={{0,2},{1,3},{2,0},{3,1},{4,6},{5,7},{6,4},{7,5},{8,10},{9,11},{10,... | collective-permute-start | bytes 786440 | tf_op jit(solution)/shard_map/ppermute | solution.py:488
  13.1 0.5 collective-permute-start.3
  13.6 3.9 %shard_map.78.refs_0_ = bf16[8,128,128]{2,1,0:T(8,128)(2,1)S(1)} custom-call(s32[1]{0:T(128)} %bitcast.ids_ref, s32[3,256]{1,0:T(4,128)S(1)} %get-tuple-element.48.centre_in, bf16[256,96,128]{2,1,0:T(8,128)(2,1)} %bitcast.11), custom_call_target="tpu_custom_call" | custom-call | flops 805306368 | bytes 3145728 | tf_op jit(solution)/shard_map/pallas_call | solution.py:94
  17.6 2.8 %collective-permute-done.3.rest_2_ = f32[12,8,128]{2,1,0:T(8,128)S(1)} collective-permute-done((f32[12,8,128]{2,1,0:T(8,128)S(1)}, f32[12,8,128]{2,1,0:T(8,128)S(1)}, u32[]{:S(2)}, u32[]{:S(2)}) %collective-permute-start.3) | collective-permute-done | bytes 49184 | tf_op jit(solution)/shard_map/ppermute | solution.py:488
  20.4 0.5 collective-permute-start.5
  20.9 1.5 %collective-permute-start.8 = (bf16[8,128,128]{2,1,0:T(8,128)(2,1)S(1)}, bf16[8,128,128]{2,1,0:T(8,128)(2,1)S(1)}, u32[]{:S(2)}, u32[]{:S(2)}) collective-permute-start(bf16[8,128,128]{2,1,0:T(8,128)(2,1)S(1)} %shard_map.78.refs_0_), channel_id=1, source_target_pairs={{0,2},{1,3},{2,0},{3,1},{4,6},{5,7},{6,4},{7,5},{8,10},{9,11},{10,... | collective-permute-start | bytes 786440 | tf_op jit(solution)/shard_map/ppermute | solution.py:488
  22.4 0.1 copy.17
  22.5 1.1 %collective-permute-done.7.rest_3_ = f32[12,8,128]{2,1,0:T(8,128)S(1)} collective-permute-done((f32[12,8,128]{2,1,0:T(8,128)S(1)}, f32[12,8,128]{2,1,0:T(8,128)S(1)}, u32[]{:S(2)}, u32[]{:S(2)}) %collective-permute-start.7) | collective-permute-done | bytes 49184 | tf_op jit(solution)/shard_map/ppermute | solution.py:488
  23.6 1.1 %shard_map.79 = (bf16[17,64,128]{2,1,0:T(8,128)(2,1)S(1)}, bf16[5,64,128]{2,1,0:T(8,128)(2,1)S(1)}, bf16[5,64,128]{2,1,0:T(8,128)(2,1)S(1)}) custom-call(s32[1]{0:T(128)} %bitcast.ids_ref, f32[256,3]{1,0:T(8,128)S(1)} %bitcast.7, bf16[8,128,128]{2,1,0:T(8,128)(2,1)S(1)} %shard_map.78.refs_0_, bf16[8,128,128]{2,1,0:T(8,128)(2,1)S(1)} %collective-permute-done.5.refs_1_, ...), custom_call_target="tpu_custom_call" | custom-call | tf_op jit(solution)/shard_map/pallas_call | solution.py:141
  24.7 1.7 %collective-permute-start.10 = (bf16[5,64,128]{2,1,0:T(8,128)(2,1)S(1)}, bf16[5,64,128]{2,1,0:T(8,128)(2,1)S(1)}, u32[]{:S(2)}, u32[]{:S(2)}) collective-permute-start(bf16[5,64,128]{2,1,0:T(8,128)(2,1)S(1)} %get-tuple-element.34), channel_id=1, source_target_pairs={{8,0},{12,4},{16,8},{20,12},{24,16},{28,20},{0,24},{4,28},{9,1},{1... | collective-permute-start | bytes 245768 | tf_op jit(solution)/shard_map/ppermute | solution.py:493
  26.4 0.4 collective-permute-start.9
  26.8 0.2 collective-permute-start.11
  27.0 4.5 %collective-permute-start.12 = (bf16[17,64,128]{2,1,0:T(8,128)(2,1)S(1)}, bf16[17,64,128]{2,1,0:T(8,128)(2,1)S(1)}, u32[]{:S(2)}, u32[]{:S(2)}) collective-permute-start(bf16[17,64,128]{2,1,0:T(8,128)(2,1)S(1)} %get-tuple-element.32.own_ref), channel_id=1, source_target_pairs={{4,0},{8,4},{12,8},{16,12},{20,16},{24,20},{28,24},{0,28},{5,1},{9... | collective-permute-start | bytes 835592 | tf_op jit(solution)/shard_map/ppermute | solution.py:493
  31.5 1.1 %collective-permute-done.9.low_ref = bf16[5,64,128]{2,1,0:T(8,128)(2,1)S(1)} collective-permute-done((bf16[5,64,128]{2,1,0:T(8,128)(2,1)S(1)}, bf16[5,64,128]{2,1,0:T(8,128)(2,1)S(1)}, u32[]{:S(2)}, u32[]{:S(2)}) %collective-permute-start.9) | collective-permute-done | bytes 81952 | tf_op jit(solution)/shard_map/ppermute | solution.py:493
  32.6 0.1 copy.18.pairs_ref
  32.7 3.0 %shard_map.83 = (bf16[3,128,4096]{2,1,0:T(8,128)(2,1)S(1)}, f32[12,32,128]{2,1,0:T(8,128)S(1)}) custom-call(s32[1]{0:T(128)} %bitcast.ids_ref, bf16[17,64,128]{2,1,0:T(8,128)(2,1)S(1)} %get-tuple-element.32.own_ref, f32[12,8,128]{2,1,0:T(8,128)S(1)} %constant_dynamic-update-slice_fusion.rest_0_, f32[12,8,128]{2,1,0:T(8,128)S(1)} %collective-permute-done.4.rest_1_, ...), custom_call_target="tpu_custom_call" | custom-call | flops 1000000 | bytes 10000 | tf_op jit(solution)/shard_map/pallas_call | solution.py:457
  35.8 1.2 %shard_map.80 = (bf16[17,64,128]{2,1,0:T(8,128)(2,1)S(1)}, bf16[17,64,128]{2,1,0:T(8,128)(2,1)S(1)}) custom-call(bf16[5,64,128]{2,1,0:T(8,128)(2,1)S(1)} %collective-permute-done.9.low_ref, bf16[5,64,128]{2,1,0:T(8,128)(2,1)S(1)} %collective-permute-done.10.up_ref), custom_call_target="tpu_custom_call" | custom-call | flops 1000000 | bytes 10000 | tf_op jit(solution)/shard_map/pallas_call | solution.py:247
  37.0 0.3 shard_map.81
  37.2 4.1 %shard_map.82.a_ref = bf16[3,256,4096]{2,1,0:T(8,128)(2,1)S(1)} custom-call(s32[1]{0:T(128)} %bitcast.ids_ref, bf16[17,64,128]{2,1,0:T(8,128)(2,1)S(1)} %get-tuple-element.40.refs_0_, bf16[17,64,128]{2,1,0:T(8,128)(2,1)S(1)} %get-tuple-element.41.refs_1_, bf16[17,64,128]{2,1,0:T(8,128)(2,1)S(1)} %get-tuple-element.42.refs_2_, ...), custom_call_target="tpu_custom_call" | custom-call | flops 1000000 | bytes 10000 | tf_op jit(solution)/shard_map/pallas_call | solution.py:466
  41.3 10.5 %shard_map.84 = (f32[5,64,256]{2,1,0:T(8,128)}, f32[5,64,256]{2,1,0:T(8,128)}) custom-call(s32[1]{0:T(128)} %bitcast.ids_ref, s32[2,5,2]{2,1,0:T(8,128)S(1)} %copy.18.pairs_ref, f32[1,256]{1,0:T(1,128)S(1)} %bitcast.9, bf16[17,64,128]{2,1,0:T(8,128)(2,1)S(1)} %get-tuple-element.32.own_ref, bf16[17,64,128]{2,1,0:T(8,128)(2,1)S(1)} %get-tuple-element.37.low2_ref, ...), custom_call_target="tpu_custom_call" | custom-call | flops 1000000 | bytes 10000 | tf_op jit(solution)/shard_map/pallas_call | solution.py:476
  (27 shorter events, 0.1 us)
Async XLA Ops:
  0.6 12.5 %copy-start = (f32[4,8,128]{2,1,0:T(8,128)S(1)}, f32[4,8,128]{2,1,0:T(8,128)}, u32[]{:S(2)}) copy-start(f32[4,8,128]{2,1,0:T(8,128)} %param.7) | copy-start | bytes 49156
  0.6 10.8 %collective-permute-start = (f32[4,8,128]{2,1,0:T(8,128)}, f32[4,8,128]{2,1,0:T(8,128)S(1)}, u32[]{:S(2)}, u32[]{:S(2)}) collective-permute-start(f32[4,8,128]{2,1,0:T(8,128)} %param.7), channel_id=1, source_target_pairs={{28,0},{0,4},{4,8},{8,12},{12,16},{16,20},{20,24},{24,28},{29,1},{... | collective-permute-start | bytes 49160 | tf_op jit(solution)/shard_map/ppermute | solution.py:493
  3.7 7.8 %collective-permute-start.1 = (f32[4,8,128]{2,1,0:T(8,128)}, f32[4,8,128]{2,1,0:T(8,128)S(1)}, u32[]{:S(2)}, u32[]{:S(2)}) collective-permute-start(f32[4,8,128]{2,1,0:T(8,128)} %param.7), channel_id=1, source_target_pairs={{4,0},{8,4},{12,8},{16,12},{20,16},{24,20},{28,24},{0,28},{5,1},{9... | collective-permute-start | bytes 49160 | tf_op jit(solution)/shard_map/ppermute | solution.py:493
  7.5 25.1 %copy-start.1 = (s32[256]{0:T(256)S(1)}, s32[256]{0:T(256)}, u32[]{:S(2)}) copy-start(s32[256]{0:T(256)} %param.10) | copy-start | bytes 3076
  7.5 25.1 %copy-start.2 = (s32[2,5,2]{1,2,0:T(2,128)S(1)}, s32[2,5,2]{1,2,0:T(2,128)}, u32[]{:S(2)}) copy-start(s32[2,5,2]{1,2,0:T(2,128)} %param.11) | copy-start | bytes 244
  11.5 8.9 %collective-permute-start.2 = (bf16[8,128,128]{2,1,0:T(8,128)(2,1)S(1)}, bf16[8,128,128]{2,1,0:T(8,128)(2,1)S(1)}, u32[]{:S(2)}, u32[]{:S(2)}) collective-permute-start(bf16[8,128,128]{2,1,0:T(8,128)(2,1)S(1)} %shard_map.77.refs_4_), channel_id=1, source_target_pairs={{0,2},{1,3},{2,0},{3,1},{4,6},{5,7},{6,4},{7,5},{8,10},{9,11},{10,... | collective-permute-start | bytes 786440 | tf_op jit(solution)/shard_map/ppermute | solution.py:488
  13.1 7.2 %collective-permute-start.3 = (f32[12,8,128]{2,1,0:T(8,128)S(1)}, f32[12,8,128]{2,1,0:T(8,128)S(1)}, u32[]{:S(2)}, u32[]{:S(2)}) collective-permute-start(f32[12,8,128]{2,1,0:T(8,128)S(1)} %constant_dynamic-update-slice_fusion.rest_0_), channel_id=1, source_target_pairs={{0,2},{1,3},{2,0},{3,1},{4,6},{5,7},{6,4},{7,5},{8,10},{9,11},{10,... | collective-permute-start | bytes 147464 | tf_op jit(solution)/shard_map/ppermute | solution.py:488
  13.6 6.7 %collective-permute-start.4 = (f32[12,8,128]{2,1,0:T(8,128)S(1)}, f32[12,8,128]{2,1,0:T(8,128)S(1)}, u32[]{:S(2)}, u32[]{:S(2)}) collective-permute-start(f32[12,8,128]{2,1,0:T(8,128)S(1)} %constant_dynamic-update-slice_fusion.rest_0_), channel_id=1, source_target_pairs={{0,1},{1,0},{2,3},{3,2},{4,5},{5,4},{6,7},{7,6},{8,9},{9,8},{10,11... | collective-permute-start | bytes 147464 | tf_op jit(solution)/shard_map/ppermute | solution.py:488
  20.4 3.2 %collective-permute-start.6 = (bf16[8,128,128]{2,1,0:T(8,128)(2,1)S(1)}, bf16[8,128,128]{2,1,0:T(8,128)(2,1)S(1)}, u32[]{:S(2)}, u32[]{:S(2)}) collective-permute-start(bf16[8,128,128]{2,1,0:T(8,128)(2,1)S(1)} %collective-permute-done.2.refs_2_), channel_id=1, source_target_pairs={{0,1},{1,0},{2,3},{3,2},{4,5},{5,4},{6,7},{7,6},{8,9},{9,8},{10,11... | collective-permute-start | bytes 786440 | tf_op jit(solution)/shard_map/ppermute | solution.py:488
  20.4 3.2 %collective-permute-start.5 = (bf16[8,128,128]{2,1,0:T(8,128)(2,1)S(1)}, bf16[8,128,128]{2,1,0:T(8,128)(2,1)S(1)}, u32[]{:S(2)}, u32[]{:S(2)}) collective-permute-start(bf16[8,128,128]{2,1,0:T(8,128)(2,1)S(1)} %shard_map.78.refs_0_), channel_id=1, source_target_pairs={{0,1},{1,0},{2,3},{3,2},{4,5},{5,4},{6,7},{7,6},{8,9},{9,8},{10,11... | collective-permute-start | bytes 786440 | tf_op jit(solution)/shard_map/ppermute | solution.py:488
  20.9 10.6 %collective-permute-start.8 = (bf16[8,128,128]{2,1,0:T(8,128)(2,1)S(1)}, bf16[8,128,128]{2,1,0:T(8,128)(2,1)S(1)}, u32[]{:S(2)}, u32[]{:S(2)}) collective-permute-start(bf16[8,128,128]{2,1,0:T(8,128)(2,1)S(1)} %shard_map.78.refs_0_), channel_id=1, source_target_pairs={{0,2},{1,3},{2,0},{3,1},{4,6},{5,7},{6,4},{7,5},{8,10},{9,11},{10,... | collective-permute-start | bytes 786440 | tf_op jit(solution)/shard_map/ppermute | solution.py:488
  22.4 1.2 %collective-permute-start.7 = (f32[12,8,128]{2,1,0:T(8,128)S(1)}, f32[12,8,128]{2,1,0:T(8,128)S(1)}, u32[]{:S(2)}, u32[]{:S(2)}) collective-permute-start(f32[12,8,128]{2,1,0:T(8,128)S(1)} %collective-permute-done.3.rest_2_), channel_id=1, source_target_pairs={{0,1},{1,0},{2,3},{3,2},{4,5},{5,4},{6,7},{7,6},{8,9},{9,8},{10,11... | collective-permute-start | bytes 147464 | tf_op jit(solution)/shard_map/ppermute | solution.py:488
  24.7 6.8 %collective-permute-start.10 = (bf16[5,64,128]{2,1,0:T(8,128)(2,1)S(1)}, bf16[5,64,128]{2,1,0:T(8,128)(2,1)S(1)}, u32[]{:S(2)}, u32[]{:S(2)}) collective-permute-start(bf16[5,64,128]{2,1,0:T(8,128)(2,1)S(1)} %get-tuple-element.34), channel_id=1, source_target_pairs={{8,0},{12,4},{16,8},{20,12},{24,16},{28,20},{0,24},{4,28},{9,1},{1... | collective-permute-start | bytes 245768 | tf_op jit(solution)/shard_map/ppermute | solution.py:493
  26.4 6.2 %collective-permute-start.9 = (bf16[5,64,128]{2,1,0:T(8,128)(2,1)S(1)}, bf16[5,64,128]{2,1,0:T(8,128)(2,1)S(1)}, u32[]{:S(2)}, u32[]{:S(2)}) collective-permute-start(bf16[5,64,128]{2,1,0:T(8,128)(2,1)S(1)} %get-tuple-element.33), channel_id=1, source_target_pairs={{24,0},{28,4},{0,8},{4,12},{8,16},{12,20},{16,24},{20,28},{25,1},{... | collective-permute-start | bytes 245768 | tf_op jit(solution)/shard_map/ppermute | solution.py:493
  26.8 14.6 %collective-permute-start.11 = (bf16[17,64,128]{2,1,0:T(8,128)(2,1)S(1)}, bf16[17,64,128]{2,1,0:T(8,128)(2,1)S(1)}, u32[]{:S(2)}, u32[]{:S(2)}) collective-permute-start(bf16[17,64,128]{2,1,0:T(8,128)(2,1)S(1)} %get-tuple-element.32.own_ref), channel_id=1, source_target_pairs={{28,0},{0,4},{4,8},{8,12},{12,16},{16,20},{20,24},{24,28},{29,1},{... | collective-permute-start | bytes 835592 | tf_op jit(solution)/shard_map/ppermute | solution.py:493
  27.0 14.3 %collective-permute-start.12 = (bf16[17,64,128]{2,1,0:T(8,128)(2,1)S(1)}, bf16[17,64,128]{2,1,0:T(8,128)(2,1)S(1)}, u32[]{:S(2)}, u32[]{:S(2)}) collective-permute-start(bf16[17,64,128]{2,1,0:T(8,128)(2,1)S(1)} %get-tuple-element.32.own_ref), channel_id=1, source_target_pairs={{4,0},{8,4},{12,8},{16,12},{20,16},{24,20},{28,24},{0,28},{5,1},{9... | collective-permute-start | bytes 835592 | tf_op jit(solution)/shard_map/ppermute | solution.py:493
  31.5 5.5 %collective-permute-start.13 = (bf16[8,128,128]{2,1,0:T(8,128)(2,1)S(1)}, bf16[8,128,128]{2,1,0:T(8,128)(2,1)S(1)}, u32[]{:S(2)}, u32[]{:S(2)}) collective-permute-start(bf16[8,128,128]{2,1,0:T(8,128)(2,1)S(1)} %shard_map.77.refs_4_), channel_id=1, source_target_pairs={{0,1},{1,0},{2,3},{3,2},{4,5},{5,4},{6,7},{7,6},{8,9},{9,8},{10,11... | collective-permute-start | bytes 786440 | tf_op jit(solution)/shard_map/ppermute | solution.py:488
  32.6 4.3 %collective-permute-start.14 = (bf16[8,128,128]{2,1,0:T(8,128)(2,1)S(1)}, bf16[8,128,128]{2,1,0:T(8,128)(2,1)S(1)}, u32[]{:S(2)}, u32[]{:S(2)}) collective-permute-start(bf16[8,128,128]{2,1,0:T(8,128)(2,1)S(1)} %collective-permute-done.8.refs_6_), channel_id=1, source_target_pairs={{0,1},{1,0},{2,3},{3,2},{4,5},{5,4},{6,7},{7,6},{8,9},{9,8},{10,11... | collective-permute-start | bytes 786440 | tf_op jit(solution)/shard_map/ppermute | solution.py:488
